TPU v7x, 256 devices: a whole 4x4x8 slice. The times are simulated.
256 devices in a mesh: row: 32 (over z, x), col: 8 (over y, core).
Axes of the slice: x: 4, y: 4, z: 8, core: 2. Of those that a mesh axis runs over, the one named last changes fastest.
Arguments:
- tiles: bfloat16 [32, 8, 64, 128, 128], P('row', 'col')
- block_rows: int32 [32, 8, 64], P('row', 'col'), may hold values from 0 to 15, as said below
- block_cols: int32 [32, 8, 64], P('row', 'col'), may hold values from 0 to 15, as said below
- tile_counts: int32 [32, 8], P('row', 'col'), may hold values from 16 to 64, as said below
- omega: bfloat16 [16384, 256], P('col'), may hold values from -6 to 6
Outputs:
- q_basis: bfloat16 [65536, 256], P('row')
- r_factor: float32 [256, 256], replicated
- z_sketch: float32 [16384, 256], P('col')
Inputs may be any that keep to these rules, and one draw needn't show every extreme that they name: `block_rows`: on each device the first tile_counts slots name distinct tiles, i.e. distinct (row block, column block) pairs; a row block may appear in several slots; block rows lie below 16. `block_cols`: block columns lie below 16. `tile_counts`: some device uses all 64 slots.
All inputs are finite; a program needn't handle non-finite values.
Results may differ from a plain program's by a relative error of at most 0.015.
Values may be sent and summed in bfloat16 or wider, within the bound.
No kernel may reach another device: no remote copies, remote signals or barrier semaphores. Data moves between devices by JAX's collectives and lax.ppermute only.
A program may use at most 64 MiB of HBM per device.

v0:
```python
import jax
import jax.numpy as jnp
from jax import lax
from jax.sharding import PartitionSpec as P

RB = 16


def on_device(tiles, block_rows, block_cols, tile_counts, omega):
    tile_local = tiles[0, 0]
    rows_local = block_rows[0, 0]
    cols_local = block_cols[0, 0]
    live = tile_counts[0, 0]
    slots = tile_local.shape[0]
    width = tile_local.shape[1]
    sketch_w = omega.shape[1]
    col_blocks = omega.shape[0] // width
    row_blocks = RB
    mask = (jnp.arange(slots) < live).astype(jnp.float32)
    picked = omega.reshape(col_blocks, width, sketch_w)[cols_local]
    product = jnp.einsum("tij,tjk->tik", tile_local, picked, preferred_element_type=jnp.float32)
    partial_value = (
        jnp.zeros((row_blocks, width, sketch_w), jnp.float32)
        .at[rows_local]
        .add(product * mask[:, None, None])
    )
    partial_value = partial_value.reshape(row_blocks * width, sketch_w)
    nrow_total = row_blocks * width * lax.axis_size("row")
    sketch = lax.psum(partial_value, "col")
    gram_local = jnp.dot(sketch.T, sketch, precision=lax.Precision.HIGHEST)
    gram = lax.psum(gram_local, "row") / nrow_total
    lower = jnp.linalg.cholesky(gram)
    q_basis = lax.linalg.triangular_solve(
        lower, sketch, left_side=False, lower=True, transpose_a=True
    ).astype(jnp.bfloat16)
    q_picked = q_basis.reshape(row_blocks, width, sketch_w)[rows_local]
    back = jnp.einsum("tij,tik->tjk", tile_local, q_picked, preferred_element_type=jnp.float32)
    z_partial = (
        jnp.zeros((col_blocks, width, sketch_w), jnp.float32)
        .at[cols_local]
        .add(back * mask[:, None, None])
    )
    z_partial = z_partial.reshape(col_blocks * width, sketch_w)
    z_sketch = lax.psum(z_partial.astype(jnp.bfloat16), "row").astype(jnp.float32)
    return (q_basis, lower.T, z_sketch)


def solution(mesh):
    placed = (
        P("row", "col", None, None, None),
        P("row", "col", None),
        P("row", "col", None),
        P("row", "col"),
        P("col", None),
    )
    return jax.shard_map(
        on_device,
        mesh=mesh,
        in_specs=placed,
        out_specs=(P("row", None), P(), P("col", None)),
        check_vma=False,
    )
```

profile of v0, /device:TPU:1, one launch (start us, length us, event | category | flops | bytes accessed | tf_op | source)
XLA Modules:
  0.0 534.6 jit_solution(14943081351982178184)
XLA Ops:
  7.2 0.0 copy-start
  7.2 0.0 all-reduce.5.cloned.1.call-start
  7.2 0.8 fusion.12
  8.7 4.0 gather_fusion
  12.7 0.0 copy-done
  12.7 7.2 %multiply_bitcast_fusion.1 = f32[64,128,256]{1,2,0:T(8,128)} fusion(f32[64]{0:T(128)S(1)} %compare_convert_fusion, bf16[64,128,256]{2,1,0:T(8,128)(2,1)} %gather_fusion, bf16[1,1,64,128,128]{4,3,2,1,0:T(8,128)(2,1)S(1)} %copy-done), kind=kOutput, calls=%fused_computation.7 | convolution fusion | flops 538968064 | bytes 14680320 | tf_op jit(solution)/shard_map/tij,tjk->tik/dot_general | solution.py:21
  19.9 0.0 copy-start.6
  19.9 9.0 %copy.14 = f32[64,128,256]{2,1,0:T(8,128)} copy(f32[64,128,256]{1,2,0:T(8,128)} %multiply_bitcast_fusion.1) | data formatting | bytes 16777216 | tf_op jit(solution)/shard_map/mul | solution.py:25
  28.9 0.0 copy-done.6
  28.9 1.5 broadcast.138.clone
  30.5 18.8 %scatter_fusion = f32[16,128,256]{2,1,0:T(8,128)} fusion(f32[16,128,256]{2,1,0:T(8,128)} %broadcast.138.clone, s32[64]{0:T(128)S(1)} %fusion.11, f32[64,128,256]{2,1,0:T(8,128)} %copy.14), kind=kCustom, calls=%fused_computation.2 | custom fusion | flops 2097152 | bytes 25166080 | tf_op jit(solution)/shard_map/scatter-add | solution.py:25
  49.3 0.0 all-reduce.5.cloned.1.call-update
  49.3 0.0 all-reduce.7.cloned.1.call-start
  49.4 72.6 %all-reduce.5.cloned.1.call-done = f32[2048,256]{1,0:T(8,128)} async-done(((f32[2048,256]{1,0:T(8,128)}), f32[2048,256]{1,0:T(8,128)}) %all-reduce.5.cloned.1.call-update) | async-done | bytes 2097168 | tf_op jit(solution)/shard_map/psum | solution.py:29
  122.0 6.4 %fusion.15 = f32[256,256]{0,1:T(8,128)} fusion(f32[2048,256]{1,0:T(8,128)} %all-reduce.5.cloned.1.call-done), kind=kOutput, calls=%fused_computation.49 | convolution fusion | flops 1610612736 | bytes 2359296 | tf_op jit(solution)/shard_map/dot_general | solution.py:30
  128.4 0.0 all-reduce.7.cloned.1.call-update
  128.4 0.2 all-reduce.9.cloned.1.call-start
  128.7 140.9 %all-reduce.7.cloned.1.call-done = f32[256,256]{0,1:T(8,128)} async-done(((f32[256,256]{0,1:T(8,128)}), f32[256,256]{0,1:T(8,128)}) %all-reduce.7.cloned.1.call-update) | async-done | bytes 262160 | tf_op jit(solution)/shard_map/psum | solution.py:31
  269.6 1.0 broadcast_multiply_fusion
  270.6 0.1 copy.16
  270.7 1.0 fusion.4
  271.7 11.7 %cholesky.50 = f32[128,128]{1,0:T(8,128)S(1)} custom-call(f32[128,128]{1,0:T(8,128)S(1)} %cholesky.118), custom_call_target="Cholesky" | custom-call | tf_op jit(solution)/shard_map/jit(cholesky)/cholesky | solution.py:32
  283.5 9.8 %custom-call.14 = f32[1,128,128]{1,2,0:T(8,128)S(1)} custom-call(f32[1,128,128]{2,1,0:T(8,128)S(1)} %get-tuple-element.32), custom_call_target="InvertDiagBlocksLowerTriangular" | custom-call | tf_op jit(solution)/shard_map/jit(cholesky)/cholesky | solution.py:32
  293.3 0.2 constant_dynamic-update-slice_fusion.1
  293.5 0.3 convolution_subtract_fusion.1
  293.8 11.7 %cholesky.105 = f32[128,128]{1,0:T(8,128)S(1)} custom-call(f32[128,128]{1,0:T(8,128)S(1)} %convolution_subtract_fusion.1), custom_call_target="Cholesky" | custom-call | tf_op jit(solution)/shard_map/jit(cholesky)/cholesky | solution.py:32
  305.5 0.6 compare_reduce_fusion
  307.5 0.1 triangular_solve.64
  307.6 4.2 while.1
  307.8 0.6 fusion.25
  308.4 1.4 bitcast_dynamic-update-slice_fusion.2
  309.8 0.6 fusion.25
  310.4 1.4 bitcast_dynamic-update-slice_fusion.2
  311.8 19.7 %custom-call.15 = f32[2,128,128]{1,2,0:T(8,128)S(1)} custom-call(f32[2,128,128]{2,1,0:T(8,128)S(1)} %get-tuple-element.10), custom_call_target="InvertDiagBlocksLowerTriangular" | custom-call | tf_op jit(solution)/shard_map/triangular_solve | solution.py:33
  331.4 0.0 copy-start.1
  331.5 2.3 fusion.14
  333.8 0.0 copy-start.4
  333.8 0.0 copy-done.1
  333.8 1.0 convolution_subtract_fusion
  334.8 1.0 convolution_convert_fusion
  335.8 0.0 copy-start.2
  335.8 0.0 copy-done.4
  335.8 0.8 copy-done.2
  336.6 0.1 pad_maximum_fusion.1
  336.7 2.8 gather_fusion.1
  339.5 7.2 %multiply_bitcast_fusion = f32[64,128,256]{1,2,0:T(8,128)} fusion(f32[64]{0:T(128)S(1)} %compare_convert_fusion, bf16[64,128,256]{2,1,0:T(8,128)(2,1)} %gather_fusion.1, bf16[1,1,64,128,128]{4,3,2,1,0:T(8,128)(2,1)S(1)} %copy-done), kind=kOutput, calls=%fused_computation.6 | convolution fusion | flops 538968064 | bytes 14680320 | tf_op jit(solution)/shard_map/tij,tik->tjk/dot_general | solution.py:37
  346.7 9.0 %copy.18 = f32[64,128,256]{2,1,0:T(8,128)} copy(f32[64,128,256]{1,2,0:T(8,128)} %multiply_bitcast_fusion) | data formatting | bytes 16777216 | tf_op jit(solution)/shard_map/mul | solution.py:41
  355.7 1.5 broadcast.138
  357.3 18.7 %scatter_fusion.1 = f32[16,128,256]{2,1,0:T(8,128)} fusion(f32[16,128,256]{2,1,0:T(8,128)} %broadcast.138, s32[64]{0:T(128)S(1)} %fusion.12, f32[64,128,256]{2,1,0:T(8,128)} %copy.18), kind=kCustom, calls=%fused_computation.3 | custom fusion | flops 2097152 | bytes 25166080 | tf_op jit(solution)/shard_map/scatter-add | solution.py:41
  375.9 0.0 copy-start.3
  375.9 0.0 copy-start.5
  375.9 2.8 convert_element_type.19
  378.8 0.0 all-reduce.9.cloned.1.call-update
  378.8 0.8 copy.19
  379.6 0.0 copy-done.3
  379.6 0.0 copy-done.5
  379.6 1.1 pad_maximum_fusion
  380.7 144.6 %all-reduce.9.cloned.1.call-done = bf16[2048,256]{1,0:T(8,128)(2,1)} async-done(((bf16[2048,256]{1,0:T(8,128)(2,1)}), bf16[2048,256]{1,0:T(8,128)(2,1)}) %all-reduce.9.cloned.1.call-update) | async-done | bytes 1048592 | tf_op jit(solution)/shard_map/psum | solution.py:44
  525.3 2.7 convert_element_type.21
  (13 shorter events, 0.2 us)
Async XLA Ops:
  7.2 5.5 %copy-start = (bf16[1,1,64,128,128]{4,3,2,1,0:T(8,128)(2,1)S(1)}, bf16[1,1,64,128,128]{4,3,2,1,0:T(8,128)(2,1)}, u32[]{:S(2)}) copy-start(bf16[1,1,64,128,128]{4,3,2,1,0:T(8,128)(2,1)} %param.5) | copy-start | bytes 6291460
  7.2 114.9 %all-reduce.5.cloned.1.call-start = ((), (), s32[]{:S(2)}) async-start(), calls=%async_computation | async-start | bytes 4194304 | tf_op jit(solution)/shard_map/psum | solution.py:29
  19.9 9.0 %copy-start.6 = (s32[1,1,64]{2,1,0:T(1,128)S(1)}, s32[1,1,64]{2,1,0:T(1,128)}, u32[]{:S(2)}) copy-start(s32[1,1,64]{2,1,0:T(1,128)} %param.6) | copy-start | bytes 772
  49.3 220.3 %all-reduce.7.cloned.1.call-start = ((), (), s32[]{:S(2)}) async-start(), calls=%async_computation.1 | async-start | bytes 524288 | tf_op jit(solution)/shard_map/psum | solution.py:31
  128.4 396.9 %all-reduce.9.cloned.1.call-start = ((), (), s32[]{:S(2)}) async-start(), calls=%async_computation.2 | async-start | bytes 2097152 | tf_op jit(solution)/shard_map/psum | solution.py:44
  331.4 2.4 copy-start.1
  333.8 2.0 copy-start.4
  335.8 0.8 copy-start.2
  375.9 3.7 copy-start.3
  375.9 3.7 copy-start.5
Sparse Core Ops, SparseCore 0:
  49.5 72.5 all-reduce.4
  128.6 140.9 all-reduce.6
  378.9 146.3 all-reduce.8
where the time goes:
time: 539 us; the launch traced here: 535 us
  waiting for transfers between devices  358 us (66%)
  other arithmetic  101 us (19%)
  local copies, waits for them, and re-layouts  33.7 us (6%)
  matrix products  25.5 us (5%)
  between operations  15.9 us (3%)
    psum x1, waiting for transfers between devices, on_device(): lax.psum(z_partial.astype(jnp.bfloat16), 'row').astype(jnp.float32)  145 us
    psum x1, waiting for transfers between devices, on_device(): gram = lax.psum(gram_local, 'row') / nrow_total  141 us
    psum x1, waiting for transfers between devices, on_device(): sketch = lax.psum(partial_value, 'col')  72.6 us
    another operation x6, other arithmetic, on_device(): lower = jnp.linalg.cholesky(gram)  34 us
    another operation x4, other arithmetic, on_device(): lax.linalg.triangular_solve(lower, sketch, left_side=False, lower=True, t...  20.9 us
    scatter-add x1, other arithmetic, on_device(): partial_value = jnp.zeros((row_blocks, width, sketch_w), jnp.float32).at[...  18.8 us
    scatter-add x1, other arithmetic, on_device(): z_partial = jnp.zeros((col_blocks, width, sketch_w), jnp.float32).at[cols...  18.7 us
  transfers between devices with their start and end apart: 3, of which 3 were waited for; matrix products, arithmetic and copies ran while one was open for 0% of the time, Pallas kernels for 0%

commit v1 on v0

v1 whole, which is shorter than its diff:
```python
import jax
import jax.numpy as jnp
from jax import lax
from jax.experimental import pallas as pl
from jax.experimental.pallas import tpu as pltpu
from jax.sharding import Mesh, PartitionSpec as P

F32 = jnp.float32
BF16 = jnp.bfloat16
TILE = 128
K = 256
RB = 16
CB = 16
SLOTS = 64
HALF = RB * TILE // 2
NROW = 65536
PARTS = 32
ROWS = CB * TILE // PARTS
EXTRA = 16
GROUP = 4
NB = 32
VMEM = pl.BlockSpec(memory_space=pltpu.VMEM)
SMEM = pl.BlockSpec(memory_space=pltpu.SMEM)


def dot(a, b, ca, cb, precision=None):
    return lax.dot_general(
        a, b, (((ca,), (cb,)), ((), ())), precision=precision, preferred_element_type=F32
    )


def iota(shape, dim):
    return lax.broadcasted_iota(jnp.int32, shape, dim)


def sketch_kernel(core_ref, rows_ref, cols_ref, live_ref, tiles_ref, omega_ref, keep_ref, send_ref, acc):
    acc[...] = jnp.zeros_like(acc)
    live = live_ref[0]
    turn = core_ref[0] * (RB // 2)

    @pl.loop(0, (live + GROUP - 1) // GROUP)
    def _(g):
        prods, places = [], []
        for i in range(GROUP):
            t = g * GROUP + i
            prod = dot(tiles_ref[t], omega_ref[cols_ref[t] & (CB - 1)], 1, 0)
            prods.append(jnp.where(t < live, prod, 0.0))
            places.append((rows_ref[t] + turn) & (RB - 1))
        for prod, place in zip(prods, places):
            acc[place] += prod

    keep_ref[...] = acc[: RB // 2].reshape(HALF, K)
    send_ref[...] = acc[RB // 2 :].reshape(HALF, K)


def place_matrix(rows, cols, shift, dtype=BF16):
    e = iota((rows, cols), 0)
    p = iota((rows, cols), 1)
    return jnp.where((p // 6) * EXTRA + p % 6 + shift == e, 1.0, 0.0).astype(dtype)


def back_kernel(core_ref, rows_ref, cols_ref, live_ref, tiles_ref, mine_ref, other_ref, out_ref, s_ref, acc):
    core = core_ref[0]
    s_ref[pl.ds(core * (RB // 2), RB // 2)] = mine_ref[...].reshape(RB // 2, TILE, K)
    s_ref[pl.ds((1 - core) * (RB // 2), RB // 2)] = other_ref[...].reshape(RB // 2, TILE, K)
    acc[...] = jnp.zeros_like(acc)
    live = live_ref[0]

    @pl.loop(0, (live + GROUP - 1) // GROUP)
    def _(g):
        prods, places = [], []
        for i in range(GROUP):
            t = g * GROUP + i
            prod = dot(tiles_ref[t], s_ref[rows_ref[t] & (RB - 1)], 0, 0)
            prods.append(jnp.where(t < live, prod, 0.0))
            places.append(cols_ref[t] & (CB - 1))
        for prod, place in zip(prods, places):
            acc[place] += prod

    gram = dot(mine_ref[...], mine_ref[...], 0, 0) + dot(other_ref[...], other_ref[...], 0, 0)
    gram = gram * (1.0 / NROW)
    low = gram[K // 2 :, K // 2 :]
    low = jnp.concatenate([low[: K // 4], low[K // 4 :]], axis=1)
    packed = jnp.concatenate([gram[: K // 2], low], axis=0)
    high = packed.astype(BF16)
    rest = (packed - high.astype(F32)).astype(BF16)
    extra = dot(place_matrix(PARTS * EXTRA, 192, 0), high, 1, 0) + dot(
        place_matrix(PARTS * EXTRA, 192, 6), rest, 1, 0
    )
    out_ref[:, :ROWS, :] = acc[...].reshape(PARTS, ROWS, K).astype(BF16)
    out_ref[:, ROWS:, :] = extra.reshape(PARTS, EXTRA, K).astype(BF16)


def sum_kernel(in_ref, out_ref):
    total = in_ref[0].astype(F32)
    for i in range(1, PARTS):
        total = total + in_ref[i].astype(F32)
    w = total[:ROWS]
    extra = total[ROWS:]
    mean = jnp.sum(w, axis=0, keepdims=True) * (1.0 / ROWS)
    top = jnp.max(jnp.abs(mean), axis=1, keepdims=True)
    lead = (mean / jnp.maximum(top, 1e-30)).astype(BF16)
    leadf = lead.astype(F32)
    norm = jnp.maximum(jnp.sum(leadf * leadf, axis=1, keepdims=True), 0.5)
    coef = (dot(lead, w.astype(BF16), 1, 1) / norm).astype(BF16)
    rest = w - dot(coef, lead, 0, 0)
    row = iota((EXTRA, K), 0)
    gram = extra + pltpu.roll(extra, EXTRA - 6, 0)
    high = gram.astype(BF16).astype(F32)
    low = pltpu.roll(gram - high, 6, 0)
    wide = jnp.concatenate([coef.astype(F32), jnp.zeros((1, K - ROWS), F32)], axis=1)
    tail = jnp.where(row < 6, high, jnp.where(row < 12, low, 0.0))
    tail = jnp.where(row == 12, leadf, jnp.where(row == 13, wide, tail))
    body = rest.astype(BF16)
    tail = tail.astype(BF16)
    for i in range(PARTS):
        out_ref[i, :ROWS, :] = body
        out_ref[i, ROWS:, :] = tail


def factor(work):
    for b in range(K // NB):
        at = b * NB
        base = at // 128 * 128
        x = work[at : at + NB, base : base + 128]
        if at > base:
            x = pltpu.roll(x, 128 - (at - base), 1)
        lane = iota((NB, 128), 1)
        row = iota((NB, 128), 0)
        x = jnp.where(lane < NB, x, jnp.where(lane - NB == row, 1.0, 0.0))
        for j in range(NB):
            pivot = x[j : j + 1, :]
            scale = 1.0 / pivot[:, j : j + 1]
            m = jnp.where(row[:, :1] > j, x[:, j : j + 1] * scale, 0.0)
            x = x - m * pivot
        diag = jnp.sum(jnp.where(lane == row, x, 0.0), axis=1, keepdims=True)
        x = x * lax.rsqrt(diag)
        inv = pltpu.roll(x, 128 - NB, 1)[:, :NB]
        u = dot(inv, work[at : at + NB, :], 1, 0, lax.Precision.HIGHEST)
        work[at : at + NB, :] = u
        if at + NB < K:
            ut = u[:, :K].T
            work[at + NB :, :] -= dot(ut[at + NB :], u, 1, 0, lax.Precision.HIGHEST)


def final_kernel(core_ref, in_ref, mine_ref, other_ref, q_ref, r_ref, z_ref, work):
    extra = in_ref[:, ROWS:, :].reshape(PARTS * EXTRA, K)
    p = iota((192, PARTS * EXTRA), 0)
    e = iota((192, PARTS * EXTRA), 1)
    first = (p // 6) * EXTRA + p % 6
    pick = jnp.where((e == first) | (e == first + 6), 1.0, 0.0).astype(BF16)
    packed = dot(pick, extra, 1, 0)
    work[: K // 2, :K] = packed[: K // 2]
    work[K // 2 :, : K // 2] = packed[: K // 2, K // 2 :].T
    work[K // 2 : 3 * K // 4, K // 2 : K] = packed[K // 2 :, : K // 2]
    work[3 * K // 4 :, K // 2 : K] = packed[K // 2 :, K // 2 :]
    work[:, K:] = jnp.where(iota((K, K), 0) == iota((K, K), 1), 1.0, 0.0)
    factor(work)
    r_ref[...] = jnp.where(iota((K, K), 0) <= iota((K, K), 1), work[:, :K], 0.0)
    inv = work[:, K:]
    high = inv.astype(BF16)
    low = (inv - high.astype(F32)).astype(BF16)

    def solve(a):
        return dot(a, high, 1, 1) + dot(a, low, 1, 1)

    core = core_ref[0]
    q_ref[pl.ds(pl.multiple_of(core * HALF, HALF), HALF), :] = solve(mine_ref[...]).astype(BF16)
    q_ref[pl.ds(pl.multiple_of((1 - core) * HALF, HALF), HALF), :] = solve(other_ref[...]).astype(BF16)
    i = iota((2 * PARTS, PARTS * EXTRA), 0)
    e = iota((2 * PARTS, PARTS * EXTRA), 1)
    want = jnp.where(i < PARTS, i * EXTRA + 12, (i - PARTS) * EXTRA + 13)
    leads = dot(jnp.where(e == want, 1.0, 0.0).astype(BF16), extra, 1, 0)
    lead = solve(leads[:PARTS].astype(BF16))
    lead_high = lead.astype(BF16)
    lead_low = (lead - lead_high.astype(F32)).astype(BF16)
    coef = leads[PARTS:].astype(BF16)
    for i in range(PARTS):
        c = coef[i : i + 1, :ROWS]
        term = dot(c, lead_high[i : i + 1], 0, 0) + dot(c, lead_low[i : i + 1], 0, 0)
        z_ref[i * ROWS : (i + 1) * ROWS, :] = solve(in_ref[i, :ROWS, :]) + term


def shape(*dims, dtype=F32):
    return jax.ShapeDtypeStruct(dims, dtype)


LIMIT = pltpu.CompilerParams(vmem_limit_bytes=40 * 1024 * 1024)


def on_device(tiles, block_rows, block_cols, tile_counts, omega):
    core = lax.axis_index("c").astype(jnp.int32).reshape(1)
    rows = block_rows[0, 0]
    cols = block_cols[0, 0]
    live = tile_counts[0]
    tiles = tiles[0, 0]
    keep, send = pl.pallas_call(
        sketch_kernel,
        out_shape=(shape(HALF, K), shape(HALF, K)),
        in_specs=[SMEM] * 4 + [VMEM] * 2,
        out_specs=(VMEM, VMEM),
        scratch_shapes=[pltpu.VMEM((RB, TILE, K), F32)],
        compiler_params=LIMIT,
        name="sketch",
    )(core, rows, cols, live, tiles, omega.reshape(CB, TILE, K))
    swap = [(0, 1), (1, 0)]
    half = keep + lax.ppermute(send, "c", swap)
    quarters = lax.all_to_all(half.astype(BF16).reshape(4, HALF // 4, K), "y", 0, 0, tiled=True)
    shard = jnp.sum(quarters.astype(F32), axis=0).astype(BF16)
    spread = jnp.broadcast_to(shard[None], (4, HALF // 4, K))
    mine = lax.all_to_all(spread, "y", 0, 0, tiled=True).reshape(HALF, K)
    other = lax.ppermute(mine, "c", swap)
    payload = pl.pallas_call(
        back_kernel,
        out_shape=shape(PARTS, ROWS + EXTRA, K, dtype=BF16),
        in_specs=[SMEM] * 4 + [VMEM] * 3,
        out_specs=VMEM,
        scratch_shapes=[pltpu.VMEM((RB, TILE, K), BF16), pltpu.VMEM((CB, TILE, K), F32)],
        compiler_params=LIMIT,
        name="back",
    )(core, rows, cols, live, tiles, mine, other)
    parts = lax.all_to_all(payload, ("z", "x"), 0, 0, tiled=True)
    spread = pl.pallas_call(
        sum_kernel,
        out_shape=shape(PARTS, ROWS + EXTRA, K, dtype=BF16),
        in_specs=[VMEM],
        out_specs=VMEM,
        compiler_params=LIMIT,
        name="total",
    )(parts)
    whole = lax.all_to_all(spread, ("z", "x"), 0, 0, tiled=True)
    return pl.pallas_call(
        final_kernel,
        out_shape=(shape(2 * HALF, K, dtype=BF16), shape(K, K), shape(CB * TILE, K)),
        in_specs=[SMEM] + [VMEM] * 3,
        out_specs=(VMEM, VMEM, VMEM),
        scratch_shapes=[pltpu.VMEM((K, 2 * K), F32)],
        compiler_params=LIMIT,
        name="finish",
    )(core, whole, mine, other)


def solution(mesh):
    grid = Mesh(mesh.devices.reshape(8, 4, 4, 2), ("z", "x", "y", "c"))
    row, col = ("z", "x"), ("y", "c")
    placed = (
        P(row, col, None, None, None),
        P(row, col, None),
        P(row, col, None),
        P(row, col),
        P(col, None),
    )
    return jax.shard_map(
        on_device,
        mesh=grid,
        in_specs=placed,
        out_specs=(P(row, None), P(), P(col, None)),
        check_vma=False,
    )
```

time: 539 us -> 164 us (0.30)
  waiting for transfers between devices: 358 us -> 3.82 us
  blocking collectives: 0 us -> 111 us
  other arithmetic: 101 us -> 0.25 us
  Pallas kernels: 0 us -> 36.9 us
  local copies, waits for them, and re-layouts: 33.7 us -> 4.17 us
  matrix products: 25.5 us -> 0 us
  between operations: 15.9 us -> 1.34 us
  starting transfers between devices: 0.3 us -> 6.74 us
    psum x3 -> x0, waiting for transfers between devices: 358 us -> none  [the longest x1 145 us: on_device(): lax.psum(z_partial.astype(jnp.bfloat16), 'row').astype(jnp.float32)]
    all_to_all x0 -> x4, blocking collectives: none -> 111 us  [the longest x1 48.9 us: on_device(): parts = lax.all_to_all(payload, ('z', 'x'), 0, 0, tiled=True)]
    another operation x10 -> x0, other arithmetic: 54.9 us -> none  [the longest x6 34 us: on_device(): lower = jnp.linalg.cholesky(gram)]
    scatter-add x2 -> x0, other arithmetic: 37.5 us -> none  [the longest x1 18.8 us: on_device(): partial_value = jnp.zeros((row_blocks, width, sketch_w), jnp.float32).at[...]
    pallas_call x0 -> x4, Pallas kernels: none -> 36.9 us  [the longest x1 31.7 us: on_device(): pl.pallas_call(final_kernel, out_shape=(shape(2 * HALF, K, dtype=BF16), s...]
    dot_general x3 -> x0, matrix products: 20.7 us -> none  [the longest x1 7.19 us: on_device(): jnp.einsum('tij,tjk->tik', tile_local, picked, preferred_element_type=jnp...]
    mul x2 -> x0, local copies, waits for them, and re-layouts: 18 us -> none  [the longest x1 9.02 us: on_device(): product * mask[:, None, None]]
    another operation x11 -> x0, local copies, waits for them, and re-layouts: 7.12 us -> none
  transfers between devices with their start and end apart: 3 -> 2, of which waited for: 3 -> 2; matrix products, arithmetic and copies ran while one was open for 0% -> 0% of each run, Pallas kernels for 0% -> 0%
where the time goes in v1:
time: 164 us
  blocking collectives  111 us (68%)
  Pallas kernels  36.9 us (22%)
  starting transfers between devices  6.74 us (4%)
  local copies, waits for them, and re-layouts  4.17 us (3%)
  waiting for transfers between devices  3.82 us (2%)
    all_to_all x1, blocking collectives, on_device(): parts = lax.all_to_all(payload, ('z', 'x'), 0, 0, tiled=True)  48.9 us
    all_to_all x1, blocking collectives, on_device(): whole = lax.all_to_all(spread, ('z', 'x'), 0, 0, tiled=True)  38.8 us
    pallas_call x1, Pallas kernels, on_device(): pl.pallas_call(final_kernel, out_shape=(shape(2 * HALF, K, dtype=BF16), s...  31.7 us
    all_to_all x1, blocking collectives, on_device(): lax.all_to_all(half.astype(BF16).reshape(4, HALF // 4, K), 'y', 0, 0, til...  12.8 us
    all_to_all x1, blocking collectives, on_device(): mine = lax.all_to_all(spread, 'y', 0, 0, tiled=True).reshape(HALF, K)  10.5 us
    ppermute x1, starting transfers between devices, on_device(): half = keep + lax.ppermute(send, 'c', swap)  4.25 us
    unnamed x14, local copies, waits for them, and re-layouts  4.13 us
  transfers between devices with their start and end apart: 2, of which 2 were waited for; matrix products, arithmetic and copies ran while one was open for 0% of the time, Pallas kernels for 0%

profile of v1, /device:TPU:1, one launch (start us, length us, event | category | flops | bytes accessed | tf_op | source)
XLA Modules:
  0.0 164.1 jit_solution(15318816448469600300)
XLA Ops:
  1.3 0.0 copy-start
  1.3 1.6 copy-done
  2.9 0.0 copy-start.2
  2.9 1.2 copy-done.2
  4.1 0.0 copy-start.3
  4.1 0.7 copy-done.3
  4.8 0.0 copy-start.5
  4.8 0.7 copy-done.5
  5.4 1.7 %sketch.1 = (f32[1024,256]{1,0:T(8,128)S(1)}, f32[1024,256]{1,0:T(8,128)S(1)}) custom-call(s32[1]{0:T(128)} %bitcast.core_ref, s32[64]{0:T(128)S(1)} %bitcast.16, s32[64]{0:T(128)S(1)} %bitcast.18, s32[1]{0:T(128)} %bitcast.8.live_ref, bf16[64,128,128]{2,1,0:T(8,128)(2,1)S(1)} %bitcast.10, bf16[16,128,256]{2,1,0:T(8,128)(2,1)S(1)} %bitcast.15), custom_call_target="tpu_custom_call" | custom-call | tf_op jit(solution)/shard_map/sketch/pallas_call | solution.py:197
  7.2 4.3 %collective-permute-start = (f32[1024,256]{1,0:T(8,128)S(1)}, f32[1024,256]{1,0:T(8,128)S(1)}, u32[]{:S(2)}, u32[]{:S(2)}) collective-permute-start(f32[1024,256]{1,0:T(8,128)S(1)} %get-tuple-element.6), channel_id=1, source_target_pairs={{0,1},{1,0},{2,3},{3,2},{4,5},{5,4},{6,7},{7,6},{8,9},{9,8},{10,11... | collective-permute-start | bytes 3145736 | tf_op jit(solution)/shard_map/ppermute | solution.py:207
  11.4 2.3 %collective-permute-done = f32[1024,256]{1,0:T(8,128)S(1)} collective-permute-done((f32[1024,256]{1,0:T(8,128)S(1)}, f32[1024,256]{1,0:T(8,128)S(1)}, u32[]{:S(2)}, u32[]{:S(2)}) %collective-permute-start) | collective-permute-done | bytes 1048608 | tf_op jit(solution)/shard_map/ppermute | solution.py:207
  13.7 0.2 add_convert_fusion
  13.9 12.8 %all_to_all.20 = bf16[4,256,256]{2,1,0:T(8,128)(2,1)S(1)} all-to-all(bf16[4,256,256]{2,1,0:T(8,128)(2,1)S(1)} %bitcast.20), channel_id=1, replica_groups=mesh['z'=8,'x'=4,'y'=4,'c'=2] {'y'}, dimensions={0} | all-to-all | bytes 1048576 | tf_op jit(solution)/shard_map/all_to_all | solution.py:208
  26.6 0.0 copy-start.1
  26.6 0.0 copy-start.4
  26.6 0.0 copy-start.6
  26.6 0.1 reduce_sum.12
  26.8 10.5 %all_to_all.21 = bf16[4,256,256]{2,1,0:T(8,128)(2,1)S(1)} all-to-all(bf16[4,256,256]{2,1,0:T(8,128)(2,1)S(1)} %broadcast_in_dim.2), channel_id=1, replica_groups=mesh['z'=8,'x'=4,'y'=4,'c'=2] {'y'}, dimensions={0} | all-to-all | bytes 1048576 | tf_op jit(solution)/shard_map/all_to_all | solution.py:211
  37.3 2.5 %collective-permute-start.1 = (bf16[1024,256]{1,0:T(8,128)(2,1)S(1)}, bf16[1024,256]{1,0:T(8,128)(2,1)S(1)}, u32[]{:S(2)}, u32[]{:S(2)}) collective-permute-start(bf16[1024,256]{1,0:T(8,128)(2,1)S(1)} %bitcast.12), channel_id=1, source_target_pairs={{0,1},{1,0},{2,3},{3,2},{4,5},{5,4},{6,7},{7,6},{8,9},{9,8},{10,11... | collective-permute-start | bytes 1572872 | tf_op jit(solution)/shard_map/ppermute | solution.py:212
  39.7 1.5 collective-permute-done.1.other_ref
  41.3 0.0 copy-done.1
  41.3 0.0 copy-done.4
  41.3 0.0 copy-done.6
  41.3 2.8 %back.1 = bf16[32,80,256]{2,1,0:T(8,128)(2,1)S(1)} custom-call(s32[1]{0:T(128)} %bitcast.core_ref, s32[64]{0:T(128)S(1)} %bitcast.17, s32[64]{0:T(128)S(1)} %bitcast.19, s32[1]{0:T(128)} %bitcast.9.live_ref, bf16[64,128,128]{2,1,0:T(8,128)(2,1)S(1)} %bitcast.11, bf16[1024,256]{1,0:T(8,128)(2,1)S(1)} %bitcast.13, ...), custom_call_target="tpu_custom_call" | custom-call | tf_op jit(solution)/shard_map/back/pallas_call | solution.py:213
  44.1 48.9 %all_to_all.22.in_ref = bf16[32,80,256]{2,1,0:T(8,128)(2,1)S(1)} all-to-all(bf16[32,80,256]{2,1,0:T(8,128)(2,1)S(1)} %back.1), channel_id=1, replica_groups=mesh['z'=8,'x'=4,'y'=4,'c'=2] {'z','x'}, dimensions={0} | all-to-all | bytes 2621440 | tf_op jit(solution)/shard_map/all_to_all | solution.py:222
  93.0 0.6 total.1
  93.6 38.8 %all_to_all.23.in_ref = bf16[32,80,256]{2,1,0:T(8,128)(2,1)S(1)} all-to-all(bf16[32,80,256]{2,1,0:T(8,128)(2,1)S(1)} %total.1), channel_id=1, replica_groups=mesh['z'=8,'x'=4,'y'=4,'c'=2] {'z','x'}, dimensions={0} | all-to-all | bytes 2621440 | tf_op jit(solution)/shard_map/all_to_all | solution.py:231
  132.4 31.7 %finish.1 = (bf16[2048,256]{1,0:T(8,128)(2,1)}, f32[256,256]{1,0:T(8,128)}, f32[2048,256]{1,0:T(8,128)}) custom-call(s32[1]{0:T(128)} %bitcast.core_ref, bf16[32,80,256]{2,1,0:T(8,128)(2,1)S(1)} %all_to_all.23.in_ref, bf16[1024,256]{1,0:T(8,128)(2,1)S(1)} %bitcast.14, bf16[1024,256]{1,0:T(8,128)(2,1)S(1)} %collective-permute-done.1.other_ref), custom_call_target="tpu_custom_call" | custom-call | tf_op jit(solution)/shard_map/finish/pallas_call | solution.py:232
  (1 shorter events, 0.0 us)
Async XLA Ops:
  1.3 1.6 copy-start
  2.9 1.2 copy-start.2
  4.1 0.7 copy-start.3
  4.8 0.7 copy-start.5
  7.2 6.5 %collective-permute-start = (f32[1024,256]{1,0:T(8,128)S(1)}, f32[1024,256]{1,0:T(8,128)S(1)}, u32[]{:S(2)}, u32[]{:S(2)}) collective-permute-start(f32[1024,256]{1,0:T(8,128)S(1)} %get-tuple-element.6), channel_id=1, source_target_pairs={{0,1},{1,0},{2,3},{3,2},{4,5},{5,4},{6,7},{7,6},{8,9},{9,8},{10,11... | collective-permute-start | bytes 3145736 | tf_op jit(solution)/shard_map/ppermute | solution.py:207
  26.6 14.6 %copy-start.1 = (bf16[1,1,64,128,128]{4,3,2,1,0:T(8,128)(2,1)S(1)}, bf16[1,1,64,128,128]{4,3,2,1,0:T(8,128)(2,1)}, u32[]{:S(2)}) copy-start(bf16[1,1,64,128,128]{4,3,2,1,0:T(8,128)(2,1)} %param.5) | copy-start | bytes 6291460
  26.6 14.6 %copy-start.4 = (s32[1,1,64]{2,1,0:T(1,128)S(1)}, s32[1,1,64]{2,1,0:T(1,128)}, u32[]{:S(2)}) copy-start(s32[1,1,64]{2,1,0:T(1,128)} %param.6) | copy-start | bytes 772
  26.6 14.6 %copy-start.6 = (s32[1,1,64]{2,1,0:T(1,128)S(1)}, s32[1,1,64]{2,1,0:T(1,128)}, u32[]{:S(2)}) copy-start(s32[1,1,64]{2,1,0:T(1,128)} %param.7) | copy-start | bytes 772
  37.3 4.0 %collective-permute-start.1 = (bf16[1024,256]{1,0:T(8,128)(2,1)S(1)}, bf16[1024,256]{1,0:T(8,128)(2,1)S(1)}, u32[]{:S(2)}, u32[]{:S(2)}) collective-permute-start(bf16[1024,256]{1,0:T(8,128)(2,1)S(1)} %bitcast.12), channel_id=1, source_target_pairs={{0,1},{1,0},{2,3},{3,2},{4,5},{5,4},{6,7},{7,6},{8,9},{9,8},{10,11... | collective-permute-start | bytes 1572872 | tf_op jit(solution)/shard_map/ppermute | solution.py:212

commit v2 on v1

--- a/solution.py
+++ b/solution.py
@@ -18,9 +18,12 @@
 ROWS = CB * TILE // PARTS
 EXTRA = 16
 GROUP = 4
-NB = 32
+NB = 64
+LOAD = 8
+PIECE = HALF // 4
 VMEM = pl.BlockSpec(memory_space=pltpu.VMEM)
 SMEM = pl.BlockSpec(memory_space=pltpu.SMEM)
+HBM = pl.BlockSpec(memory_space=pltpu.HBM)
 
 
 def dot(a, b, ca, cb, precision=None):
@@ -33,21 +36,41 @@
     return lax.broadcasted_iota(jnp.int32, shape, dim)
 
 
-def sketch_kernel(core_ref, rows_ref, cols_ref, live_ref, tiles_ref, omega_ref, keep_ref, send_ref, acc):
+def sketch_kernel(where_ref, rows_hbm, cols_hbm, live_hbm, tiles_hbm, omega_hbm, keep_ref, send_ref,
+                  acc, rows_ref, cols_ref, live_ref, tiles_ref, omega_ref, small_sem, tile_sem):
+    small = [
+        pltpu.make_async_copy(rows_hbm, rows_ref, small_sem.at[0]),
+        pltpu.make_async_copy(cols_hbm, cols_ref, small_sem.at[1]),
+        pltpu.make_async_copy(live_hbm, live_ref, small_sem.at[2]),
+        pltpu.make_async_copy(omega_hbm, omega_ref, small_sem.at[3]),
+    ]
+    big = [
+        pltpu.make_async_copy(
+            tiles_hbm.at[0, 0, pl.ds(g * LOAD, LOAD)], tiles_ref.at[pl.ds(g * LOAD, LOAD)], tile_sem.at[g]
+        )
+        for g in range(SLOTS // LOAD)
+    ]
+    for copy in small + big:
+        copy.start()
     acc[...] = jnp.zeros_like(acc)
-    live = live_ref[0]
-    turn = core_ref[0] * (RB // 2)
-
-    @pl.loop(0, (live + GROUP - 1) // GROUP)
-    def _(g):
-        prods, places = [], []
-        for i in range(GROUP):
-            t = g * GROUP + i
-            prod = dot(tiles_ref[t], omega_ref[cols_ref[t] & (CB - 1)], 1, 0)
-            prods.append(jnp.where(t < live, prod, 0.0))
-            places.append((rows_ref[t] + turn) & (RB - 1))
-        for prod, place in zip(prods, places):
-            acc[place] += prod
+    for copy in small:
+        copy.wait()
+    live = live_ref[0, 0]
+    core, chip = where_ref[0], where_ref[1]
+    for g, copy in enumerate(big):
+        copy.wait()
+
+        @pl.when(g * LOAD < live)
+        def _():
+            prods, places = [], []
+            for t in range(g * LOAD, (g + 1) * LOAD):
+                prod = dot(tiles_ref[t], omega_ref[cols_ref[0, 0, t] & (CB - 1)], 1, 0)
+                prods.append(jnp.where(t < live, prod, 0.0))
+                block = rows_ref[0, 0, t] & (RB - 1)
+                half = (block // 8 + core) & 1
+                places.append(half * 8 + ((block - 2 * chip) & 7))
+            for prod, place in zip(prods, places):
+                acc[place] += prod
 
     keep_ref[...] = acc[: RB // 2].reshape(HALF, K)
     send_ref[...] = acc[RB // 2 :].reshape(HALF, K)
@@ -59,10 +82,13 @@
     return jnp.where((p // 6) * EXTRA + p % 6 + shift == e, 1.0, 0.0).astype(dtype)
 
 
-def back_kernel(core_ref, rows_ref, cols_ref, live_ref, tiles_ref, mine_ref, other_ref, out_ref, s_ref, acc):
-    core = core_ref[0]
-    s_ref[pl.ds(core * (RB // 2), RB // 2)] = mine_ref[...].reshape(RB // 2, TILE, K)
-    s_ref[pl.ds((1 - core) * (RB // 2), RB // 2)] = other_ref[...].reshape(RB // 2, TILE, K)
+def back_kernel(where_ref, rows_ref, cols_ref, live_ref, tiles_ref, mine_ref, other_ref, out_ref, s_ref, acc):
+    core, chip = where_ref[0], where_ref[1]
+    for k in range(4):
+        at = ((chip - k) & 3) * 2
+        part = pl.ds(k * PIECE, PIECE)
+        s_ref[pl.ds(core * 8 + at, 2)] = mine_ref[part, :].reshape(2, TILE, K)
+        s_ref[pl.ds((1 - core) * 8 + at, 2)] = other_ref[part, :].reshape(2, TILE, K)
     acc[...] = jnp.zeros_like(acc)
     live = live_ref[0]
 
@@ -91,12 +117,28 @@
     out_ref[:, ROWS:, :] = extra.reshape(PARTS, EXTRA, K).astype(BF16)
 
 
+def resplit(extra):
+    row = iota(extra.shape, 0) % EXTRA
+    gram = extra + pltpu.roll(extra, extra.shape[0] - 6, 0)
+    high = gram.astype(BF16).astype(F32)
+    low = pltpu.roll(gram - high, 6, 0)
+    return jnp.where(row < 6, high, jnp.where(row < 12, low, 0.0))
+
+
+def partial_kernel(in_ref, out_ref):
+    total = in_ref[0].astype(F32)
+    for i in range(1, 4):
+        total = total + in_ref[i].astype(F32)
+    out_ref[:, :ROWS, :] = total[:, :ROWS, :].astype(BF16)
+    extra = resplit(total[:, ROWS:, :].reshape(8 * EXTRA, K))
+    out_ref[:, ROWS:, :] = extra.reshape(8, EXTRA, K).astype(BF16)
+
+
 def sum_kernel(in_ref, out_ref):
     total = in_ref[0].astype(F32)
-    for i in range(1, PARTS):
+    for i in range(1, 8):
         total = total + in_ref[i].astype(F32)
     w = total[:ROWS]
-    extra = total[ROWS:]
     mean = jnp.sum(w, axis=0, keepdims=True) * (1.0 / ROWS)
     top = jnp.max(jnp.abs(mean), axis=1, keepdims=True)
     lead = (mean / jnp.maximum(top, 1e-30)).astype(BF16)
@@ -105,36 +147,67 @@
     coef = (dot(lead, w.astype(BF16), 1, 1) / norm).astype(BF16)
     rest = w - dot(coef, lead, 0, 0)
     row = iota((EXTRA, K), 0)
-    gram = extra + pltpu.roll(extra, EXTRA - 6, 0)
-    high = gram.astype(BF16).astype(F32)
-    low = pltpu.roll(gram - high, 6, 0)
     wide = jnp.concatenate([coef.astype(F32), jnp.zeros((1, K - ROWS), F32)], axis=1)
-    tail = jnp.where(row < 6, high, jnp.where(row < 12, low, 0.0))
-    tail = jnp.where(row == 12, leadf, jnp.where(row == 13, wide, tail))
+    tail = jnp.where(row == 12, leadf, jnp.where(row == 13, wide, resplit(total[ROWS:])))
     body = rest.astype(BF16)
     tail = tail.astype(BF16)
-    for i in range(PARTS):
+    for i in range(8):
         out_ref[i, :ROWS, :] = body
         out_ref[i, ROWS:, :] = tail
 
 
+def eliminate(x):
+    groups = NB // 8
+    xs = [x[8 * g : 8 * g + 8] for g in range(groups)]
+    sub = iota((8, 128), 0)
+
+    def wide(a):
+        return jnp.broadcast_to(a, (8, 128))
+
+    for t in range(groups):
+        at = 8 * t
+        head = xs[t]
+        cols = [wide(head[:, at + m : at + m + 1]) for m in range(8)]
+        s = [[wide(cols[m][i : i + 1, :]) if m >= i else None for m in range(8)] for i in range(8)]
+        rows = [wide(head[i : i + 1, :]) for i in range(8)]
+        ratio = [[None] * 8 for _ in range(8)]
+        scaled = []
+        for j in range(8):
+            inv = pltpu.reciprocal(s[j][j], approx=True)
+            inv = inv * (2.0 - s[j][j] * inv)
+            for m in range(j + 1, 8):
+                ratio[j][m] = s[j][m] * inv
+            for i in range(j + 1, 8):
+                for m in range(i, 8):
+                    s[i][m] = s[i][m] - ratio[j][i] * s[j][m]
+                rows[i] = rows[i] - ratio[j][i] * rows[j]
+            scaled.append(rows[j] * inv)
+        for g in range(t + 1, groups):
+            left, x = [], xs[g]
+            for j in range(8):
+                e = wide(xs[g][:, at + j : at + j + 1])
+                for m in range(j):
+                    e = e - ratio[m][j] * left[m]
+                left.append(e)
+                x = x - e * scaled[j]
+            xs[g] = x
+        out = rows[0] * lax.rsqrt(s[0][0])
+        for j in range(1, 8):
+            out = jnp.where(sub == j, rows[j] * lax.rsqrt(s[j][j]), out)
+        xs[t] = out
+    return jnp.concatenate(xs, axis=0)
+
+
 def factor(work):
+    lane = iota((NB, 128), 1)
+    row = iota((NB, 128), 0)
     for b in range(K // NB):
         at = b * NB
         base = at // 128 * 128
         x = work[at : at + NB, base : base + 128]
         if at > base:
             x = pltpu.roll(x, 128 - (at - base), 1)
-        lane = iota((NB, 128), 1)
-        row = iota((NB, 128), 0)
-        x = jnp.where(lane < NB, x, jnp.where(lane - NB == row, 1.0, 0.0))
-        for j in range(NB):
-            pivot = x[j : j + 1, :]
-            scale = 1.0 / pivot[:, j : j + 1]
-            m = jnp.where(row[:, :1] > j, x[:, j : j + 1] * scale, 0.0)
-            x = x - m * pivot
-        diag = jnp.sum(jnp.where(lane == row, x, 0.0), axis=1, keepdims=True)
-        x = x * lax.rsqrt(diag)
+        x = eliminate(jnp.where(lane < NB, x, jnp.where(lane - NB == row, 1.0, 0.0)))
         inv = pltpu.roll(x, 128 - NB, 1)[:, :NB]
         u = dot(inv, work[at : at + NB, :], 1, 0, lax.Precision.HIGHEST)
         work[at : at + NB, :] = u
@@ -143,7 +216,7 @@
             work[at + NB :, :] -= dot(ut[at + NB :], u, 1, 0, lax.Precision.HIGHEST)
 
 
-def final_kernel(core_ref, in_ref, mine_ref, other_ref, q_ref, r_ref, z_ref, work):
+def final_kernel(where_ref, in_ref, mine_ref, other_ref, q_ref, r_ref, z_ref, work):
     extra = in_ref[:, ROWS:, :].reshape(PARTS * EXTRA, K)
     p = iota((192, PARTS * EXTRA), 0)
     e = iota((192, PARTS * EXTRA), 1)
@@ -164,9 +237,11 @@
     def solve(a):
         return dot(a, high, 1, 1) + dot(a, low, 1, 1)
 
-    core = core_ref[0]
-    q_ref[pl.ds(pl.multiple_of(core * HALF, HALF), HALF), :] = solve(mine_ref[...]).astype(BF16)
-    q_ref[pl.ds(pl.multiple_of((1 - core) * HALF, HALF), HALF), :] = solve(other_ref[...]).astype(BF16)
+    core, chip = where_ref[0], where_ref[1]
+    for half, ref in ((core, mine_ref), (1 - core, other_ref)):
+        for k in range(4):
+            at = pl.multiple_of(half * HALF + ((chip - k) & 3) * PIECE, PIECE)
+            q_ref[pl.ds(at, PIECE), :] = solve(ref[k * PIECE : (k + 1) * PIECE, :]).astype(BF16)
     i = iota((2 * PARTS, PARTS * EXTRA), 0)
     e = iota((2 * PARTS, PARTS * EXTRA), 1)
     want = jnp.where(i < PARTS, i * EXTRA + 12, (i - PARTS) * EXTRA + 13)
@@ -189,26 +264,37 @@
 
 
 def on_device(tiles, block_rows, block_cols, tile_counts, omega):
-    core = lax.axis_index("c").astype(jnp.int32).reshape(1)
-    rows = block_rows[0, 0]
-    cols = block_cols[0, 0]
-    live = tile_counts[0]
-    tiles = tiles[0, 0]
+    where = jnp.stack([lax.axis_index("c"), lax.axis_index("y")]).astype(jnp.int32)
+    swap = [(0, 1), (1, 0)]
     keep, send = pl.pallas_call(
         sketch_kernel,
         out_shape=(shape(HALF, K), shape(HALF, K)),
-        in_specs=[SMEM] * 4 + [VMEM] * 2,
+        in_specs=[SMEM] + [HBM] * 5,
         out_specs=(VMEM, VMEM),
-        scratch_shapes=[pltpu.VMEM((RB, TILE, K), F32)],
+        scratch_shapes=[
+            pltpu.VMEM((RB, TILE, K), F32),
+            pltpu.SMEM((1, 1, SLOTS), jnp.int32),
+            pltpu.SMEM((1, 1, SLOTS), jnp.int32),
+            pltpu.SMEM((1, 1), jnp.int32),
+            pltpu.VMEM((SLOTS, TILE, TILE), BF16),
+            pltpu.VMEM((CB, TILE, K), BF16),
+            pltpu.SemaphoreType.DMA((4,)),
+            pltpu.SemaphoreType.DMA((SLOTS // LOAD,)),
+        ],
         compiler_params=LIMIT,
         name="sketch",
-    )(core, rows, cols, live, tiles, omega.reshape(CB, TILE, K))
-    swap = [(0, 1), (1, 0)]
+    )(where, block_rows, block_cols, tile_counts, tiles, omega.reshape(CB, TILE, K))
+
+    def turn(a, k):
+        return lax.ppermute(a, "y", [(i, (i + k) % 4) for i in range(4)])
+
     half = keep + lax.ppermute(send, "c", swap)
-    quarters = lax.all_to_all(half.astype(BF16).reshape(4, HALF // 4, K), "y", 0, 0, tiled=True)
-    shard = jnp.sum(quarters.astype(F32), axis=0).astype(BF16)
-    spread = jnp.broadcast_to(shard[None], (4, HALF // 4, K))
-    mine = lax.all_to_all(spread, "y", 0, 0, tiled=True).reshape(HALF, K)
+    quarters = half.reshape(4, PIECE, K)
+    shard = quarters[0]
+    for k in (2, 1, 3):
+        shard = shard + turn(quarters[k].astype(BF16), k).astype(F32)
+    shard = shard.astype(BF16)
+    mine = jnp.concatenate([shard] + [turn(shard, k) for k in (1, 2, 3)], axis=0)
     other = lax.ppermute(mine, "c", swap)
     payload = pl.pallas_call(
         back_kernel,
@@ -218,17 +304,27 @@
         scratch_shapes=[pltpu.VMEM((RB, TILE, K), BF16), pltpu.VMEM((CB, TILE, K), F32)],
         compiler_params=LIMIT,
         name="back",
-    )(core, rows, cols, live, tiles, mine, other)
-    parts = lax.all_to_all(payload, ("z", "x"), 0, 0, tiled=True)
+    )(where, block_rows[0, 0], block_cols[0, 0], tile_counts[0], tiles[0, 0], mine, other)
+    size = (ROWS + EXTRA, K)
+    parts = lax.all_to_all(payload.reshape(4, 8, *size), "x", 0, 0, tiled=True)
+    parts = pl.pallas_call(
+        partial_kernel,
+        out_shape=shape(8, *size, dtype=BF16),
+        in_specs=[VMEM],
+        out_specs=VMEM,
+        compiler_params=LIMIT,
+        name="partial",
+    )(parts)
     spread = pl.pallas_call(
         sum_kernel,
-        out_shape=shape(PARTS, ROWS + EXTRA, K, dtype=BF16),
+        out_shape=shape(8, *size, dtype=BF16),
         in_specs=[VMEM],
         out_specs=VMEM,
         compiler_params=LIMIT,
         name="total",
-    )(parts)
-    whole = lax.all_to_all(spread, ("z", "x"), 0, 0, tiled=True)
+    )(lax.all_to_all(parts, "z", 0, 0, tiled=True))
+    line = lax.all_to_all(spread, "z", 0, 0, tiled=True)
+    whole = lax.all_to_all(jnp.broadcast_to(line[None], (4, 8, *size)), "x", 0, 0, tiled=True)
     return pl.pallas_call(
         final_kernel,
         out_shape=(shape(2 * HALF, K, dtype=BF16), shape(K, K), shape(CB * TILE, K)),
@@ -237,7 +333,7 @@
         scratch_shapes=[pltpu.VMEM((K, 2 * K), F32)],
         compiler_params=LIMIT,
         name="finish",
-    )(core, whole, mine, other)
+    )(where, whole.reshape(PARTS, *size), mine, other)
 
 
 def solution(mesh):

time: 164 us -> 136 us (0.83); the launches traced: 164 us -> 138 us
  blocking collectives: 111 us -> 77.9 us
  waiting for transfers between devices: 3.82 us -> 19.2 us
  Pallas kernels: 36.9 us -> 24.9 us
  starting transfers between devices: 6.74 us -> 10.1 us
    all_to_all x4, blocking collectives: 111 us -> 77.9 us  [the longest x1 25 us: on_device(): lax.all_to_all(parts, 'z', 0, 0, tiled=True)]
    ppermute x0 -> x6, waiting for transfers between devices: none -> 15.4 us  [turn(): return lax.ppermute(a, 'y', [(i, (i + k) % 4) for i in range(4)])]
    pallas_call x1, Pallas kernels: 31.7 us -> 17.8 us  [on_device(): pl.pallas_call(final_kernel, out_shape=(shape(2 * HALF, K, dtype=BF16), s...]
    ppermute x0 -> x6, starting transfers between devices: none -> 4.84 us  [turn(): return lax.ppermute(a, 'y', [(i, (i + k) % 4) for i in range(4)])]
    ppermute x1, starting transfers between devices: 2.48 us -> 0.73 us  [on_device(): other = lax.ppermute(mine, 'c', swap)]
    unnamed x14 -> x8, local copies, waits for them, and re-layouts: 4.13 us -> 4.12 us
  transfers between devices with their start and end apart: 2 -> 8, of which waited for: 2 -> 8; matrix products, arithmetic and copies ran while one was open for 0% -> 0% of each run, Pallas kernels for 0% -> 0%
where the time goes in v2:
time: 136 us; the launch traced here: 138 us
  blocking collectives  77.9 us (57%)
  Pallas kernels  24.9 us (18%)
  waiting for transfers between devices  19.2 us (14%)
  starting transfers between devices  10.1 us (7%)
  local copies, waits for them, and re-layouts  4.24 us (3%)
    all_to_all x1, blocking collectives, on_device(): lax.all_to_all(parts, 'z', 0, 0, tiled=True)  25 us
    all_to_all x1, blocking collectives, on_device(): lax.all_to_all(jnp.broadcast_to(line[None], (4, 8, *size)), 'x', 0, 0, ti...  20.8 us
    all_to_all x1, blocking collectives, on_device(): parts = lax.all_to_all(payload.reshape(4, 8, *size), 'x', 0, 0, tiled=True)  18.6 us
    pallas_call x1, Pallas kernels, on_device(): pl.pallas_call(final_kernel, out_shape=(shape(2 * HALF, K, dtype=BF16), s...  17.8 us
    ppermute x6, waiting for transfers between devices, turn(): return lax.ppermute(a, 'y', [(i, (i + k) % 4) for i in range(4)])  15.4 us
    all_to_all x1, blocking collectives, on_device(): line = lax.all_to_all(spread, 'z', 0, 0, tiled=True)  13.4 us
    ppermute x6, starting transfers between devices, turn(): return lax.ppermute(a, 'y', [(i, (i + k) % 4) for i in range(4)])  4.84 us
    ppermute x1, starting transfers between devices, on_device(): half = keep + lax.ppermute(send, 'c', swap)  4.51 us
  transfers between devices with their start and end apart: 8, of which 8 were waited for; matrix products, arithmetic and copies ran while one was open for 0% of the time, Pallas kernels for 0%

profile of v2, /device:TPU:1, one launch (start us, length us, event | category | flops | bytes accessed | tf_op | source)
XLA Modules:
  0.0 138.0 jit_solution(4560007511441851454)
XLA Ops:
  1.3 0.1 pad_add_fusion.where_ref
  1.4 0.0 copy-start
  1.4 1.6 %copy-done = bf16[1,1,64,128,128]{4,3,2,1,0:T(8,128)(2,1)S(1)} copy-done((bf16[1,1,64,128,128]{4,3,2,1,0:T(8,128)(2,1)S(1)}, bf16[1,1,64,128,128]{4,3,2,1,0:T(8,128)(2,1)}, u32[]{:S(2)}) %copy-start) | copy-done | bytes 2097176
  2.9 0.0 copy-start.1
  2.9 1.2 copy-done.1
  4.2 0.0 copy-start.2
  4.2 0.7 copy-done.2
  4.8 0.0 copy-start.3
  4.8 0.7 copy-done.3
  5.5 2.6 %sketch.1 = (f32[1024,256]{1,0:T(8,128)S(1)}, f32[1024,256]{1,0:T(8,128)S(1)}) custom-call(s32[2]{0:T(128)S(1)} %pad_add_fusion.where_ref, s32[1,1,64]{2,1,0:T(1,128)S(1)} %copy-done.2, s32[1,1,64]{2,1,0:T(1,128)S(1)} %copy-done.3, s32[1,1]{1,0:T(1,128)} %copy.8.live_hbm, bf16[1,1,64,128,128]{4,3,2,1,0:T(8,128)(2,1)S(1)} %copy-done, ...), custom_call_target="tpu_custom_call" | custom-call | tf_op jit(solution)/shard_map/sketch/pallas_call | solution.py:269
  8.1 4.5 %collective-permute-start = (f32[1024,256]{1,0:T(8,128)S(1)}, f32[1024,256]{1,0:T(8,128)S(1)}, u32[]{:S(2)}, u32[]{:S(2)}) collective-permute-start(f32[1024,256]{1,0:T(8,128)S(1)} %get-tuple-element.6), channel_id=1, source_target_pairs={{0,1},{1,0},{2,3},{3,2},{4,5},{5,4},{6,7},{7,6},{8,9},{9,8},{10,11... | collective-permute-start | bytes 3145736 | tf_op jit(solution)/shard_map/ppermute | solution.py:291
  12.6 2.3 %collective-permute-done = f32[1024,256]{1,0:T(8,128)S(1)} collective-permute-done((f32[1024,256]{1,0:T(8,128)S(1)}, f32[1024,256]{1,0:T(8,128)S(1)}, u32[]{:S(2)}, u32[]{:S(2)}) %collective-permute-start) | collective-permute-done | bytes 1048608 | tf_op jit(solution)/shard_map/ppermute | solution.py:291
  14.8 0.2 fusion.3
  15.0 1.3 collective-permute-start.1
  16.3 0.0 collective-permute-start.3
  16.3 1.5 %collective-permute-start.2 = (bf16[256,256]{1,0:T(8,128)(2,1)S(1)}, bf16[256,256]{1,0:T(8,128)(2,1)S(1)}, u32[]{:S(2)}, u32[]{:S(2)}) collective-permute-start(bf16[256,256]{1,0:T(8,128)(2,1)S(1)} %get-tuple-element.11), channel_id=1, source_target_pairs={{0,2},{2,4},{4,6},{6,0},{1,3},{3,5},{5,7},{7,1},{8,10},{10,12},{12... | collective-permute-start | bytes 393224 | tf_op jit(solution)/shard_map/ppermute | solution.py:289
  17.8 3.6 %collective-permute-done.1 = bf16[256,256]{1,0:T(8,128)(2,1)S(1)} collective-permute-done((bf16[256,256]{1,0:T(8,128)(2,1)S(1)}, bf16[256,256]{1,0:T(8,128)(2,1)S(1)}, u32[]{:S(2)}, u32[]{:S(2)}) %collective-permute-start.1) | collective-permute-done | bytes 131104 | tf_op jit(solution)/shard_map/ppermute | solution.py:289
  21.3 1.5 %collective-permute-done.3 = bf16[256,256]{1,0:T(8,128)(2,1)S(1)} collective-permute-done((bf16[256,256]{1,0:T(8,128)(2,1)S(1)}, bf16[256,256]{1,0:T(8,128)(2,1)S(1)}, u32[]{:S(2)}, u32[]{:S(2)}) %collective-permute-start.3) | collective-permute-done | bytes 131104 | tf_op jit(solution)/shard_map/ppermute | solution.py:289
  22.8 2.1 %collective-permute-done.2 = bf16[256,256]{1,0:T(8,128)(2,1)S(1)} collective-permute-done((bf16[256,256]{1,0:T(8,128)(2,1)S(1)}, bf16[256,256]{1,0:T(8,128)(2,1)S(1)}, u32[]{:S(2)}, u32[]{:S(2)}) %collective-permute-start.2) | collective-permute-done | bytes 131104 | tf_op jit(solution)/shard_map/ppermute | solution.py:289
  24.9 0.1 fusion.2
  24.9 0.9 collective-permute-start.6
  25.8 0.5 collective-permute-start.5
  26.3 0.8 collective-permute-start.4
  27.0 2.5 %collective-permute-done.6 = bf16[256,256]{1,0:T(8,128)(2,1)S(1)} collective-permute-done((bf16[256,256]{1,0:T(8,128)(2,1)S(1)}, bf16[256,256]{1,0:T(8,128)(2,1)S(1)}, u32[]{:S(2)}, u32[]{:S(2)}) %collective-permute-start.6) | collective-permute-done | bytes 131104 | tf_op jit(solution)/shard_map/ppermute | solution.py:289
  29.6 1.8 %collective-permute-done.5 = bf16[256,256]{1,0:T(8,128)(2,1)S(1)} collective-permute-done((bf16[256,256]{1,0:T(8,128)(2,1)S(1)}, bf16[256,256]{1,0:T(8,128)(2,1)S(1)}, u32[]{:S(2)}, u32[]{:S(2)}) %collective-permute-start.5) | collective-permute-done | bytes 131104 | tf_op jit(solution)/shard_map/ppermute | solution.py:289
  31.4 4.0 %collective-permute-done.4 = bf16[256,256]{1,0:T(8,128)(2,1)S(1)} collective-permute-done((bf16[256,256]{1,0:T(8,128)(2,1)S(1)}, bf16[256,256]{1,0:T(8,128)(2,1)S(1)}, u32[]{:S(2)}, u32[]{:S(2)}) %collective-permute-start.4) | collective-permute-done | bytes 131104 | tf_op jit(solution)/shard_map/ppermute | solution.py:289
  35.4 0.7 collective-permute-start.7
  36.1 1.5 %collective-permute-done.7.other_ref = bf16[1024,256]{1,0:T(8,128)(2,1)S(1)} collective-permute-done((bf16[1024,256]{1,0:T(8,128)(2,1)S(1)}, bf16[1024,256]{1,0:T(8,128)(2,1)S(1)}, u32[]{:S(2)}, u32[]{:S(2)}) %collective-permute-start.7) | collective-permute-done | bytes 524320 | tf_op jit(solution)/shard_map/ppermute | solution.py:298
  37.7 3.9 %back.1 = bf16[32,80,256]{2,1,0:T(8,128)(2,1)S(1)} custom-call(s32[2]{0:T(128)S(1)} %pad_add_fusion.where_ref, s32[64]{0:T(128)S(1)} %bitcast.14, s32[64]{0:T(128)S(1)} %bitcast.15, s32[1]{0:T(128)} %bitcast.9.live_ref, bf16[64,128,128]{2,1,0:T(8,128)(2,1)S(1)} %bitcast.10, bf16[1024,256]{1,0:T(8,128)(2,1)S(1)} %pad_maximum_fusion.mine_ref, ...), custom_call_target="tpu_custom_call" | custom-call | tf_op jit(solution)/shard_map/back/pallas_call | solution.py:299
  41.6 18.6 %all_to_all.20.in_ref = bf16[4,8,80,256]{3,2,1,0:T(8,128)(2,1)S(1)} all-to-all(bf16[4,8,80,256]{3,2,1,0:T(8,128)(2,1)S(1)} %bitcast.12), channel_id=1, replica_groups=mesh['z'=8,'x'=4,'y'=4,'c'=2] {'x'}, dimensions={0} | all-to-all | bytes 2621440 | tf_op jit(solution)/shard_map/all_to_all | solution.py:309
  60.2 0.2 partial.1
  60.4 25.0 %all_to_all.21.in_ref = bf16[8,80,256]{2,1,0:T(8,128)(2,1)S(1)} all-to-all(bf16[8,80,256]{2,1,0:T(8,128)(2,1)S(1)} %partial.1), channel_id=1, replica_groups=mesh['z'=8,'x'=4,'y'=4,'c'=2] {'z'}, dimensions={0} | all-to-all | bytes 655360 | tf_op jit(solution)/shard_map/all_to_all | solution.py:325
  85.4 0.4 total.1
  85.8 13.4 %all_to_all.22 = bf16[8,80,256]{2,1,0:T(8,128)(2,1)S(1)} all-to-all(bf16[8,80,256]{2,1,0:T(8,128)(2,1)S(1)} %total.1), channel_id=1, replica_groups=mesh['z'=8,'x'=4,'y'=4,'c'=2] {'z'}, dimensions={0} | all-to-all | bytes 655360 | tf_op jit(solution)/shard_map/all_to_all | solution.py:326
  99.2 0.1 broadcast_in_dim.2
  99.3 20.8 %all_to_all.23 = bf16[4,8,80,256]{3,2,1,0:T(8,128)(2,1)S(1)} all-to-all(bf16[4,8,80,256]{3,2,1,0:T(8,128)(2,1)S(1)} %broadcast_in_dim.2), channel_id=1, replica_groups=mesh['z'=8,'x'=4,'y'=4,'c'=2] {'x'}, dimensions={0} | all-to-all | bytes 2621440 | tf_op jit(solution)/shard_map/all_to_all | solution.py:327
  120.2 17.8 %finish.1 = (bf16[2048,256]{1,0:T(8,128)(2,1)}, f32[256,256]{1,0:T(8,128)}, f32[2048,256]{1,0:T(8,128)}) custom-call(s32[2]{0:T(128)S(1)} %pad_add_fusion.where_ref, bf16[32,80,256]{2,1,0:T(8,128)(2,1)S(1)} %bitcast.11, bf16[1024,256]{1,0:T(8,128)(2,1)S(1)} %pad_maximum_fusion.mine_ref, bf16[1024,256]{1,0:T(8,128)(2,1)S(1)} %collective-permute-done.7.other_ref), custom_call_target="tpu_custom_call" | custom-call | tf_op jit(solution)/shard_map/finish/pallas_call | solution.py:328
  (2 shorter events, 0.1 us)
Async XLA Ops:
  1.4 1.6 %copy-start = (bf16[1,1,64,128,128]{4,3,2,1,0:T(8,128)(2,1)S(1)}, bf16[1,1,64,128,128]{4,3,2,1,0:T(8,128)(2,1)}, u32[]{:S(2)}) copy-start(bf16[1,1,64,128,128]{4,3,2,1,0:T(8,128)(2,1)} %tiles_hbm.1) | copy-start | bytes 6291460
  2.9 1.2 copy-start.1
  4.2 0.7 copy-start.2
  4.8 0.7 copy-start.3
  8.1 6.8 %collective-permute-start = (f32[1024,256]{1,0:T(8,128)S(1)}, f32[1024,256]{1,0:T(8,128)S(1)}, u32[]{:S(2)}, u32[]{:S(2)}) collective-permute-start(f32[1024,256]{1,0:T(8,128)S(1)} %get-tuple-element.6), channel_id=1, source_target_pairs={{0,1},{1,0},{2,3},{3,2},{4,5},{5,4},{6,7},{7,6},{8,9},{9,8},{10,11... | collective-permute-start | bytes 3145736 | tf_op jit(solution)/shard_map/ppermute | solution.py:291
  15.0 6.3 %collective-permute-start.1 = (bf16[256,256]{1,0:T(8,128)(2,1)S(1)}, bf16[256,256]{1,0:T(8,128)(2,1)S(1)}, u32[]{:S(2)}, u32[]{:S(2)}) collective-permute-start(bf16[256,256]{1,0:T(8,128)(2,1)S(1)} %get-tuple-element.9), channel_id=1, source_target_pairs={{0,4},{2,6},{4,0},{6,2},{1,5},{3,7},{5,1},{7,3},{8,12},{10,14},{12... | collective-permute-start | bytes 393224 | tf_op jit(solution)/shard_map/ppermute | solution.py:289
  16.3 6.5 %collective-permute-start.3 = (bf16[256,256]{1,0:T(8,128)(2,1)S(1)}, bf16[256,256]{1,0:T(8,128)(2,1)S(1)}, u32[]{:S(2)}, u32[]{:S(2)}) collective-permute-start(bf16[256,256]{1,0:T(8,128)(2,1)S(1)} %get-tuple-element.10), channel_id=1, source_target_pairs={{0,6},{2,0},{4,2},{6,4},{1,7},{3,1},{5,3},{7,5},{8,14},{10,8},{12,... | collective-permute-start | bytes 393224 | tf_op jit(solution)/shard_map/ppermute | solution.py:289
  16.3 8.6 %collective-permute-start.2 = (bf16[256,256]{1,0:T(8,128)(2,1)S(1)}, bf16[256,256]{1,0:T(8,128)(2,1)S(1)}, u32[]{:S(2)}, u32[]{:S(2)}) collective-permute-start(bf16[256,256]{1,0:T(8,128)(2,1)S(1)} %get-tuple-element.11), channel_id=1, source_target_pairs={{0,2},{2,4},{4,6},{6,0},{1,3},{3,5},{5,7},{7,1},{8,10},{10,12},{12... | collective-permute-start | bytes 393224 | tf_op jit(solution)/shard_map/ppermute | solution.py:289
  24.9 4.7 %collective-permute-start.6 = (bf16[256,256]{1,0:T(8,128)(2,1)S(1)}, bf16[256,256]{1,0:T(8,128)(2,1)S(1)}, u32[]{:S(2)}, u32[]{:S(2)}) collective-permute-start(bf16[256,256]{1,0:T(8,128)(2,1)S(1)} %fusion.2), channel_id=1, source_target_pairs={{0,6},{2,0},{4,2},{6,4},{1,7},{3,1},{5,3},{7,5},{8,14},{10,8},{12,... | collective-permute-start | bytes 393224 | tf_op jit(solution)/shard_map/ppermute | solution.py:289
  25.8 5.6 %collective-permute-start.5 = (bf16[256,256]{1,0:T(8,128)(2,1)S(1)}, bf16[256,256]{1,0:T(8,128)(2,1)S(1)}, u32[]{:S(2)}, u32[]{:S(2)}) collective-permute-start(bf16[256,256]{1,0:T(8,128)(2,1)S(1)} %fusion.2), channel_id=1, source_target_pairs={{0,4},{2,6},{4,0},{6,2},{1,5},{3,7},{5,1},{7,3},{8,12},{10,14},{12... | collective-permute-start | bytes 393224 | tf_op jit(solution)/shard_map/ppermute | solution.py:289
  26.3 9.1 %collective-permute-start.4 = (bf16[256,256]{1,0:T(8,128)(2,1)S(1)}, bf16[256,256]{1,0:T(8,128)(2,1)S(1)}, u32[]{:S(2)}, u32[]{:S(2)}) collective-permute-start(bf16[256,256]{1,0:T(8,128)(2,1)S(1)} %fusion.2), channel_id=1, source_target_pairs={{0,2},{2,4},{4,6},{6,0},{1,3},{3,5},{5,7},{7,1},{8,10},{10,12},{12... | collective-permute-start | bytes 393224 | tf_op jit(solution)/shard_map/ppermute | solution.py:289
  35.4 2.3 %collective-permute-start.7 = (bf16[1024,256]{1,0:T(8,128)(2,1)S(1)}, bf16[1024,256]{1,0:T(8,128)(2,1)S(1)}, u32[]{:S(2)}, u32[]{:S(2)}) collective-permute-start(bf16[1024,256]{1,0:T(8,128)(2,1)S(1)} %pad_maximum_fusion.mine_ref), channel_id=1, source_target_pairs={{0,1},{1,0},{2,3},{3,2},{4,5},{5,4},{6,7},{7,6},{8,9},{9,8},{10,11... | collective-permute-start | bytes 1572872 | tf_op jit(solution)/shard_map/ppermute | solution.py:298

commit v3 on v2

--- a/solution.py
+++ b/solution.py
@@ -20,6 +20,9 @@
 GROUP = 4
 NB = 64
 LOAD = 8
+LIVE = 3
+AT = 4
+COLS = AT + SLOTS
 PIECE = HALF // 4
 VMEM = pl.BlockSpec(memory_space=pltpu.VMEM)
 SMEM = pl.BlockSpec(memory_space=pltpu.SMEM)
@@ -36,27 +39,22 @@
     return lax.broadcasted_iota(jnp.int32, shape, dim)
 
 
-def sketch_kernel(where_ref, rows_hbm, cols_hbm, live_hbm, tiles_hbm, omega_hbm, keep_ref, send_ref,
-                  acc, rows_ref, cols_ref, live_ref, tiles_ref, omega_ref, small_sem, tile_sem):
-    small = [
-        pltpu.make_async_copy(rows_hbm, rows_ref, small_sem.at[0]),
-        pltpu.make_async_copy(cols_hbm, cols_ref, small_sem.at[1]),
-        pltpu.make_async_copy(live_hbm, live_ref, small_sem.at[2]),
-        pltpu.make_async_copy(omega_hbm, omega_ref, small_sem.at[3]),
-    ]
+def sketch_kernel(meta_ref, tiles_hbm, omega_hbm, keep_ref, send_ref, acc, tiles_ref, omega_ref, omega_sem, tile_sem):
+    test = pltpu.make_async_copy(omega_hbm, omega_ref, omega_sem)
     big = [
         pltpu.make_async_copy(
             tiles_hbm.at[0, 0, pl.ds(g * LOAD, LOAD)], tiles_ref.at[pl.ds(g * LOAD, LOAD)], tile_sem.at[g]
         )
         for g in range(SLOTS // LOAD)
     ]
-    for copy in small + big:
+    big[0].start()
+    test.start()
+    for copy in big[1:]:
         copy.start()
     acc[...] = jnp.zeros_like(acc)
-    for copy in small:
-        copy.wait()
-    live = live_ref[0, 0]
-    core, chip = where_ref[0], where_ref[1]
+    live = meta_ref[LIVE]
+    core, chip = meta_ref[0], meta_ref[1]
+    test.wait()
     for g, copy in enumerate(big):
         copy.wait()
 
@@ -64,9 +62,9 @@
         def _():
             prods, places = [], []
             for t in range(g * LOAD, (g + 1) * LOAD):
-                prod = dot(tiles_ref[t], omega_ref[cols_ref[0, 0, t] & (CB - 1)], 1, 0)
+                prod = dot(tiles_ref[t], omega_ref[meta_ref[COLS + t] & (CB - 1)], 1, 0)
                 prods.append(jnp.where(t < live, prod, 0.0))
-                block = rows_ref[0, 0, t] & (RB - 1)
+                block = meta_ref[AT + t] & (RB - 1)
                 half = (block // 8 + core) & 1
                 places.append(half * 8 + ((block - 2 * chip) & 7))
             for prod, place in zip(prods, places):
@@ -82,24 +80,33 @@
     return jnp.where((p // 6) * EXTRA + p % 6 + shift == e, 1.0, 0.0).astype(dtype)
 
 
-def back_kernel(where_ref, rows_ref, cols_ref, live_ref, tiles_ref, mine_ref, other_ref, out_ref, s_ref, acc):
-    core, chip = where_ref[0], where_ref[1]
+def flip_kernel(meta_ref, tiles_ref, out_ref):
+    live = meta_ref[LIVE]
+
+    @pl.loop(0, SLOTS // GROUP)
+    def _(g):
+        for i in range(GROUP):
+            t = g * GROUP + i
+            tile = tiles_ref[t].T
+            out_ref[t] = jnp.where(t < live, tile, jnp.zeros_like(tile))
+
+
+def back_kernel(meta_ref, tiles_ref, mine_ref, other_ref, out_ref, s_ref, acc):
+    core, chip = meta_ref[0], meta_ref[1]
     for k in range(4):
         at = ((chip - k) & 3) * 2
         part = pl.ds(k * PIECE, PIECE)
         s_ref[pl.ds(core * 8 + at, 2)] = mine_ref[part, :].reshape(2, TILE, K)
         s_ref[pl.ds((1 - core) * 8 + at, 2)] = other_ref[part, :].reshape(2, TILE, K)
     acc[...] = jnp.zeros_like(acc)
-    live = live_ref[0]
-
-    @pl.loop(0, (live + GROUP - 1) // GROUP)
+
+    @pl.loop(0, (meta_ref[LIVE] + LOAD - 1) // LOAD)
     def _(g):
         prods, places = [], []
-        for i in range(GROUP):
-            t = g * GROUP + i
-            prod = dot(tiles_ref[t], s_ref[rows_ref[t] & (RB - 1)], 0, 0)
-            prods.append(jnp.where(t < live, prod, 0.0))
-            places.append(cols_ref[t] & (CB - 1))
+        for i in range(LOAD):
+            t = g * LOAD + i
+            prods.append(dot(tiles_ref[t], s_ref[meta_ref[AT + t] & (RB - 1)], 1, 0))
+            places.append(meta_ref[COLS + t] & (CB - 1))
         for prod, place in zip(prods, places):
             acc[place] += prod
 
@@ -216,11 +223,13 @@
             work[at + NB :, :] -= dot(ut[at + NB :], u, 1, 0, lax.Precision.HIGHEST)
 
 
-def final_kernel(where_ref, in_ref, mine_ref, other_ref, q_ref, r_ref, z_ref, work):
-    extra = in_ref[:, ROWS:, :].reshape(PARTS * EXTRA, K)
+def factor_kernel(meta_ref, e0_ref, e1_ref, e2_ref, e3_ref, mine_ref, other_ref,
+                  q_ref, r_ref, inv_ref, lead_ref, coef_ref, work):
+    extra = jnp.concatenate([e[...].reshape(8 * EXTRA, K) for e in (e0_ref, e1_ref, e2_ref, e3_ref)], axis=0)
     p = iota((192, PARTS * EXTRA), 0)
     e = iota((192, PARTS * EXTRA), 1)
-    first = (p // 6) * EXTRA + p % 6
+    slot = p // 6
+    first = (((meta_ref[2] - slot // 8) & 3) * 8 + slot % 8) * EXTRA + p % 6
     pick = jnp.where((e == first) | (e == first + 6), 1.0, 0.0).astype(BF16)
     packed = dot(pick, extra, 1, 0)
     work[: K // 2, :K] = packed[: K // 2]
@@ -233,27 +242,38 @@
     inv = work[:, K:]
     high = inv.astype(BF16)
     low = (inv - high.astype(F32)).astype(BF16)
-
-    def solve(a):
-        return dot(a, high, 1, 1) + dot(a, low, 1, 1)
-
-    core, chip = where_ref[0], where_ref[1]
-    for half, ref in ((core, mine_ref), (1 - core, other_ref)):
-        for k in range(4):
-            at = pl.multiple_of(half * HALF + ((chip - k) & 3) * PIECE, PIECE)
-            q_ref[pl.ds(at, PIECE), :] = solve(ref[k * PIECE : (k + 1) * PIECE, :]).astype(BF16)
+    inv_ref[:K, :] = high
+    inv_ref[K:, :] = low
     i = iota((2 * PARTS, PARTS * EXTRA), 0)
     e = iota((2 * PARTS, PARTS * EXTRA), 1)
     want = jnp.where(i < PARTS, i * EXTRA + 12, (i - PARTS) * EXTRA + 13)
     leads = dot(jnp.where(e == want, 1.0, 0.0).astype(BF16), extra, 1, 0)
-    lead = solve(leads[:PARTS].astype(BF16))
-    lead_high = lead.astype(BF16)
-    lead_low = (lead - lead_high.astype(F32)).astype(BF16)
-    coef = leads[PARTS:].astype(BF16)
-    for i in range(PARTS):
-        c = coef[i : i + 1, :ROWS]
-        term = dot(c, lead_high[i : i + 1], 0, 0) + dot(c, lead_low[i : i + 1], 0, 0)
-        z_ref[i * ROWS : (i + 1) * ROWS, :] = solve(in_ref[i, :ROWS, :]) + term
+    lead = leads[:PARTS].astype(BF16)
+    lead_ref[...] = dot(lead, high, 1, 1) + dot(lead, low, 1, 1)
+    coef_ref[...] = leads[PARTS:, :TILE].T
+    core, chip = meta_ref[0], meta_ref[1]
+    for half, ref in ((core, mine_ref), (1 - core, other_ref)):
+        for k in range(4):
+            a = ref[k * PIECE : (k + 1) * PIECE, :]
+            at = pl.multiple_of(half * HALF + ((chip - k) & 3) * PIECE, PIECE)
+            q_ref[pl.ds(at, PIECE), :] = (dot(a, high, 1, 1) + dot(a, low, 1, 1)).astype(BF16)
+
+
+def back_solve_kernel(meta_ref, b0_ref, b1_ref, b2_ref, b3_ref, inv_ref, lead_ref, coef_ref, z_hbm, z_ref, sem):
+    copies = []
+    for k, ref in enumerate((b0_ref, b1_ref, b2_ref, b3_ref)):
+        a = ref[...].reshape(8 * ROWS, K)
+        z = dot(a, inv_ref[:K, :], 1, 1) + dot(a, inv_ref[K:, :], 1, 1)
+        for i in range(8):
+            s = 8 * k + i
+            term = coef_ref[:ROWS, s : s + 1] * lead_ref[s : s + 1, :]
+            z_ref[k, i * ROWS : (i + 1) * ROWS, :] = z[i * ROWS : (i + 1) * ROWS] + term
+        at = pl.multiple_of(((meta_ref[2] - k) & 3) * 8 * ROWS, 8 * ROWS)
+        copy = pltpu.make_async_copy(z_ref.at[k], z_hbm.at[pl.ds(at, 8 * ROWS), :], sem.at[k])
+        copy.start()
+        copies.append(copy)
+    for copy in copies:
+        copy.wait()
 
 
 def shape(*dims, dtype=F32):
@@ -264,47 +284,56 @@
 
 
 def on_device(tiles, block_rows, block_cols, tile_counts, omega):
-    where = jnp.stack([lax.axis_index("c"), lax.axis_index("y")]).astype(jnp.int32)
+    places = [lax.axis_index(axis).astype(jnp.int32).reshape(1) for axis in ("c", "y", "x")]
+    meta = jnp.concatenate(places + [tile_counts[0], block_rows[0, 0], block_cols[0, 0]])
     swap = [(0, 1), (1, 0)]
     keep, send = pl.pallas_call(
         sketch_kernel,
         out_shape=(shape(HALF, K), shape(HALF, K)),
-        in_specs=[SMEM] + [HBM] * 5,
+        in_specs=[SMEM] + [HBM] * 2,
         out_specs=(VMEM, VMEM),
         scratch_shapes=[
             pltpu.VMEM((RB, TILE, K), F32),
-            pltpu.SMEM((1, 1, SLOTS), jnp.int32),
-            pltpu.SMEM((1, 1, SLOTS), jnp.int32),
-            pltpu.SMEM((1, 1), jnp.int32),
             pltpu.VMEM((SLOTS, TILE, TILE), BF16),
             pltpu.VMEM((CB, TILE, K), BF16),
-            pltpu.SemaphoreType.DMA((4,)),
+            pltpu.SemaphoreType.DMA,
             pltpu.SemaphoreType.DMA((SLOTS // LOAD,)),
         ],
-        compiler_params=LIMIT,
+        compiler_params=pltpu.CompilerParams(vmem_limit_bytes=51 * 1024 * 1024),
         name="sketch",
-    )(where, block_rows, block_cols, tile_counts, tiles, omega.reshape(CB, TILE, K))
-
-    def turn(a, k):
-        return lax.ppermute(a, "y", [(i, (i + k) % 4) for i in range(4)])
+    )(meta, tiles, omega.reshape(CB, TILE, K))
+
+    def turn(a, k, axis="y"):
+        return lax.ppermute(a, axis, [(i, (i + k) % 4) for i in range(4)])
 
     half = keep + lax.ppermute(send, "c", swap)
     quarters = half.reshape(4, PIECE, K)
+    sent = [quarters[k].astype(BF16) for k in range(4)]
+    sent[2], later = lax.optimization_barrier((sent[2], meta))
+    flipped = pl.pallas_call(
+        flip_kernel,
+        out_shape=shape(SLOTS, TILE, TILE, dtype=BF16),
+        in_specs=[SMEM, VMEM],
+        out_specs=VMEM,
+        compiler_params=LIMIT,
+        cost_estimate=pl.CostEstimate(flops=4 * 10**9, bytes_accessed=4 * 2**20, transcendentals=0),
+        name="flip",
+    )(later, tiles[0, 0])
     shard = quarters[0]
     for k in (2, 1, 3):
-        shard = shard + turn(quarters[k].astype(BF16), k).astype(F32)
-    shard = shard.astype(BF16)
+        shard = shard + turn(sent[k], k).astype(F32)
+    shard, flipped = lax.optimization_barrier((shard.astype(BF16), flipped))
     mine = jnp.concatenate([shard] + [turn(shard, k) for k in (1, 2, 3)], axis=0)
     other = lax.ppermute(mine, "c", swap)
     payload = pl.pallas_call(
         back_kernel,
         out_shape=shape(PARTS, ROWS + EXTRA, K, dtype=BF16),
-        in_specs=[SMEM] * 4 + [VMEM] * 3,
+        in_specs=[SMEM] + [VMEM] * 3,
         out_specs=VMEM,
         scratch_shapes=[pltpu.VMEM((RB, TILE, K), BF16), pltpu.VMEM((CB, TILE, K), F32)],
         compiler_params=LIMIT,
         name="back",
-    )(where, block_rows[0, 0], block_cols[0, 0], tile_counts[0], tiles[0, 0], mine, other)
+    )(meta, flipped, mine, other)
     size = (ROWS + EXTRA, K)
     parts = lax.all_to_all(payload.reshape(4, 8, *size), "x", 0, 0, tiled=True)
     parts = pl.pallas_call(
@@ -324,16 +353,37 @@
         name="total",
     )(lax.all_to_all(parts, "z", 0, 0, tiled=True))
     line = lax.all_to_all(spread, "z", 0, 0, tiled=True)
-    whole = lax.all_to_all(jnp.broadcast_to(line[None], (4, 8, *size)), "x", 0, 0, tiled=True)
-    return pl.pallas_call(
-        final_kernel,
-        out_shape=(shape(2 * HALF, K, dtype=BF16), shape(K, K), shape(CB * TILE, K)),
-        in_specs=[SMEM] + [VMEM] * 3,
-        out_specs=(VMEM, VMEM, VMEM),
+    body, extra = line[:, :ROWS, :], line[:, ROWS:, :]
+    extras = [extra] + [turn(extra, k, "x") for k in (2, 1, 3)]
+    bodies = [body] + [turn(body, k, "x") for k in (2, 1, 3)]
+    extras = [extras[0], extras[2], extras[1], extras[3]]
+    bodies = [bodies[0], bodies[2], bodies[1], bodies[3]]
+    q, r, inv, lead, coef = pl.pallas_call(
+        factor_kernel,
+        out_shape=(
+            shape(2 * HALF, K, dtype=BF16),
+            shape(K, K),
+            shape(2 * K, K, dtype=BF16),
+            shape(PARTS, K),
+            shape(TILE, PARTS),
+        ),
+        in_specs=[SMEM] + [VMEM] * 6,
+        out_specs=(VMEM,) * 5,
         scratch_shapes=[pltpu.VMEM((K, 2 * K), F32)],
         compiler_params=LIMIT,
-        name="finish",
-    )(where, whole.reshape(PARTS, *size), mine, other)
+        cost_estimate=pl.CostEstimate(flops=12 * 10**9, bytes_accessed=4 * 2**20, transcendentals=0),
+        name="factor",
+    )(meta, *extras, mine, other)
+    z = pl.pallas_call(
+        back_solve_kernel,
+        out_shape=shape(CB * TILE, K),
+        in_specs=[SMEM] + [VMEM] * 7,
+        out_specs=HBM,
+        scratch_shapes=[pltpu.VMEM((4, 8 * ROWS, K), F32), pltpu.SemaphoreType.DMA((4,))],
+        compiler_params=LIMIT,
+        name="z",
+    )(meta, *bodies, inv, lead, coef)
+    return q, r, z
 
 
 def solution(mesh):

time: 136 us -> 124 us (0.912)
  the two profiles are of different devices: /device:TPU:1 before, /device:TPU:8 now
where the time goes in v3:
time: 124 us; the launch traced here: 123 us
  blocking collectives  59.9 us (48%)
  Pallas kernels  24.7 us (20%)
  waiting for transfers between devices  18 us (15%)
  starting transfers between devices  17.9 us (14%)
  between operations  1.56 us (1%)
    all_to_all x1, blocking collectives, on_device(): lax.all_to_all(parts, 'z', 0, 0, tiled=True)  23 us
    all_to_all x1, blocking collectives, on_device(): parts = lax.all_to_all(payload.reshape(4, 8, *size), 'x', 0, 0, tiled=True)  22 us
    ppermute x12, starting transfers between devices, turn(): return lax.ppermute(a, axis, [(i, (i + k) % 4) for i in range(4)])  17.3 us
    all_to_all x1, blocking collectives, on_device(): line = lax.all_to_all(spread, 'z', 0, 0, tiled=True)  14.9 us
    pallas_call x1, Pallas kernels, on_device(): pl.pallas_call(factor_kernel, out_shape=(shape(2 * HALF, K, dtype=BF16),...  14.2 us
    ppermute x12, waiting for transfers between devices, turn(): return lax.ppermute(a, axis, [(i, (i + k) % 4) for i in range(4)])  13.9 us
    pallas_call x1, Pallas kernels, on_device(): pl.pallas_call(sketch_kernel, out_shape=(shape(HALF, K), shape(HALF, K)),...  3.18 us
  transfers between devices with their start and end apart: 14, of which 7 were waited for; matrix products, arithmetic and copies ran while one was open for 0% of the time, Pallas kernels for 13%

profile of v3, /device:TPU:8, one launch (start us, length us, event | category | flops | bytes accessed | tf_op | source)
XLA Modules:
  0.0 123.2 jit_solution(140441447467790287)
XLA Ops:
  1.3 0.8 concatenate.6.meta_ref
  2.0 3.2 %sketch.1 = (f32[1024,256]{1,0:T(8,128)S(1)}, f32[1024,256]{1,0:T(8,128)S(1)}) custom-call(s32[132]{0:T(256)S(1)} %concatenate.6.meta_ref, bf16[1,1,64,128,128]{4,3,2,1,0:T(8,128)(2,1)} %tiles_hbm.1, bf16[16,128,256]{2,1,0:T(8,128)(2,1)} %bitcast.12), custom_call_target="tpu_custom_call" | custom-call | tf_op jit(solution)/shard_map/sketch/pallas_call | solution.py:290
  5.2 0.5 collective-permute-start
  5.7 2.3 %collective-permute-done = f32[1024,256]{1,0:T(8,128)S(1)} collective-permute-done((f32[1024,256]{1,0:T(8,128)S(1)}, f32[1024,256]{1,0:T(8,128)S(1)}, u32[]{:S(2)}, u32[]{:S(2)}) %collective-permute-start) | collective-permute-done | bytes 1048608 | tf_op jit(solution)/shard_map/ppermute | solution.py:309
  8.0 0.0 copy-start
  8.0 0.2 fusion.3
  8.2 2.9 %collective-permute-start.1 = (bf16[256,256]{1,0:T(8,128)(2,1)S(1)}, bf16[256,256]{1,0:T(8,128)(2,1)S(1)}, u32[]{:S(2)}, u32[]{:S(2)}) collective-permute-start(bf16[256,256]{1,0:T(8,128)(2,1)S(1)} %get-tuple-element.16), channel_id=1, source_target_pairs={{0,4},{2,6},{4,0},{6,2},{1,5},{3,7},{5,1},{7,3},{8,12},{10,14},{12... | collective-permute-start | bytes 393224 | tf_op jit(solution)/shard_map/ppermute | solution.py:307
  11.1 2.5 %collective-permute-start.3 = (bf16[256,256]{1,0:T(8,128)(2,1)S(1)}, bf16[256,256]{1,0:T(8,128)(2,1)S(1)}, u32[]{:S(2)}, u32[]{:S(2)}) collective-permute-start(bf16[256,256]{1,0:T(8,128)(2,1)S(1)} %get-tuple-element.28), channel_id=1, source_target_pairs={{0,6},{2,0},{4,2},{6,4},{1,7},{3,1},{5,3},{7,5},{8,14},{10,8},{12,... | collective-permute-start | bytes 393224 | tf_op jit(solution)/shard_map/ppermute | solution.py:307
  13.7 0.0 collective-permute-start.2
  13.7 0.0 copy-done
  13.7 2.0 %flip.1.tiles_ref = bf16[64,128,128]{2,1,0:T(8,128)(2,1)S(1)} custom-call(s32[132]{0:T(256)S(1)} %concatenate.6.meta_ref, bf16[64,128,128]{2,1,0:T(8,128)(2,1)S(1)} %bitcast.11), custom_call_target="tpu_custom_call" | custom-call | flops 4000000000 | bytes 4194304 | tf_op jit(solution)/shard_map/flip/pallas_call | solution.py:313
  15.6 0.0 collective-permute-done.1
  15.7 2.7 %collective-permute-done.3 = bf16[256,256]{1,0:T(8,128)(2,1)S(1)} collective-permute-done((bf16[256,256]{1,0:T(8,128)(2,1)S(1)}, bf16[256,256]{1,0:T(8,128)(2,1)S(1)}, u32[]{:S(2)}, u32[]{:S(2)}) %collective-permute-start.3) | collective-permute-done | bytes 131104 | tf_op jit(solution)/shard_map/ppermute | solution.py:307
  18.4 1.6 %collective-permute-done.2 = bf16[256,256]{1,0:T(8,128)(2,1)S(1)} collective-permute-done((bf16[256,256]{1,0:T(8,128)(2,1)S(1)}, bf16[256,256]{1,0:T(8,128)(2,1)S(1)}, u32[]{:S(2)}, u32[]{:S(2)}) %collective-permute-start.2) | collective-permute-done | bytes 131104 | tf_op jit(solution)/shard_map/ppermute | solution.py:307
  20.0 0.1 fusion.2
  20.1 1.5 %collective-permute-start.4 = (bf16[256,256]{1,0:T(8,128)(2,1)S(1)}, bf16[256,256]{1,0:T(8,128)(2,1)S(1)}, u32[]{:S(2)}, u32[]{:S(2)}) collective-permute-start(bf16[256,256]{1,0:T(8,128)(2,1)S(1)} %fusion.2), channel_id=1, source_target_pairs={{0,2},{2,4},{4,6},{6,0},{1,3},{3,5},{5,7},{7,1},{8,10},{10,12},{12... | collective-permute-start | bytes 393224 | tf_op jit(solution)/shard_map/ppermute | solution.py:307
  21.6 0.7 collective-permute-start.6
  22.3 2.0 %collective-permute-start.5 = (bf16[256,256]{1,0:T(8,128)(2,1)S(1)}, bf16[256,256]{1,0:T(8,128)(2,1)S(1)}, u32[]{:S(2)}, u32[]{:S(2)}) collective-permute-start(bf16[256,256]{1,0:T(8,128)(2,1)S(1)} %fusion.2), channel_id=1, source_target_pairs={{0,4},{2,6},{4,0},{6,2},{1,5},{3,7},{5,1},{7,3},{8,12},{10,14},{12... | collective-permute-start | bytes 393224 | tf_op jit(solution)/shard_map/ppermute | solution.py:307
  24.3 1.7 %collective-permute-done.4 = bf16[256,256]{1,0:T(8,128)(2,1)S(1)} collective-permute-done((bf16[256,256]{1,0:T(8,128)(2,1)S(1)}, bf16[256,256]{1,0:T(8,128)(2,1)S(1)}, u32[]{:S(2)}, u32[]{:S(2)}) %collective-permute-start.4) | collective-permute-done | bytes 131104 | tf_op jit(solution)/shard_map/ppermute | solution.py:307
  25.9 4.5 %collective-permute-done.5 = bf16[256,256]{1,0:T(8,128)(2,1)S(1)} collective-permute-done((bf16[256,256]{1,0:T(8,128)(2,1)S(1)}, bf16[256,256]{1,0:T(8,128)(2,1)S(1)}, u32[]{:S(2)}, u32[]{:S(2)}) %collective-permute-start.5) | collective-permute-done | bytes 131104 | tf_op jit(solution)/shard_map/ppermute | solution.py:307
  30.5 0.0 collective-permute-done.6
  30.5 0.1 collective-permute-start.7
  30.6 1.9 %collective-permute-done.7.other_ref = bf16[1024,256]{1,0:T(8,128)(2,1)S(1)} collective-permute-done((bf16[1024,256]{1,0:T(8,128)(2,1)S(1)}, bf16[1024,256]{1,0:T(8,128)(2,1)S(1)}, u32[]{:S(2)}, u32[]{:S(2)}) %collective-permute-start.7) | collective-permute-done | bytes 524320 | tf_op jit(solution)/shard_map/ppermute | solution.py:327
  32.5 2.4 %back.1 = bf16[32,80,256]{2,1,0:T(8,128)(2,1)S(1)} custom-call(s32[132]{0:T(256)S(1)} %concatenate.6.meta_ref, bf16[64,128,128]{2,1,0:T(8,128)(2,1)S(1)} %flip.1.tiles_ref, bf16[1024,256]{1,0:T(8,128)(2,1)S(1)} %constant_dynamic-update-slice_fusion.mine_ref, bf16[1024,256]{1,0:T(8,128)(2,1)S(1)} %collective-permute-done.7.other_ref), custom_call_target="tpu_custom_call" | custom-call | tf_op jit(solution)/shard_map/back/pallas_call | solution.py:328
  34.9 22.0 %all_to_all.15.in_ref = bf16[4,8,80,256]{3,2,1,0:T(8,128)(2,1)S(1)} all-to-all(bf16[4,8,80,256]{3,2,1,0:T(8,128)(2,1)S(1)} %bitcast.10), channel_id=1, replica_groups=mesh['z'=8,'x'=4,'y'=4,'c'=2] {'x'}, dimensions={0} | all-to-all | bytes 2621440 | tf_op jit(solution)/shard_map/all_to_all | solution.py:338
  56.9 0.2 partial.1
  57.1 23.0 %all_to_all.16.in_ref = bf16[8,80,256]{2,1,0:T(8,128)(2,1)S(1)} all-to-all(bf16[8,80,256]{2,1,0:T(8,128)(2,1)S(1)} %partial.1), channel_id=1, replica_groups=mesh['z'=8,'x'=4,'y'=4,'c'=2] {'z'}, dimensions={0} | all-to-all | bytes 655360 | tf_op jit(solution)/shard_map/all_to_all | solution.py:354
  80.1 0.4 total.1
  80.6 14.9 %all_to_all.17 = bf16[8,80,256]{2,1,0:T(8,128)(2,1)S(1)} all-to-all(bf16[8,80,256]{2,1,0:T(8,128)(2,1)S(1)} %total.1), channel_id=1, replica_groups=mesh['z'=8,'x'=4,'y'=4,'c'=2] {'z'}, dimensions={0} | all-to-all | bytes 655360 | tf_op jit(solution)/shard_map/all_to_all | solution.py:355
  95.4 1.2 collective-permute-start.10
  96.6 1.5 %collective-permute-start.9 = (bf16[8,16,256]{2,1,0:T(8,128)(2,1)S(1)}, bf16[8,16,256]{2,1,0:T(8,128)(2,1)S(1)}, u32[]{:S(2)}, u32[]{:S(2)}) collective-permute-start(bf16[8,16,256]{2,1,0:T(8,128)(2,1)S(1)} %slice.35.e0_ref), channel_id=1, source_target_pairs={{0,16},{8,24},{16,0},{24,8},{1,17},{9,25},{17,1},{25,9},{2,18},{10... | collective-permute-start | bytes 196616 | tf_op jit(solution)/shard_map/ppermute | solution.py:307
  98.1 0.0 collective-permute-start.8
  98.1 3.3 %collective-permute-start.13 = (bf16[8,64,256]{2,1,0:T(8,128)(2,1)S(1)}, bf16[8,64,256]{2,1,0:T(8,128)(2,1)S(1)}, u32[]{:S(2)}, u32[]{:S(2)}) collective-permute-start(bf16[8,64,256]{2,1,0:T(8,128)(2,1)S(1)} %slice.36.b0_ref), channel_id=1, source_target_pairs={{0,24},{8,0},{16,8},{24,16},{1,25},{9,1},{17,9},{25,17},{2,26},{10... | collective-permute-start | bytes 786440 | tf_op jit(solution)/shard_map/ppermute | solution.py:307
  101.4 0.8 collective-permute-start.12
  102.3 0.0 collective-permute-done.10.e3_ref
  102.3 0.9 collective-permute-start.11
  103.1 0.0 collective-permute-done.9.e2_ref
  103.2 3.3 %collective-permute-done.8.e1_ref = bf16[8,16,256]{2,1,0:T(8,128)(2,1)S(1)} collective-permute-done((bf16[8,16,256]{2,1,0:T(8,128)(2,1)S(1)}, bf16[8,16,256]{2,1,0:T(8,128)(2,1)S(1)}, u32[]{:S(2)}, u32[]{:S(2)}) %collective-permute-start.8) | collective-permute-done | bytes 65568 | tf_op jit(solution)/shard_map/ppermute | solution.py:307
  106.4 14.2 %factor.1 = (bf16[2048,256]{1,0:T(8,128)(2,1)}, f32[256,256]{1,0:T(8,128)}, bf16[512,256]{1,0:T(8,128)(2,1)S(1)}, f32[32,256]{1,0:T(8,128)S(1)}, f32[128,32]{1,0:T(8,128)S(1)}) custom-call(s32[132]{0:T(256)S(1)} %concatenate.6.meta_ref, bf16[8,16,256]{2,1,0:T(8,128)(2,1)S(1)} %slice.35.e0_ref, bf16[8,16,256]{2,1,0:T(8,128)(2,1)S(1)} %collective-permute-done.8.e1_ref, ...), custom_call_target="tpu_custom_call" | custom-call | flops 12000000000 | bytes 4194304 | tf_op jit(solution)/shard_map/factor/pallas_call | solution.py:361
  120.6 0.0 collective-permute-done.13.b3_ref
  120.6 0.0 collective-permute-done.12.b2_ref
  120.6 0.0 collective-permute-done.11.b1_ref
  120.6 2.4 %z.1 = f32[2048,256]{1,0:T(8,128)} custom-call(s32[132]{0:T(256)S(1)} %concatenate.6.meta_ref, bf16[8,64,256]{2,1,0:T(8,128)(2,1)S(1)} %slice.36.b0_ref, bf16[8,64,256]{2,1,0:T(8,128)(2,1)S(1)} %collective-permute-done.11.b1_ref, bf16[8,64,256]{2,1,0:T(8,128)(2,1)S(1)} %collective-permute-done.12.b2_ref, ...), custom_call_target="tpu_custom_call" | custom-call | tf_op jit(solution)/shard_map/z/pallas_call | solution.py:377
  (7 shorter events, 0.1 us)
Async XLA Ops:
  5.2 2.8 %collective-permute-start = (f32[1024,256]{1,0:T(8,128)S(1)}, f32[1024,256]{1,0:T(8,128)S(1)}, u32[]{:S(2)}, u32[]{:S(2)}) collective-permute-start(f32[1024,256]{1,0:T(8,128)S(1)} %get-tuple-element.15), channel_id=1, source_target_pairs={{0,1},{1,0},{2,3},{3,2},{4,5},{5,4},{6,7},{7,6},{8,9},{9,8},{10,11... | collective-permute-start | bytes 3145736 | tf_op jit(solution)/shard_map/ppermute | solution.py:309
  8.0 5.7 %copy-start = (bf16[1,1,64,128,128]{4,3,2,1,0:T(8,128)(2,1)S(1)}, bf16[1,1,64,128,128]{4,3,2,1,0:T(8,128)(2,1)}, u32[]{:S(2)}) copy-start(bf16[1,1,64,128,128]{4,3,2,1,0:T(8,128)(2,1)} %tiles_hbm.1) | copy-start | bytes 6291460
  8.2 7.5 %collective-permute-start.1 = (bf16[256,256]{1,0:T(8,128)(2,1)S(1)}, bf16[256,256]{1,0:T(8,128)(2,1)S(1)}, u32[]{:S(2)}, u32[]{:S(2)}) collective-permute-start(bf16[256,256]{1,0:T(8,128)(2,1)S(1)} %get-tuple-element.16), channel_id=1, source_target_pairs={{0,4},{2,6},{4,0},{6,2},{1,5},{3,7},{5,1},{7,3},{8,12},{10,14},{12... | collective-permute-start | bytes 393224 | tf_op jit(solution)/shard_map/ppermute | solution.py:307
  11.1 7.3 %collective-permute-start.3 = (bf16[256,256]{1,0:T(8,128)(2,1)S(1)}, bf16[256,256]{1,0:T(8,128)(2,1)S(1)}, u32[]{:S(2)}, u32[]{:S(2)}) collective-permute-start(bf16[256,256]{1,0:T(8,128)(2,1)S(1)} %get-tuple-element.28), channel_id=1, source_target_pairs={{0,6},{2,0},{4,2},{6,4},{1,7},{3,1},{5,3},{7,5},{8,14},{10,8},{12,... | collective-permute-start | bytes 393224 | tf_op jit(solution)/shard_map/ppermute | solution.py:307
  13.7 6.3 %collective-permute-start.2 = (bf16[256,256]{1,0:T(8,128)(2,1)S(1)}, bf16[256,256]{1,0:T(8,128)(2,1)S(1)}, u32[]{:S(2)}, u32[]{:S(2)}) collective-permute-start(bf16[256,256]{1,0:T(8,128)(2,1)S(1)} %get-tuple-element.29), channel_id=1, source_target_pairs={{0,2},{2,4},{4,6},{6,0},{1,3},{3,5},{5,7},{7,1},{8,10},{10,12},{12... | collective-permute-start | bytes 393224 | tf_op jit(solution)/shard_map/ppermute | solution.py:307
  20.1 5.9 %collective-permute-start.4 = (bf16[256,256]{1,0:T(8,128)(2,1)S(1)}, bf16[256,256]{1,0:T(8,128)(2,1)S(1)}, u32[]{:S(2)}, u32[]{:S(2)}) collective-permute-start(bf16[256,256]{1,0:T(8,128)(2,1)S(1)} %fusion.2), channel_id=1, source_target_pairs={{0,2},{2,4},{4,6},{6,0},{1,3},{3,5},{5,7},{7,1},{8,10},{10,12},{12... | collective-permute-start | bytes 393224 | tf_op jit(solution)/shard_map/ppermute | solution.py:307
  21.6 8.9 %collective-permute-start.6 = (bf16[256,256]{1,0:T(8,128)(2,1)S(1)}, bf16[256,256]{1,0:T(8,128)(2,1)S(1)}, u32[]{:S(2)}, u32[]{:S(2)}) collective-permute-start(bf16[256,256]{1,0:T(8,128)(2,1)S(1)} %fusion.2), channel_id=1, source_target_pairs={{0,6},{2,0},{4,2},{6,4},{1,7},{3,1},{5,3},{7,5},{8,14},{10,8},{12,... | collective-permute-start | bytes 393224 | tf_op jit(solution)/shard_map/ppermute | solution.py:307
  22.3 8.2 %collective-permute-start.5 = (bf16[256,256]{1,0:T(8,128)(2,1)S(1)}, bf16[256,256]{1,0:T(8,128)(2,1)S(1)}, u32[]{:S(2)}, u32[]{:S(2)}) collective-permute-start(bf16[256,256]{1,0:T(8,128)(2,1)S(1)} %fusion.2), channel_id=1, source_target_pairs={{0,4},{2,6},{4,0},{6,2},{1,5},{3,7},{5,1},{7,3},{8,12},{10,14},{12... | collective-permute-start | bytes 393224 | tf_op jit(solution)/shard_map/ppermute | solution.py:307
  30.5 2.0 %collective-permute-start.7 = (bf16[1024,256]{1,0:T(8,128)(2,1)S(1)}, bf16[1024,256]{1,0:T(8,128)(2,1)S(1)}, u32[]{:S(2)}, u32[]{:S(2)}) collective-permute-start(bf16[1024,256]{1,0:T(8,128)(2,1)S(1)} %constant_dynamic-update-slice_fusion.mine_ref), channel_id=1, source_target_pairs={{0,1},{1,0},{2,3},{3,2},{4,5},{5,4},{6,7},{7,6},{8,9},{9,8},{10,11... | collective-permute-start | bytes 1572872 | tf_op jit(solution)/shard_map/ppermute | solution.py:327
  95.4 6.8 %collective-permute-start.10 = (bf16[8,16,256]{2,1,0:T(8,128)(2,1)S(1)}, bf16[8,16,256]{2,1,0:T(8,128)(2,1)S(1)}, u32[]{:S(2)}, u32[]{:S(2)}) collective-permute-start(bf16[8,16,256]{2,1,0:T(8,128)(2,1)S(1)} %slice.35.e0_ref), channel_id=1, source_target_pairs={{0,24},{8,0},{16,8},{24,16},{1,25},{9,1},{17,9},{25,17},{2,26},{10... | collective-permute-start | bytes 196616 | tf_op jit(solution)/shard_map/ppermute | solution.py:307
  96.6 6.6 %collective-permute-start.9 = (bf16[8,16,256]{2,1,0:T(8,128)(2,1)S(1)}, bf16[8,16,256]{2,1,0:T(8,128)(2,1)S(1)}, u32[]{:S(2)}, u32[]{:S(2)}) collective-permute-start(bf16[8,16,256]{2,1,0:T(8,128)(2,1)S(1)} %slice.35.e0_ref), channel_id=1, source_target_pairs={{0,16},{8,24},{16,0},{24,8},{1,17},{9,25},{17,1},{25,9},{2,18},{10... | collective-permute-start | bytes 196616 | tf_op jit(solution)/shard_map/ppermute | solution.py:307
  98.1 8.3 %collective-permute-start.8 = (bf16[8,16,256]{2,1,0:T(8,128)(2,1)S(1)}, bf16[8,16,256]{2,1,0:T(8,128)(2,1)S(1)}, u32[]{:S(2)}, u32[]{:S(2)}) collective-permute-start(bf16[8,16,256]{2,1,0:T(8,128)(2,1)S(1)} %slice.35.e0_ref), channel_id=1, source_target_pairs={{0,8},{8,16},{16,24},{24,0},{1,9},{9,17},{17,25},{25,1},{2,10},{10... | collective-permute-start | bytes 196616 | tf_op jit(solution)/shard_map/ppermute | solution.py:307
  98.1 22.5 %collective-permute-start.13 = (bf16[8,64,256]{2,1,0:T(8,128)(2,1)S(1)}, bf16[8,64,256]{2,1,0:T(8,128)(2,1)S(1)}, u32[]{:S(2)}, u32[]{:S(2)}) collective-permute-start(bf16[8,64,256]{2,1,0:T(8,128)(2,1)S(1)} %slice.36.b0_ref), channel_id=1, source_target_pairs={{0,24},{8,0},{16,8},{24,16},{1,25},{9,1},{17,9},{25,17},{2,26},{10... | collective-permute-start | bytes 786440 | tf_op jit(solution)/shard_map/ppermute | solution.py:307
  101.4 19.2 %collective-permute-start.12 = (bf16[8,64,256]{2,1,0:T(8,128)(2,1)S(1)}, bf16[8,64,256]{2,1,0:T(8,128)(2,1)S(1)}, u32[]{:S(2)}, u32[]{:S(2)}) collective-permute-start(bf16[8,64,256]{2,1,0:T(8,128)(2,1)S(1)} %slice.36.b0_ref), channel_id=1, source_target_pairs={{0,16},{8,24},{16,0},{24,8},{1,17},{9,25},{17,1},{25,9},{2,18},{10... | collective-permute-start | bytes 786440 | tf_op jit(solution)/shard_map/ppermute | solution.py:307
  102.3 18.3 %collective-permute-start.11 = (bf16[8,64,256]{2,1,0:T(8,128)(2,1)S(1)}, bf16[8,64,256]{2,1,0:T(8,128)(2,1)S(1)}, u32[]{:S(2)}, u32[]{:S(2)}) collective-permute-start(bf16[8,64,256]{2,1,0:T(8,128)(2,1)S(1)} %slice.36.b0_ref), channel_id=1, source_target_pairs={{0,8},{8,16},{16,24},{24,0},{1,9},{9,17},{17,25},{25,1},{2,10},{10... | collective-permute-start | bytes 786440 | tf_op jit(solution)/shard_map/ppermute | solution.py:307

commit v4 on v3

--- a/solution.py
+++ b/solution.py
@@ -1,3 +1,5 @@
+import functools
+
 import jax
 import jax.numpy as jnp
 from jax import lax
@@ -23,6 +25,7 @@
 LIVE = 3
 AT = 4
 COLS = AT + SLOTS
+START = COLS + SLOTS
 PIECE = HALF // 4
 VMEM = pl.BlockSpec(memory_space=pltpu.VMEM)
 SMEM = pl.BlockSpec(memory_space=pltpu.SMEM)
@@ -74,54 +77,95 @@
     send_ref[...] = acc[RB // 2 :].reshape(HALF, K)
 
 
-def place_matrix(rows, cols, shift, dtype=BF16):
-    e = iota((rows, cols), 0)
-    p = iota((rows, cols), 1)
-    return jnp.where((p // 6) * EXTRA + p % 6 + shift == e, 1.0, 0.0).astype(dtype)
-
-
-def flip_kernel(meta_ref, tiles_ref, out_ref):
+def flip_kernel(meta_ref, tiles_ref, out_ref, sorted_ref, count, source):
     live = meta_ref[LIVE]
+    for i in range(8):
+        count[i] = 0
+    for i in range(3):
+        sorted_ref[i] = meta_ref[i]
+
+    def turned(t):
+        return (meta_ref[COLS + t] - 4 * meta_ref[2]) & (CB - 1)
+
+    def chunk(t):
+        return jnp.where(t < live, turned(t) // 4, 4)
+
+    @pl.loop(0, SLOTS)
+    def _(t):
+        c = chunk(t)
+        count[c] = count[c] + 1
+
+    begin = jnp.int32(0)
+    for i in range(5):
+        here = count[i]
+        sorted_ref[START + i] = begin
+        count[i] = begin
+        begin = begin + here
+
+    @pl.loop(0, SLOTS)
+    def _(t):
+        c = chunk(t)
+        at = count[c]
+        count[c] = at + 1
+        source[at] = t
+        sorted_ref[AT + at] = meta_ref[AT + t] & (RB - 1)
+        sorted_ref[COLS + at] = turned(t)
 
     @pl.loop(0, SLOTS // GROUP)
     def _(g):
         for i in range(GROUP):
             t = g * GROUP + i
-            tile = tiles_ref[t].T
+            tile = tiles_ref[source[t]].T
             out_ref[t] = jnp.where(t < live, tile, jnp.zeros_like(tile))
 
 
-def back_kernel(meta_ref, tiles_ref, mine_ref, other_ref, out_ref, s_ref, acc):
-    core, chip = meta_ref[0], meta_ref[1]
+def gram_kernel(mine_ref, out_ref):
+    out_ref[...] = dot(mine_ref[...], mine_ref[...], 0, 0)
+
+
+def slab_kernel(meta_ref, mine_ref, other_ref, gram_ref, s_ref, g0_ref, g1_ref, g2_ref, g3_ref):
+    core, chip, x = meta_ref[0], meta_ref[1], meta_ref[2]
     for k in range(4):
         at = ((chip - k) & 3) * 2
         part = pl.ds(k * PIECE, PIECE)
         s_ref[pl.ds(core * 8 + at, 2)] = mine_ref[part, :].reshape(2, TILE, K)
         s_ref[pl.ds((1 - core) * 8 + at, 2)] = other_ref[part, :].reshape(2, TILE, K)
-    acc[...] = jnp.zeros_like(acc)
-
-    @pl.loop(0, (meta_ref[LIVE] + LOAD - 1) // LOAD)
-    def _(g):
-        prods, places = [], []
-        for i in range(LOAD):
-            t = g * LOAD + i
-            prods.append(dot(tiles_ref[t], s_ref[meta_ref[AT + t] & (RB - 1)], 1, 0))
-            places.append(meta_ref[COLS + t] & (CB - 1))
-        for prod, place in zip(prods, places):
-            acc[place] += prod
-
-    gram = dot(mine_ref[...], mine_ref[...], 0, 0) + dot(other_ref[...], other_ref[...], 0, 0)
-    gram = gram * (1.0 / NROW)
+    gram = (gram_ref[...] + dot(other_ref[...], other_ref[...], 0, 0)) * (1.0 / NROW)
     low = gram[K // 2 :, K // 2 :]
     low = jnp.concatenate([low[: K // 4], low[K // 4 :]], axis=1)
     packed = jnp.concatenate([gram[: K // 2], low], axis=0)
     high = packed.astype(BF16)
     rest = (packed - high.astype(F32)).astype(BF16)
-    extra = dot(place_matrix(PARTS * EXTRA, 192, 0), high, 1, 0) + dot(
-        place_matrix(PARTS * EXTRA, 192, 6), rest, 1, 0
+    e = iota((PARTS * EXTRA, 192), 0)
+    p = iota((PARTS * EXTRA, 192), 1)
+    slot = p // 6
+    first = (((slot // 8 - x) & 3) * 8 + slot % 8) * EXTRA + p % 6
+    extra = dot(jnp.where(e == first, 1.0, 0.0).astype(BF16), high, 1, 0) + dot(
+        jnp.where(e == first + 6, 1.0, 0.0).astype(BF16), rest, 1, 0
     )
-    out_ref[:, :ROWS, :] = acc[...].reshape(PARTS, ROWS, K).astype(BF16)
-    out_ref[:, ROWS:, :] = extra.reshape(PARTS, EXTRA, K).astype(BF16)
+    for k, ref in enumerate((g0_ref, g1_ref, g2_ref, g3_ref)):
+        ref[...] = extra[k * 8 * EXTRA : (k + 1) * 8 * EXTRA].reshape(8, EXTRA, K).astype(BF16)
+
+
+def back_kernel(first, last, meta_ref, tiles_ref, s_ref, *refs):
+    *out_refs, acc = refs
+    begin, end = meta_ref[START + first], meta_ref[START + last + 1]
+    acc[...] = jnp.zeros_like(acc)
+
+    @pl.loop(0, (end - begin + LOAD - 1) // LOAD)
+    def _(g):
+        prods, places = [], []
+        for i in range(LOAD):
+            t = begin + g * LOAD + i
+            safe = jnp.minimum(t, SLOTS - 1)
+            prod = dot(tiles_ref[safe], s_ref[meta_ref[AT + safe]], 1, 0)
+            prods.append(jnp.where(t < end, prod, 0.0))
+            places.append(jnp.where(t < end, meta_ref[COLS + safe] - 4 * first, 0))
+        for prod, place in zip(prods, places):
+            acc[place] += prod
+
+    for k, ref in enumerate(out_refs):
+        ref[...] = acc[4 * k : 4 * k + 4].reshape(8, ROWS, K).astype(BF16)
 
 
 def resplit(extra):
@@ -132,20 +176,31 @@
     return jnp.where(row < 6, high, jnp.where(row < 12, low, 0.0))
 
 
-def partial_kernel(in_ref, out_ref):
-    total = in_ref[0].astype(F32)
-    for i in range(1, 4):
-        total = total + in_ref[i].astype(F32)
-    out_ref[:, :ROWS, :] = total[:, :ROWS, :].astype(BF16)
-    extra = resplit(total[:, ROWS:, :].reshape(8 * EXTRA, K))
-    out_ref[:, ROWS:, :] = extra.reshape(8, EXTRA, K).astype(BF16)
-
-
-def sum_kernel(in_ref, out_ref):
-    total = in_ref[0].astype(F32)
+def gram_sum_kernel(a_ref, b_ref, c_ref, d_ref, out_ref):
+    total = jnp.zeros((8 * EXTRA, K), F32)
+    for ref in (a_ref, b_ref, c_ref, d_ref):
+        total = total + ref[...].reshape(8 * EXTRA, K).astype(F32)
+    out_ref[...] = resplit(total).reshape(8, EXTRA, K).astype(BF16)
+
+
+def partial_kernel(a_ref, b_ref, c_ref, d_ref, gram_ref, out_ref):
+    total = a_ref[...].astype(F32)
+    for ref in (b_ref, c_ref, d_ref):
+        total = total + ref[...].astype(F32)
+    out_ref[:, :ROWS, :] = total.astype(BF16)
+    gram = gram_ref[0].astype(F32)
     for i in range(1, 8):
-        total = total + in_ref[i].astype(F32)
-    w = total[:ROWS]
+        gram = gram + gram_ref[i].astype(F32)
+    gram = resplit(gram).astype(BF16)
+    for i in range(8):
+        out_ref[i, ROWS:, :] = gram
+
+
+def sum_kernel(in_ref, out_ref, gram_ref):
+    w = in_ref[0, :ROWS, :].astype(F32)
+    for i in range(1, 8):
+        w = w + in_ref[i, :ROWS, :].astype(F32)
+    gram_ref[...] = in_ref[:, ROWS:, :]
     mean = jnp.sum(w, axis=0, keepdims=True) * (1.0 / ROWS)
     top = jnp.max(jnp.abs(mean), axis=1, keepdims=True)
     lead = (mean / jnp.maximum(top, 1e-30)).astype(BF16)
@@ -155,9 +210,8 @@
     rest = w - dot(coef, lead, 0, 0)
     row = iota((EXTRA, K), 0)
     wide = jnp.concatenate([coef.astype(F32), jnp.zeros((1, K - ROWS), F32)], axis=1)
-    tail = jnp.where(row == 12, leadf, jnp.where(row == 13, wide, resplit(total[ROWS:])))
+    tail = jnp.where(row == 0, leadf, jnp.where(row == 1, wide, 0.0)).astype(BF16)
     body = rest.astype(BF16)
-    tail = tail.astype(BF16)
     for i in range(8):
         out_ref[i, :ROWS, :] = body
         out_ref[i, ROWS:, :] = tail
@@ -223,8 +277,7 @@
             work[at + NB :, :] -= dot(ut[at + NB :], u, 1, 0, lax.Precision.HIGHEST)
 
 
-def factor_kernel(meta_ref, e0_ref, e1_ref, e2_ref, e3_ref, mine_ref, other_ref,
-                  q_ref, r_ref, inv_ref, lead_ref, coef_ref, work):
+def factor_kernel(meta_ref, e0_ref, e1_ref, e2_ref, e3_ref, s_ref, q_ref, r_ref, inv_ref, work):
     extra = jnp.concatenate([e[...].reshape(8 * EXTRA, K) for e in (e0_ref, e1_ref, e2_ref, e3_ref)], axis=0)
     p = iota((192, PARTS * EXTRA), 0)
     e = iota((192, PARTS * EXTRA), 1)
@@ -244,30 +297,27 @@
     low = (inv - high.astype(F32)).astype(BF16)
     inv_ref[:K, :] = high
     inv_ref[K:, :] = low
-    i = iota((2 * PARTS, PARTS * EXTRA), 0)
-    e = iota((2 * PARTS, PARTS * EXTRA), 1)
-    want = jnp.where(i < PARTS, i * EXTRA + 12, (i - PARTS) * EXTRA + 13)
-    leads = dot(jnp.where(e == want, 1.0, 0.0).astype(BF16), extra, 1, 0)
-    lead = leads[:PARTS].astype(BF16)
-    lead_ref[...] = dot(lead, high, 1, 1) + dot(lead, low, 1, 1)
-    coef_ref[...] = leads[PARTS:, :TILE].T
-    core, chip = meta_ref[0], meta_ref[1]
-    for half, ref in ((core, mine_ref), (1 - core, other_ref)):
-        for k in range(4):
-            a = ref[k * PIECE : (k + 1) * PIECE, :]
-            at = pl.multiple_of(half * HALF + ((chip - k) & 3) * PIECE, PIECE)
-            q_ref[pl.ds(at, PIECE), :] = (dot(a, high, 1, 1) + dot(a, low, 1, 1)).astype(BF16)
-
-
-def back_solve_kernel(meta_ref, b0_ref, b1_ref, b2_ref, b3_ref, inv_ref, lead_ref, coef_ref, z_hbm, z_ref, sem):
+    for k in range(4):
+        a = s_ref[4 * k : 4 * k + 4].reshape(4 * TILE, K)
+        q_ref[k * 4 * TILE : (k + 1) * 4 * TILE, :] = (dot(a, high, 1, 1) + dot(a, low, 1, 1)).astype(BF16)
+
+
+def back_solve_kernel(meta_ref, b0_ref, b1_ref, b2_ref, b3_ref, inv_ref, z_hbm, z_ref, sem):
+    i = iota((EXTRA, 8 * EXTRA), 0)
+    e = iota((EXTRA, 8 * EXTRA), 1)
+    pick = jnp.where(e == (i % 8) * EXTRA + i // 8, 1.0, 0.0).astype(BF16)
     copies = []
     for k, ref in enumerate((b0_ref, b1_ref, b2_ref, b3_ref)):
-        a = ref[...].reshape(8 * ROWS, K)
+        leads = dot(pick, ref[:, ROWS:, :].reshape(8 * EXTRA, K), 1, 0)
+        lead = leads[:8].astype(BF16)
+        lead = dot(lead, inv_ref[:K, :], 1, 1) + dot(lead, inv_ref[K:, :], 1, 1)
+        coef = leads[8:, :TILE].T
+        a = ref[:, :ROWS, :].reshape(8 * ROWS, K)
         z = dot(a, inv_ref[:K, :], 1, 1) + dot(a, inv_ref[K:, :], 1, 1)
-        for i in range(8):
-            s = 8 * k + i
-            term = coef_ref[:ROWS, s : s + 1] * lead_ref[s : s + 1, :]
-            z_ref[k, i * ROWS : (i + 1) * ROWS, :] = z[i * ROWS : (i + 1) * ROWS] + term
+        for s in range(8):
+            z_ref[k, s * ROWS : (s + 1) * ROWS, :] = (
+                z[s * ROWS : (s + 1) * ROWS] + coef[:ROWS, s : s + 1] * lead[s : s + 1, :]
+            )
         at = pl.multiple_of(((meta_ref[2] - k) & 3) * 8 * ROWS, 8 * ROWS)
         copy = pltpu.make_async_copy(z_ref.at[k], z_hbm.at[pl.ds(at, 8 * ROWS), :], sem.at[k])
         copy.start()
@@ -278,6 +328,10 @@
 
 def shape(*dims, dtype=F32):
     return jax.ShapeDtypeStruct(dims, dtype)
+
+
+def cost(us):
+    return pl.CostEstimate(flops=us * 10**9, bytes_accessed=2**20, transcendentals=0)
 
 
 LIMIT = pltpu.CompilerParams(vmem_limit_bytes=40 * 1024 * 1024)
@@ -310,13 +364,14 @@
     quarters = half.reshape(4, PIECE, K)
     sent = [quarters[k].astype(BF16) for k in range(4)]
     sent[2], later = lax.optimization_barrier((sent[2], meta))
-    flipped = pl.pallas_call(
+    flipped, order = pl.pallas_call(
         flip_kernel,
-        out_shape=shape(SLOTS, TILE, TILE, dtype=BF16),
+        out_shape=(shape(SLOTS, TILE, TILE, dtype=BF16), shape(START + 8, dtype=jnp.int32)),
         in_specs=[SMEM, VMEM],
-        out_specs=VMEM,
-        compiler_params=LIMIT,
-        cost_estimate=pl.CostEstimate(flops=4 * 10**9, bytes_accessed=4 * 2**20, transcendentals=0),
+        out_specs=(VMEM, SMEM),
+        scratch_shapes=[pltpu.SMEM((8,), jnp.int32), pltpu.SMEM((SLOTS,), jnp.int32)],
+        compiler_params=LIMIT,
+        cost_estimate=cost(4),
         name="flip",
     )(later, tiles[0, 0])
     shard = quarters[0]
@@ -325,64 +380,87 @@
     shard, flipped = lax.optimization_barrier((shard.astype(BF16), flipped))
     mine = jnp.concatenate([shard] + [turn(shard, k) for k in (1, 2, 3)], axis=0)
     other = lax.ppermute(mine, "c", swap)
-    payload = pl.pallas_call(
-        back_kernel,
-        out_shape=shape(PARTS, ROWS + EXTRA, K, dtype=BF16),
+    half_gram = pl.pallas_call(
+        gram_kernel,
+        out_shape=shape(K, K),
+        in_specs=[VMEM],
+        out_specs=VMEM,
+        compiler_params=LIMIT,
+        cost_estimate=cost(1),
+        name="gram",
+    )(mine)
+    slab, *grams = pl.pallas_call(
+        slab_kernel,
+        out_shape=(shape(RB, TILE, K, dtype=BF16),) + (shape(8, EXTRA, K, dtype=BF16),) * 4,
         in_specs=[SMEM] + [VMEM] * 3,
+        out_specs=(VMEM,) * 5,
+        compiler_params=LIMIT,
+        cost_estimate=cost(1),
+        name="slab",
+    )(meta, mine, other, half_gram)
+    grams = [grams[0]] + [turn(grams[k], k, "x") for k in (1, 2, 3)]
+    backs = []
+    for first, last in ((1, 3), (0, 0)):
+        count = last - first + 1
+        backs += pl.pallas_call(
+            functools.partial(back_kernel, first, last),
+            out_shape=(shape(8, ROWS, K, dtype=BF16),) * count,
+            in_specs=[SMEM] + [VMEM] * 2,
+            out_specs=(VMEM,) * count,
+            scratch_shapes=[pltpu.VMEM((4 * count, TILE, K), F32)],
+            compiler_params=LIMIT,
+            cost_estimate=cost(10 if first else 1),
+            name=f"back{first}",
+        )(order, flipped, slab)
+    backs = [backs[3]] + [turn(backs[k - 1], k, "x") for k in (1, 2, 3)]
+    grams = pl.pallas_call(
+        gram_sum_kernel,
+        out_shape=shape(8, EXTRA, K, dtype=BF16),
+        in_specs=[VMEM] * 4,
         out_specs=VMEM,
-        scratch_shapes=[pltpu.VMEM((RB, TILE, K), BF16), pltpu.VMEM((CB, TILE, K), F32)],
-        compiler_params=LIMIT,
-        name="back",
-    )(meta, flipped, mine, other)
+        compiler_params=LIMIT,
+        name="gram_sum",
+    )(*grams)
+    grams = lax.all_to_all(grams, "z", 0, 0, tiled=True)
     size = (ROWS + EXTRA, K)
-    parts = lax.all_to_all(payload.reshape(4, 8, *size), "x", 0, 0, tiled=True)
     parts = pl.pallas_call(
         partial_kernel,
         out_shape=shape(8, *size, dtype=BF16),
+        in_specs=[VMEM] * 5,
+        out_specs=VMEM,
+        compiler_params=LIMIT,
+        name="partial",
+    )(*backs, grams)
+    spread, gram = pl.pallas_call(
+        sum_kernel,
+        out_shape=(shape(8, *size, dtype=BF16), shape(8, EXTRA, K, dtype=BF16)),
         in_specs=[VMEM],
-        out_specs=VMEM,
-        compiler_params=LIMIT,
-        name="partial",
-    )(parts)
-    spread = pl.pallas_call(
-        sum_kernel,
-        out_shape=shape(8, *size, dtype=BF16),
-        in_specs=[VMEM],
-        out_specs=VMEM,
+        out_specs=(VMEM, VMEM),
         compiler_params=LIMIT,
         name="total",
     )(lax.all_to_all(parts, "z", 0, 0, tiled=True))
+    extras = [gram] + [turn(gram, k, "x") for k in (1, 2, 3)]
     line = lax.all_to_all(spread, "z", 0, 0, tiled=True)
-    body, extra = line[:, :ROWS, :], line[:, ROWS:, :]
-    extras = [extra] + [turn(extra, k, "x") for k in (2, 1, 3)]
-    bodies = [body] + [turn(body, k, "x") for k in (2, 1, 3)]
-    extras = [extras[0], extras[2], extras[1], extras[3]]
-    bodies = [bodies[0], bodies[2], bodies[1], bodies[3]]
-    q, r, inv, lead, coef = pl.pallas_call(
+    bodies = [line] + [turn(line, k, "x") for k in (1, 2, 3)]
+    q, r, inv = pl.pallas_call(
         factor_kernel,
-        out_shape=(
-            shape(2 * HALF, K, dtype=BF16),
-            shape(K, K),
-            shape(2 * K, K, dtype=BF16),
-            shape(PARTS, K),
-            shape(TILE, PARTS),
-        ),
-        in_specs=[SMEM] + [VMEM] * 6,
-        out_specs=(VMEM,) * 5,
+        out_shape=(shape(2 * HALF, K, dtype=BF16), shape(K, K), shape(2 * K, K, dtype=BF16)),
+        in_specs=[SMEM] + [VMEM] * 5,
+        out_specs=(VMEM,) * 3,
         scratch_shapes=[pltpu.VMEM((K, 2 * K), F32)],
         compiler_params=LIMIT,
-        cost_estimate=pl.CostEstimate(flops=12 * 10**9, bytes_accessed=4 * 2**20, transcendentals=0),
+        cost_estimate=cost(13),
         name="factor",
-    )(meta, *extras, mine, other)
+    )(meta, *extras, slab)
     z = pl.pallas_call(
         back_solve_kernel,
         out_shape=shape(CB * TILE, K),
-        in_specs=[SMEM] + [VMEM] * 7,
+        in_specs=[SMEM] + [VMEM] * 5,
         out_specs=HBM,
         scratch_shapes=[pltpu.VMEM((4, 8 * ROWS, K), F32), pltpu.SemaphoreType.DMA((4,))],
         compiler_params=LIMIT,
         name="z",
-    )(meta, *bodies, inv, lead, coef)
+    )(meta, *bodies, inv)
     return q, r, z
 
 

time: 124 us -> 127 us (1.024)
  the two profiles are of different devices: /device:TPU:8 before, /device:TPU:2 now
where the time goes in v4:
time: 127 us; the launch traced here: 126 us
  starting transfers between devices  40.9 us (32%)
  Pallas kernels  34.1 us (27%)
  waiting for transfers between devices  33.3 us (26%)
  blocking collectives  13.8 us (11%)
  local copies, waits for them, and re-layouts  2.42 us (2%)
  between operations  1.66 us (1%)
    ppermute x18, starting transfers between devices, turn(): return lax.ppermute(a, axis, [(i, (i + k) % 4) for i in range(4)])  29.9 us
    ppermute x18, waiting for transfers between devices, turn(): return lax.ppermute(a, axis, [(i, (i + k) % 4) for i in range(4)])  18.6 us
    pallas_call x1, Pallas kernels, on_device(): pl.pallas_call(factor_kernel, out_shape=(shape(2 * HALF, K, dtype=BF16),...  14 us
    all_to_all x1, blocking collectives, on_device(): lax.all_to_all(parts, 'z', 0, 0, tiled=True)  13.8 us
    all_to_all x1, starting transfers between devices, on_device(): grams = lax.all_to_all(grams, 'z', 0, 0, tiled=True)  7.41 us
    all_to_all x1, waiting for transfers between devices, on_device(): line = lax.all_to_all(spread, 'z', 0, 0, tiled=True)  5.25 us
    all_to_all x1, waiting for transfers between devices, on_device(): grams = lax.all_to_all(grams, 'z', 0, 0, tiled=True)  5.25 us
    pallas_call x1, Pallas kernels, on_device(): pl.pallas_call(sketch_kernel, out_shape=(shape(HALF, K), shape(HALF, K)),...  4.95 us
  transfers between devices with their start and end apart: 22, of which 9 were waited for; matrix products, arithmetic and copies ran while one was open for 0% of the time, Pallas kernels for 17%

profile of v4, /device:TPU:2, one launch (start us, length us, event | category | flops | bytes accessed | tf_op | source)
XLA Modules:
  0.0 126.4 jit_solution(1172164078613720050)
XLA Ops:
  1.3 0.8 concatenate.6.meta_ref
  2.0 4.9 %sketch.1 = (f32[1024,256]{1,0:T(8,128)S(1)}, f32[1024,256]{1,0:T(8,128)S(1)}) custom-call(s32[132]{0:T(256)S(1)} %concatenate.6.meta_ref, bf16[1,1,64,128,128]{4,3,2,1,0:T(8,128)(2,1)} %tiles_hbm.1, bf16[16,128,256]{2,1,0:T(8,128)(2,1)} %bitcast.10), custom_call_target="tpu_custom_call" | custom-call | tf_op jit(solution)/shard_map/sketch/pallas_call | solution.py:344
  7.0 0.1 collective-permute-start
  7.1 2.6 %collective-permute-done = f32[1024,256]{1,0:T(8,128)S(1)} collective-permute-done((f32[1024,256]{1,0:T(8,128)S(1)}, f32[1024,256]{1,0:T(8,128)S(1)}, u32[]{:S(2)}, u32[]{:S(2)}) %collective-permute-start) | collective-permute-done | bytes 1048608 | tf_op jit(solution)/shard_map/ppermute | solution.py:363
  9.7 0.0 copy-start
  9.7 0.2 fusion.3
  9.9 2.8 %collective-permute-start.1 = (bf16[256,256]{1,0:T(8,128)(2,1)S(1)}, bf16[256,256]{1,0:T(8,128)(2,1)S(1)}, u32[]{:S(2)}, u32[]{:S(2)}) collective-permute-start(bf16[256,256]{1,0:T(8,128)(2,1)S(1)} %get-tuple-element.28), channel_id=1, source_target_pairs={{0,4},{2,6},{4,0},{6,2},{1,5},{3,7},{5,1},{7,3},{8,12},{10,14},{12... | collective-permute-start | bytes 393224 | tf_op jit(solution)/shard_map/ppermute | solution.py:361
  12.7 0.0 collective-permute-start.2
  12.7 3.2 %collective-permute-start.3 = (bf16[256,256]{1,0:T(8,128)(2,1)S(1)}, bf16[256,256]{1,0:T(8,128)(2,1)S(1)}, u32[]{:S(2)}, u32[]{:S(2)}) collective-permute-start(bf16[256,256]{1,0:T(8,128)(2,1)S(1)} %get-tuple-element.48), channel_id=1, source_target_pairs={{0,6},{2,0},{4,2},{6,4},{1,7},{3,1},{5,3},{7,5},{8,14},{10,8},{12,... | collective-permute-start | bytes 393224 | tf_op jit(solution)/shard_map/ppermute | solution.py:361
  15.9 0.0 copy-done
  15.9 4.7 %flip.1 = (bf16[64,128,128]{2,1,0:T(8,128)(2,1)S(1)}, s32[140]{0:T(256)S(1)}) custom-call(s32[132]{0:T(256)S(1)} %concatenate.6.meta_ref, bf16[64,128,128]{2,1,0:T(8,128)(2,1)S(1)} %bitcast.9), custom_call_target="tpu_custom_call" | custom-call | flops 4000000000 | bytes 1048576 | tf_op jit(solution)/shard_map/flip/pallas_call | solution.py:367
  20.6 0.0 copy-start.1
  20.6 0.0 collective-permute-done.1
  20.6 0.0 collective-permute-done.2
  20.6 0.0 collective-permute-done.3
  20.6 0.1 fusion.2
  20.7 0.7 collective-permute-start.4
  21.5 2.6 %collective-permute-start.6 = (bf16[256,256]{1,0:T(8,128)(2,1)S(1)}, bf16[256,256]{1,0:T(8,128)(2,1)S(1)}, u32[]{:S(2)}, u32[]{:S(2)}) collective-permute-start(bf16[256,256]{1,0:T(8,128)(2,1)S(1)} %fusion.2), channel_id=1, source_target_pairs={{0,6},{2,0},{4,2},{6,4},{1,7},{3,1},{5,3},{7,5},{8,14},{10,8},{12,... | collective-permute-start | bytes 393224 | tf_op jit(solution)/shard_map/ppermute | solution.py:361
  24.0 0.0 collective-permute-start.5
  24.0 2.9 %collective-permute-done.4 = bf16[256,256]{1,0:T(8,128)(2,1)S(1)} collective-permute-done((bf16[256,256]{1,0:T(8,128)(2,1)S(1)}, bf16[256,256]{1,0:T(8,128)(2,1)S(1)}, u32[]{:S(2)}, u32[]{:S(2)}) %collective-permute-start.4) | collective-permute-done | bytes 131104 | tf_op jit(solution)/shard_map/ppermute | solution.py:361
  27.0 3.5 %collective-permute-done.5 = bf16[256,256]{1,0:T(8,128)(2,1)S(1)} collective-permute-done((bf16[256,256]{1,0:T(8,128)(2,1)S(1)}, bf16[256,256]{1,0:T(8,128)(2,1)S(1)}, u32[]{:S(2)}, u32[]{:S(2)}) %collective-permute-start.5) | collective-permute-done | bytes 131104 | tf_op jit(solution)/shard_map/ppermute | solution.py:361
  30.5 0.0 collective-permute-done.6
  30.5 0.1 collective-permute-start.7
  30.6 0.3 gram.1.gram_ref
  31.0 1.5 %collective-permute-done.7.other_ref = bf16[1024,256]{1,0:T(8,128)(2,1)S(1)} collective-permute-done((bf16[1024,256]{1,0:T(8,128)(2,1)S(1)}, bf16[1024,256]{1,0:T(8,128)(2,1)S(1)}, u32[]{:S(2)}, u32[]{:S(2)}) %collective-permute-start.7) | collective-permute-done | bytes 524320 | tf_op jit(solution)/shard_map/ppermute | solution.py:382
  32.5 1.4 %slab.1 = (bf16[16,128,256]{2,1,0:T(8,128)(2,1)S(1)}, bf16[8,16,256]{2,1,0:T(8,128)(2,1)S(1)}, bf16[8,16,256]{2,1,0:T(8,128)(2,1)S(1)}, bf16[8,16,256]{2,1,0:T(8,128)(2,1)S(1)}, bf16[8,16,256]{2,1,0:T(8,128)(2,1)S(1)}) custom-call(s32[132]{0:T(256)S(1)} %concatenate.6.meta_ref, bf16[1024,256]{1,0:T(8,128)(2,1)S(1)} %constant_dynamic-update-slice_fusion.mine_ref, ...), custom_call_target="tpu_custom_call" | custom-call | flops 1000000000 | bytes 1048576 | tf_op jit(solution)/shard_map/slab/pallas_call | solution.py:392
  34.0 0.0 copy-done.1
  34.0 2.6 %back1.1 = (bf16[8,64,256]{2,1,0:T(8,128)(2,1)S(1)}, bf16[8,64,256]{2,1,0:T(8,128)(2,1)S(1)}, bf16[8,64,256]{2,1,0:T(8,128)(2,1)S(1)}) custom-call(s32[140]{0:T(256)S(1)} %get-tuple-element.27.meta_ref, bf16[64,128,128]{2,1,0:T(8,128)(2,1)S(1)} %get-tuple-element.30.tiles_ref, bf16[16,128,256]{2,1,0:T(8,128)(2,1)S(1)} %get-tuple-element.32.s_ref), custom_call_target="tpu_custom_call" | custom-call | flops 10000000000 | bytes 1048576 | tf_op jit(solution)/shard_map/back1/pallas_call | solution.py:405
  36.5 1.5 %collective-permute-start.8 = (bf16[8,64,256]{2,1,0:T(8,128)(2,1)S(1)}, bf16[8,64,256]{2,1,0:T(8,128)(2,1)S(1)}, u32[]{:S(2)}, u32[]{:S(2)}) collective-permute-start(bf16[8,64,256]{2,1,0:T(8,128)(2,1)S(1)} %get-tuple-element.33), channel_id=1, source_target_pairs={{0,8},{8,16},{16,24},{24,0},{1,9},{9,17},{17,25},{25,1},{2,10},{10... | collective-permute-start | bytes 786440 | tf_op jit(solution)/shard_map/ppermute | solution.py:361
  38.0 2.4 %collective-permute-start.9 = (bf16[8,64,256]{2,1,0:T(8,128)(2,1)S(1)}, bf16[8,64,256]{2,1,0:T(8,128)(2,1)S(1)}, u32[]{:S(2)}, u32[]{:S(2)}) collective-permute-start(bf16[8,64,256]{2,1,0:T(8,128)(2,1)S(1)} %get-tuple-element.34), channel_id=1, source_target_pairs={{0,16},{8,24},{16,0},{24,8},{1,17},{9,25},{17,1},{25,9},{2,18},{10... | collective-permute-start | bytes 786440 | tf_op jit(solution)/shard_map/ppermute | solution.py:361
  40.5 0.0 collective-permute-start.10
  40.5 2.0 %collective-permute-start.11 = (bf16[8,16,256]{2,1,0:T(8,128)(2,1)S(1)}, bf16[8,16,256]{2,1,0:T(8,128)(2,1)S(1)}, u32[]{:S(2)}, u32[]{:S(2)}) collective-permute-start(bf16[8,16,256]{2,1,0:T(8,128)(2,1)S(1)} %get-tuple-element.37), channel_id=1, source_target_pairs={{0,8},{8,16},{16,24},{24,0},{1,9},{9,17},{17,25},{25,1},{2,10},{10... | collective-permute-start | bytes 196616 | tf_op jit(solution)/shard_map/ppermute | solution.py:361
  42.5 2.3 %collective-permute-start.12 = (bf16[8,16,256]{2,1,0:T(8,128)(2,1)S(1)}, bf16[8,16,256]{2,1,0:T(8,128)(2,1)S(1)}, u32[]{:S(2)}, u32[]{:S(2)}) collective-permute-start(bf16[8,16,256]{2,1,0:T(8,128)(2,1)S(1)} %get-tuple-element.38), channel_id=1, source_target_pairs={{0,16},{8,24},{16,0},{24,8},{1,17},{9,25},{17,1},{25,9},{2,18},{10... | collective-permute-start | bytes 196616 | tf_op jit(solution)/shard_map/ppermute | solution.py:361
  44.8 8.1 %collective-permute-done.11.b_ref = bf16[8,16,256]{2,1,0:T(8,128)(2,1)S(1)} collective-permute-done((bf16[8,16,256]{2,1,0:T(8,128)(2,1)S(1)}, bf16[8,16,256]{2,1,0:T(8,128)(2,1)S(1)}, u32[]{:S(2)}, u32[]{:S(2)}) %collective-permute-start.11) | collective-permute-done | bytes 65568 | tf_op jit(solution)/shard_map/ppermute | solution.py:361
  52.9 0.7 collective-permute-start.13
  53.6 1.6 %collective-permute-done.12.c_ref = bf16[8,16,256]{2,1,0:T(8,128)(2,1)S(1)} collective-permute-done((bf16[8,16,256]{2,1,0:T(8,128)(2,1)S(1)}, bf16[8,16,256]{2,1,0:T(8,128)(2,1)S(1)}, u32[]{:S(2)}, u32[]{:S(2)}) %collective-permute-start.12) | collective-permute-done | bytes 65568 | tf_op jit(solution)/shard_map/ppermute | solution.py:361
  55.3 2.4 %collective-permute-done.13.d_ref = bf16[8,16,256]{2,1,0:T(8,128)(2,1)S(1)} collective-permute-done((bf16[8,16,256]{2,1,0:T(8,128)(2,1)S(1)}, bf16[8,16,256]{2,1,0:T(8,128)(2,1)S(1)}, u32[]{:S(2)}, u32[]{:S(2)}) %collective-permute-start.13) | collective-permute-done | bytes 65568 | tf_op jit(solution)/shard_map/ppermute | solution.py:361
  57.6 0.7 gram_sum.1
  58.3 7.4 %all-to-all-start = ((bf16[8,16,256]{2,1,0:T(8,128)(2,1)}), bf16[8,16,256]{2,1,0:T(8,128)(2,1)S(1)}, u32[]{:S(2)}, u32[]{:S(2)}) async-start(bf16[8,16,256]{2,1,0:T(8,128)(2,1)} %gram_sum.1), calls=%async_computation | async-start | bytes 131072 | tf_op jit(solution)/shard_map/all_to_all | solution.py:424
  65.8 1.6 %copy-done.2 = bf16[64,128,128]{2,1,0:T(8,128)(2,1)S(1)} copy-done((bf16[64,128,128]{2,1,0:T(8,128)(2,1)S(1)}, bf16[64,128,128]{2,1,0:T(8,128)(2,1)}, u32[]{:S(2)}) %copy-start.2) | copy-done | bytes 2097176
  67.3 1.5 %back0.1.a_ref = bf16[8,64,256]{2,1,0:T(8,128)(2,1)S(1)} custom-call(s32[140]{0:T(256)S(1)} %get-tuple-element.27.meta_ref, bf16[64,128,128]{2,1,0:T(8,128)(2,1)S(1)} %copy-done.2, bf16[16,128,256]{2,1,0:T(8,128)(2,1)S(1)} %get-tuple-element.32.s_ref), custom_call_target="tpu_custom_call" | custom-call | flops 1000000000 | bytes 1048576 | tf_op jit(solution)/shard_map/back0/pallas_call | solution.py:405
  68.9 5.3 %all-to-all-done.gram_ref = bf16[8,16,256]{2,1,0:T(8,128)(2,1)S(1)} async-done(((bf16[8,16,256]{2,1,0:T(8,128)(2,1)}), bf16[8,16,256]{2,1,0:T(8,128)(2,1)S(1)}, u32[]{:S(2)}, u32[]{:S(2)}) %all-to-all-start) | async-done | bytes 65568 | tf_op jit(solution)/shard_map/all_to_all | solution.py:424
  74.1 0.0 collective-permute-done.8.b_ref
  74.1 0.0 collective-permute-done.9.c_ref
  74.1 0.0 collective-permute-done.10.d_ref
  74.1 0.2 partial.1
  74.3 13.8 %all_to_all.15.in_ref = bf16[8,80,256]{2,1,0:T(8,128)(2,1)S(1)} all-to-all(bf16[8,80,256]{2,1,0:T(8,128)(2,1)S(1)} %partial.1), channel_id=1, replica_groups=mesh['z'=8,'x'=4,'y'=4,'c'=2] {'z'}, dimensions={0} | all-to-all | bytes 655360 | tf_op jit(solution)/shard_map/all_to_all | solution.py:441
  88.1 1.2 total.1
  89.2 3.4 %all-to-all-start.2 = ((bf16[8,80,256]{2,1,0:T(8,128)(2,1)}), bf16[8,80,256]{2,1,0:T(8,128)(2,1)S(1)}, u32[]{:S(2)}, u32[]{:S(2)}) async-start(bf16[8,80,256]{2,1,0:T(8,128)(2,1)} %get-tuple-element.43), calls=%async_computation.2 | async-start | bytes 655360 | tf_op jit(solution)/shard_map/all_to_all | solution.py:443
  92.7 0.8 collective-permute-start.16
  93.5 2.5 %collective-permute-start.15 = (bf16[8,16,256]{2,1,0:T(8,128)(2,1)S(1)}, bf16[8,16,256]{2,1,0:T(8,128)(2,1)S(1)}, u32[]{:S(2)}, u32[]{:S(2)}) collective-permute-start(bf16[8,16,256]{2,1,0:T(8,128)(2,1)S(1)} %get-tuple-element.40.e0_ref), channel_id=1, source_target_pairs={{0,16},{8,24},{16,0},{24,8},{1,17},{9,25},{17,1},{25,9},{2,18},{10... | collective-permute-start | bytes 196616 | tf_op jit(solution)/shard_map/ppermute | solution.py:361
  96.0 2.5 %collective-permute-start.14 = (bf16[8,16,256]{2,1,0:T(8,128)(2,1)S(1)}, bf16[8,16,256]{2,1,0:T(8,128)(2,1)S(1)}, u32[]{:S(2)}, u32[]{:S(2)}) collective-permute-start(bf16[8,16,256]{2,1,0:T(8,128)(2,1)S(1)} %get-tuple-element.40.e0_ref), channel_id=1, source_target_pairs={{0,8},{8,16},{16,24},{24,0},{1,9},{9,17},{17,25},{25,1},{2,10},{10... | collective-permute-start | bytes 196616 | tf_op jit(solution)/shard_map/ppermute | solution.py:361
  98.5 5.3 %all-to-all-done.2.b0_ref = bf16[8,80,256]{2,1,0:T(8,128)(2,1)S(1)} async-done(((bf16[8,80,256]{2,1,0:T(8,128)(2,1)}), bf16[8,80,256]{2,1,0:T(8,128)(2,1)S(1)}, u32[]{:S(2)}, u32[]{:S(2)}) %all-to-all-start.2) | async-done | bytes 327712 | tf_op jit(solution)/shard_map/all_to_all | solution.py:443
  103.8 0.7 collective-permute-start.19
  104.5 2.5 %collective-permute-start.18 = (bf16[8,80,256]{2,1,0:T(8,128)(2,1)S(1)}, bf16[8,80,256]{2,1,0:T(8,128)(2,1)S(1)}, u32[]{:S(2)}, u32[]{:S(2)}) collective-permute-start(bf16[8,80,256]{2,1,0:T(8,128)(2,1)S(1)} %all-to-all-done.2.b0_ref), channel_id=1, source_target_pairs={{0,16},{8,24},{16,0},{24,8},{1,17},{9,25},{17,1},{25,9},{2,18},{10... | collective-permute-start | bytes 983048 | tf_op jit(solution)/shard_map/ppermute | solution.py:361
  107.0 0.0 collective-permute-done.16.e3_ref
  107.0 2.5 %collective-permute-start.17 = (bf16[8,80,256]{2,1,0:T(8,128)(2,1)S(1)}, bf16[8,80,256]{2,1,0:T(8,128)(2,1)S(1)}, u32[]{:S(2)}, u32[]{:S(2)}) collective-permute-start(bf16[8,80,256]{2,1,0:T(8,128)(2,1)S(1)} %all-to-all-done.2.b0_ref), channel_id=1, source_target_pairs={{0,8},{8,16},{16,24},{24,0},{1,9},{9,17},{17,25},{25,1},{2,10},{10... | collective-permute-start | bytes 983048 | tf_op jit(solution)/shard_map/ppermute | solution.py:361
  109.5 0.0 collective-permute-done.15.e2_ref
  109.5 0.0 collective-permute-done.14.e1_ref
  109.5 14.0 %factor.1 = (bf16[2048,256]{1,0:T(8,128)(2,1)}, f32[256,256]{1,0:T(8,128)}, bf16[512,256]{1,0:T(8,128)(2,1)S(1)}) custom-call(s32[132]{0:T(256)S(1)} %concatenate.6.meta_ref, bf16[8,16,256]{2,1,0:T(8,128)(2,1)S(1)} %get-tuple-element.40.e0_ref, bf16[8,16,256]{2,1,0:T(8,128)(2,1)S(1)} %collective-permute-done.14.e1_ref, ...), custom_call_target="tpu_custom_call" | custom-call | flops 12999999488 | bytes 1048576 | tf_op jit(solution)/shard_map/factor/pallas_call | solution.py:445
  123.5 0.0 collective-permute-done.19.b3_ref
  123.5 0.0 collective-permute-done.18.b2_ref
  123.5 0.0 collective-permute-done.17.b1_ref
  123.6 2.6 %z.1 = f32[2048,256]{1,0:T(8,128)} custom-call(s32[132]{0:T(256)S(1)} %concatenate.6.meta_ref, bf16[8,80,256]{2,1,0:T(8,128)(2,1)S(1)} %all-to-all-done.2.b0_ref, bf16[8,80,256]{2,1,0:T(8,128)(2,1)S(1)} %collective-permute-done.17.b1_ref, bf16[8,80,256]{2,1,0:T(8,128)(2,1)S(1)} %collective-permute-done.18.b2_ref, ...), custom_call_target="tpu_custom_call" | custom-call | tf_op jit(solution)/shard_map/z/pallas_call | solution.py:455
  (6 shorter events, 0.1 us)
Async XLA Ops:
  7.0 2.7 %collective-permute-start = (f32[1024,256]{1,0:T(8,128)S(1)}, f32[1024,256]{1,0:T(8,128)S(1)}, u32[]{:S(2)}, u32[]{:S(2)}) collective-permute-start(f32[1024,256]{1,0:T(8,128)S(1)} %get-tuple-element.25), channel_id=1, source_target_pairs={{0,1},{1,0},{2,3},{3,2},{4,5},{5,4},{6,7},{7,6},{8,9},{9,8},{10,11... | collective-permute-start | bytes 3145736 | tf_op jit(solution)/shard_map/ppermute | solution.py:363
  9.7 6.2 %copy-start = (bf16[1,1,64,128,128]{4,3,2,1,0:T(8,128)(2,1)S(1)}, bf16[1,1,64,128,128]{4,3,2,1,0:T(8,128)(2,1)}, u32[]{:S(2)}) copy-start(bf16[1,1,64,128,128]{4,3,2,1,0:T(8,128)(2,1)} %tiles_hbm.1) | copy-start | bytes 6291460
  9.9 10.7 %collective-permute-start.1 = (bf16[256,256]{1,0:T(8,128)(2,1)S(1)}, bf16[256,256]{1,0:T(8,128)(2,1)S(1)}, u32[]{:S(2)}, u32[]{:S(2)}) collective-permute-start(bf16[256,256]{1,0:T(8,128)(2,1)S(1)} %get-tuple-element.28), channel_id=1, source_target_pairs={{0,4},{2,6},{4,0},{6,2},{1,5},{3,7},{5,1},{7,3},{8,12},{10,14},{12... | collective-permute-start | bytes 393224 | tf_op jit(solution)/shard_map/ppermute | solution.py:361
  12.7 7.9 %collective-permute-start.2 = (bf16[256,256]{1,0:T(8,128)(2,1)S(1)}, bf16[256,256]{1,0:T(8,128)(2,1)S(1)}, u32[]{:S(2)}, u32[]{:S(2)}) collective-permute-start(bf16[256,256]{1,0:T(8,128)(2,1)S(1)} %get-tuple-element.47), channel_id=1, source_target_pairs={{0,2},{2,4},{4,6},{6,0},{1,3},{3,5},{5,7},{7,1},{8,10},{10,12},{12... | collective-permute-start | bytes 393224 | tf_op jit(solution)/shard_map/ppermute | solution.py:361
  12.7 7.9 %collective-permute-start.3 = (bf16[256,256]{1,0:T(8,128)(2,1)S(1)}, bf16[256,256]{1,0:T(8,128)(2,1)S(1)}, u32[]{:S(2)}, u32[]{:S(2)}) collective-permute-start(bf16[256,256]{1,0:T(8,128)(2,1)S(1)} %get-tuple-element.48), channel_id=1, source_target_pairs={{0,6},{2,0},{4,2},{6,4},{1,7},{3,1},{5,3},{7,5},{8,14},{10,8},{12,... | collective-permute-start | bytes 393224 | tf_op jit(solution)/shard_map/ppermute | solution.py:361
  20.6 13.4 %copy-start.1 = (bf16[64,128,128]{2,1,0:T(8,128)(2,1)}, bf16[64,128,128]{2,1,0:T(8,128)(2,1)S(1)}, u32[]{:S(2)}) copy-start(bf16[64,128,128]{2,1,0:T(8,128)(2,1)S(1)} %get-tuple-element.30.tiles_ref) | copy-start | bytes 6291460
  20.7 6.3 %collective-permute-start.4 = (bf16[256,256]{1,0:T(8,128)(2,1)S(1)}, bf16[256,256]{1,0:T(8,128)(2,1)S(1)}, u32[]{:S(2)}, u32[]{:S(2)}) collective-permute-start(bf16[256,256]{1,0:T(8,128)(2,1)S(1)} %fusion.2), channel_id=1, source_target_pairs={{0,2},{2,4},{4,6},{6,0},{1,3},{3,5},{5,7},{7,1},{8,10},{10,12},{12... | collective-permute-start | bytes 393224 | tf_op jit(solution)/shard_map/ppermute | solution.py:361
  21.5 9.1 %collective-permute-start.6 = (bf16[256,256]{1,0:T(8,128)(2,1)S(1)}, bf16[256,256]{1,0:T(8,128)(2,1)S(1)}, u32[]{:S(2)}, u32[]{:S(2)}) collective-permute-start(bf16[256,256]{1,0:T(8,128)(2,1)S(1)} %fusion.2), channel_id=1, source_target_pairs={{0,6},{2,0},{4,2},{6,4},{1,7},{3,1},{5,3},{7,5},{8,14},{10,8},{12,... | collective-permute-start | bytes 393224 | tf_op jit(solution)/shard_map/ppermute | solution.py:361
  24.0 6.5 %collective-permute-start.5 = (bf16[256,256]{1,0:T(8,128)(2,1)S(1)}, bf16[256,256]{1,0:T(8,128)(2,1)S(1)}, u32[]{:S(2)}, u32[]{:S(2)}) collective-permute-start(bf16[256,256]{1,0:T(8,128)(2,1)S(1)} %fusion.2), channel_id=1, source_target_pairs={{0,4},{2,6},{4,0},{6,2},{1,5},{3,7},{5,1},{7,3},{8,12},{10,14},{12... | collective-permute-start | bytes 393224 | tf_op jit(solution)/shard_map/ppermute | solution.py:361
  30.5 2.0 %collective-permute-start.7 = (bf16[1024,256]{1,0:T(8,128)(2,1)S(1)}, bf16[1024,256]{1,0:T(8,128)(2,1)S(1)}, u32[]{:S(2)}, u32[]{:S(2)}) collective-permute-start(bf16[1024,256]{1,0:T(8,128)(2,1)S(1)} %constant_dynamic-update-slice_fusion.mine_ref), channel_id=1, source_target_pairs={{0,1},{1,0},{2,3},{3,2},{4,5},{5,4},{6,7},{7,6},{8,9},{9,8},{10,11... | collective-permute-start | bytes 1572872 | tf_op jit(solution)/shard_map/ppermute | solution.py:382
  36.5 37.6 %collective-permute-start.8 = (bf16[8,64,256]{2,1,0:T(8,128)(2,1)S(1)}, bf16[8,64,256]{2,1,0:T(8,128)(2,1)S(1)}, u32[]{:S(2)}, u32[]{:S(2)}) collective-permute-start(bf16[8,64,256]{2,1,0:T(8,128)(2,1)S(1)} %get-tuple-element.33), channel_id=1, source_target_pairs={{0,8},{8,16},{16,24},{24,0},{1,9},{9,17},{17,25},{25,1},{2,10},{10... | collective-permute-start | bytes 786440 | tf_op jit(solution)/shard_map/ppermute | solution.py:361
  38.0 36.1 %collective-permute-start.9 = (bf16[8,64,256]{2,1,0:T(8,128)(2,1)S(1)}, bf16[8,64,256]{2,1,0:T(8,128)(2,1)S(1)}, u32[]{:S(2)}, u32[]{:S(2)}) collective-permute-start(bf16[8,64,256]{2,1,0:T(8,128)(2,1)S(1)} %get-tuple-element.34), channel_id=1, source_target_pairs={{0,16},{8,24},{16,0},{24,8},{1,17},{9,25},{17,1},{25,9},{2,18},{10... | collective-permute-start | bytes 786440 | tf_op jit(solution)/shard_map/ppermute | solution.py:361
  40.5 33.7 %collective-permute-start.10 = (bf16[8,64,256]{2,1,0:T(8,128)(2,1)S(1)}, bf16[8,64,256]{2,1,0:T(8,128)(2,1)S(1)}, u32[]{:S(2)}, u32[]{:S(2)}) collective-permute-start(bf16[8,64,256]{2,1,0:T(8,128)(2,1)S(1)} %get-tuple-element.35), channel_id=1, source_target_pairs={{0,24},{8,0},{16,8},{24,16},{1,25},{9,1},{17,9},{25,17},{2,26},{10... | collective-permute-start | bytes 786440 | tf_op jit(solution)/shard_map/ppermute | solution.py:361
  40.5 12.4 %collective-permute-start.11 = (bf16[8,16,256]{2,1,0:T(8,128)(2,1)S(1)}, bf16[8,16,256]{2,1,0:T(8,128)(2,1)S(1)}, u32[]{:S(2)}, u32[]{:S(2)}) collective-permute-start(bf16[8,16,256]{2,1,0:T(8,128)(2,1)S(1)} %get-tuple-element.37), channel_id=1, source_target_pairs={{0,8},{8,16},{16,24},{24,0},{1,9},{9,17},{17,25},{25,1},{2,10},{10... | collective-permute-start | bytes 196616 | tf_op jit(solution)/shard_map/ppermute | solution.py:361
  42.5 12.8 %collective-permute-start.12 = (bf16[8,16,256]{2,1,0:T(8,128)(2,1)S(1)}, bf16[8,16,256]{2,1,0:T(8,128)(2,1)S(1)}, u32[]{:S(2)}, u32[]{:S(2)}) collective-permute-start(bf16[8,16,256]{2,1,0:T(8,128)(2,1)S(1)} %get-tuple-element.38), channel_id=1, source_target_pairs={{0,16},{8,24},{16,0},{24,8},{1,17},{9,25},{17,1},{25,9},{2,18},{10... | collective-permute-start | bytes 196616 | tf_op jit(solution)/shard_map/ppermute | solution.py:361
  52.9 4.7 %collective-permute-start.13 = (bf16[8,16,256]{2,1,0:T(8,128)(2,1)S(1)}, bf16[8,16,256]{2,1,0:T(8,128)(2,1)S(1)}, u32[]{:S(2)}, u32[]{:S(2)}) collective-permute-start(bf16[8,16,256]{2,1,0:T(8,128)(2,1)S(1)} %get-tuple-element.39), channel_id=1, source_target_pairs={{0,24},{8,0},{16,8},{24,16},{1,25},{9,1},{17,9},{25,17},{2,26},{10... | collective-permute-start | bytes 196616 | tf_op jit(solution)/shard_map/ppermute | solution.py:361
  58.3 15.8 %all-to-all-start = ((bf16[8,16,256]{2,1,0:T(8,128)(2,1)}), bf16[8,16,256]{2,1,0:T(8,128)(2,1)S(1)}, u32[]{:S(2)}, u32[]{:S(2)}) async-start(bf16[8,16,256]{2,1,0:T(8,128)(2,1)} %gram_sum.1), calls=%async_computation | async-start | bytes 131072 | tf_op jit(solution)/shard_map/all_to_all | solution.py:424
  65.8 1.6 %copy-start.2 = (bf16[64,128,128]{2,1,0:T(8,128)(2,1)S(1)}, bf16[64,128,128]{2,1,0:T(8,128)(2,1)}, u32[]{:S(2)}) copy-start(bf16[64,128,128]{2,1,0:T(8,128)(2,1)} %copy-done.1) | copy-start | bytes 6291460
  89.2 14.5 %all-to-all-start.2 = ((bf16[8,80,256]{2,1,0:T(8,128)(2,1)}), bf16[8,80,256]{2,1,0:T(8,128)(2,1)S(1)}, u32[]{:S(2)}, u32[]{:S(2)}) async-start(bf16[8,80,256]{2,1,0:T(8,128)(2,1)} %get-tuple-element.43), calls=%async_computation.2 | async-start | bytes 655360 | tf_op jit(solution)/shard_map/all_to_all | solution.py:443
  92.7 14.4 %collective-permute-start.16 = (bf16[8,16,256]{2,1,0:T(8,128)(2,1)S(1)}, bf16[8,16,256]{2,1,0:T(8,128)(2,1)S(1)}, u32[]{:S(2)}, u32[]{:S(2)}) collective-permute-start(bf16[8,16,256]{2,1,0:T(8,128)(2,1)S(1)} %get-tuple-element.40.e0_ref), channel_id=1, source_target_pairs={{0,24},{8,0},{16,8},{24,16},{1,25},{9,1},{17,9},{25,17},{2,26},{10... | collective-permute-start | bytes 196616 | tf_op jit(solution)/shard_map/ppermute | solution.py:361
  93.5 16.1 %collective-permute-start.15 = (bf16[8,16,256]{2,1,0:T(8,128)(2,1)S(1)}, bf16[8,16,256]{2,1,0:T(8,128)(2,1)S(1)}, u32[]{:S(2)}, u32[]{:S(2)}) collective-permute-start(bf16[8,16,256]{2,1,0:T(8,128)(2,1)S(1)} %get-tuple-element.40.e0_ref), channel_id=1, source_target_pairs={{0,16},{8,24},{16,0},{24,8},{1,17},{9,25},{17,1},{25,9},{2,18},{10... | collective-permute-start | bytes 196616 | tf_op jit(solution)/shard_map/ppermute | solution.py:361
  96.0 13.5 %collective-permute-start.14 = (bf16[8,16,256]{2,1,0:T(8,128)(2,1)S(1)}, bf16[8,16,256]{2,1,0:T(8,128)(2,1)S(1)}, u32[]{:S(2)}, u32[]{:S(2)}) collective-permute-start(bf16[8,16,256]{2,1,0:T(8,128)(2,1)S(1)} %get-tuple-element.40.e0_ref), channel_id=1, source_target_pairs={{0,8},{8,16},{16,24},{24,0},{1,9},{9,17},{17,25},{25,1},{2,10},{10... | collective-permute-start | bytes 196616 | tf_op jit(solution)/shard_map/ppermute | solution.py:361
  103.8 19.8 %collective-permute-start.19 = (bf16[8,80,256]{2,1,0:T(8,128)(2,1)S(1)}, bf16[8,80,256]{2,1,0:T(8,128)(2,1)S(1)}, u32[]{:S(2)}, u32[]{:S(2)}) collective-permute-start(bf16[8,80,256]{2,1,0:T(8,128)(2,1)S(1)} %all-to-all-done.2.b0_ref), channel_id=1, source_target_pairs={{0,24},{8,0},{16,8},{24,16},{1,25},{9,1},{17,9},{25,17},{2,26},{10... | collective-permute-start | bytes 983048 | tf_op jit(solution)/shard_map/ppermute | solution.py:361
  104.5 19.0 %collective-permute-start.18 = (bf16[8,80,256]{2,1,0:T(8,128)(2,1)S(1)}, bf16[8,80,256]{2,1,0:T(8,128)(2,1)S(1)}, u32[]{:S(2)}, u32[]{:S(2)}) collective-permute-start(bf16[8,80,256]{2,1,0:T(8,128)(2,1)S(1)} %all-to-all-done.2.b0_ref), channel_id=1, source_target_pairs={{0,16},{8,24},{16,0},{24,8},{1,17},{9,25},{17,1},{25,9},{2,18},{10... | collective-permute-start | bytes 983048 | tf_op jit(solution)/shard_map/ppermute | solution.py:361
  107.0 16.5 %collective-permute-start.17 = (bf16[8,80,256]{2,1,0:T(8,128)(2,1)S(1)}, bf16[8,80,256]{2,1,0:T(8,128)(2,1)S(1)}, u32[]{:S(2)}, u32[]{:S(2)}) collective-permute-start(bf16[8,80,256]{2,1,0:T(8,128)(2,1)S(1)} %all-to-all-done.2.b0_ref), channel_id=1, source_target_pairs={{0,8},{8,16},{16,24},{24,0},{1,9},{9,17},{17,25},{25,1},{2,10},{10... | collective-permute-start | bytes 983048 | tf_op jit(solution)/shard_map/ppermute | solution.py:361

commit v5 on v4

--- a/solution.py
+++ b/solution.py
@@ -19,13 +19,16 @@
 PARTS = 32
 ROWS = CB * TILE // PARTS
 EXTRA = 16
+TAIL = 8
 GROUP = 4
 NB = 64
+FIRST = 1
 LOAD = 8
 LIVE = 3
 AT = 4
 COLS = AT + SLOTS
 START = COLS + SLOTS
+SOURCE = START + 8
 PIECE = HALF // 4
 VMEM = pl.BlockSpec(memory_space=pltpu.VMEM)
 SMEM = pl.BlockSpec(memory_space=pltpu.SMEM)
@@ -74,10 +77,10 @@
                 acc[place] += prod
 
     keep_ref[...] = acc[: RB // 2].reshape(HALF, K)
-    send_ref[...] = acc[RB // 2 :].reshape(HALF, K)
-
-
-def flip_kernel(meta_ref, tiles_ref, out_ref, sorted_ref, count, source):
+    send_ref[...] = acc[RB // 2 :].reshape(HALF, K).astype(BF16)
+
+
+def order_kernel(meta_ref, sorted_ref, count):
     live = meta_ref[LIVE]
     for i in range(8):
         count[i] = 0
@@ -107,16 +110,17 @@
         c = chunk(t)
         at = count[c]
         count[c] = at + 1
-        source[at] = t
+        sorted_ref[SOURCE + at] = t
         sorted_ref[AT + at] = meta_ref[AT + t] & (RB - 1)
         sorted_ref[COLS + at] = turned(t)
 
+
+def flip_kernel(meta_ref, tiles_ref, out_ref):
     @pl.loop(0, SLOTS // GROUP)
     def _(g):
         for i in range(GROUP):
             t = g * GROUP + i
-            tile = tiles_ref[source[t]].T
-            out_ref[t] = jnp.where(t < live, tile, jnp.zeros_like(tile))
+            out_ref[t] = tiles_ref[meta_ref[SOURCE + t]].T
 
 
 def gram_kernel(mine_ref, out_ref):
@@ -208,7 +212,7 @@
     norm = jnp.maximum(jnp.sum(leadf * leadf, axis=1, keepdims=True), 0.5)
     coef = (dot(lead, w.astype(BF16), 1, 1) / norm).astype(BF16)
     rest = w - dot(coef, lead, 0, 0)
-    row = iota((EXTRA, K), 0)
+    row = iota((TAIL, K), 0)
     wide = jnp.concatenate([coef.astype(F32), jnp.zeros((1, K - ROWS), F32)], axis=1)
     tail = jnp.where(row == 0, leadf, jnp.where(row == 1, wide, 0.0)).astype(BF16)
     body = rest.astype(BF16)
@@ -235,7 +239,6 @@
         scaled = []
         for j in range(8):
             inv = pltpu.reciprocal(s[j][j], approx=True)
-            inv = inv * (2.0 - s[j][j] * inv)
             for m in range(j + 1, 8):
                 ratio[j][m] = s[j][m] * inv
             for i in range(j + 1, 8):
@@ -259,10 +262,10 @@
     return jnp.concatenate(xs, axis=0)
 
 
-def factor(work):
+def factor(work, blocks):
     lane = iota((NB, 128), 1)
     row = iota((NB, 128), 0)
-    for b in range(K // NB):
+    for b in blocks:
         at = b * NB
         base = at // 128 * 128
         x = work[at : at + NB, base : base + 128]
@@ -270,14 +273,15 @@
             x = pltpu.roll(x, 128 - (at - base), 1)
         x = eliminate(jnp.where(lane < NB, x, jnp.where(lane - NB == row, 1.0, 0.0)))
         inv = pltpu.roll(x, 128 - NB, 1)[:, :NB]
-        u = dot(inv, work[at : at + NB, :], 1, 0, lax.Precision.HIGHEST)
-        work[at : at + NB, :] = u
+        for lo, hi in ((base, K), (K, K + min(base + 128, K))):
+            work[at : at + NB, lo:hi] = dot(inv, work[at : at + NB, lo:hi], 1, 0, lax.Precision.HIGHEST)
         if at + NB < K:
-            ut = u[:, :K].T
-            work[at + NB :, :] -= dot(ut[at + NB :], u, 1, 0, lax.Precision.HIGHEST)
-
-
-def factor_kernel(meta_ref, e0_ref, e1_ref, e2_ref, e3_ref, s_ref, q_ref, r_ref, inv_ref, work):
+            down = work[at : at + NB, :K].T[at + NB :]
+            for lo, hi in (((at + NB) // 128 * 128, K), (K, K + min(base + 128, K))):
+                work[at + NB :, lo:hi] -= dot(down, work[at : at + NB, lo:hi], 1, 0, lax.Precision.HIGHEST)
+
+
+def first_kernel(meta_ref, e0_ref, e1_ref, e2_ref, e3_ref, work):
     extra = jnp.concatenate([e[...].reshape(8 * EXTRA, K) for e in (e0_ref, e1_ref, e2_ref, e3_ref)], axis=0)
     p = iota((192, PARTS * EXTRA), 0)
     e = iota((192, PARTS * EXTRA), 1)
@@ -290,38 +294,49 @@
     work[K // 2 : 3 * K // 4, K // 2 : K] = packed[K // 2 :, : K // 2]
     work[3 * K // 4 :, K // 2 : K] = packed[K // 2 :, K // 2 :]
     work[:, K:] = jnp.where(iota((K, K), 0) == iota((K, K), 1), 1.0, 0.0)
-    factor(work)
+    factor(work, range(FIRST))
+
+
+def rest_kernel(begun_ref, r_ref, inv_ref, work):
+    work[...] = begun_ref[...]
+    factor(work, range(FIRST, K // NB))
     r_ref[...] = jnp.where(iota((K, K), 0) <= iota((K, K), 1), work[:, :K], 0.0)
     inv = work[:, K:]
     high = inv.astype(BF16)
-    low = (inv - high.astype(F32)).astype(BF16)
     inv_ref[:K, :] = high
-    inv_ref[K:, :] = low
+    inv_ref[K:, :] = (inv - high.astype(F32)).astype(BF16)
+
+
+def q_kernel(s_ref, inv_ref, q_ref):
     for k in range(4):
         a = s_ref[4 * k : 4 * k + 4].reshape(4 * TILE, K)
-        q_ref[k * 4 * TILE : (k + 1) * 4 * TILE, :] = (dot(a, high, 1, 1) + dot(a, low, 1, 1)).astype(BF16)
-
-
-def back_solve_kernel(meta_ref, b0_ref, b1_ref, b2_ref, b3_ref, inv_ref, z_hbm, z_ref, sem):
-    i = iota((EXTRA, 8 * EXTRA), 0)
-    e = iota((EXTRA, 8 * EXTRA), 1)
-    pick = jnp.where(e == (i % 8) * EXTRA + i // 8, 1.0, 0.0).astype(BF16)
+        rows = slice(k * 4 * TILE, (k + 1) * 4 * TILE)
+        q_ref[rows, :] = (dot(a, inv_ref[:K, :], 1, 1) + dot(a, inv_ref[K:, :], 1, 1)).astype(BF16)
+
+
+def solve_kernel(meta_ref, b0_ref, b1_ref, b2_ref, b3_ref, inv_ref, z_hbm, z_ref, sem):
+    def solve(a):
+        return dot(a, inv_ref[:K, :], 1, 1) + dot(a, inv_ref[K:, :], 1, 1)
+
+    refs = (b0_ref, b1_ref, b2_ref, b3_ref)
+    tails = jnp.concatenate([ref[:, ROWS:, :].reshape(8 * TAIL, K) for ref in refs], axis=0)
+    i = iota((2 * PARTS, PARTS * TAIL), 0)
+    e = iota((2 * PARTS, PARTS * TAIL), 1)
+    pick = jnp.where(e == (i % PARTS) * TAIL + i // PARTS, 1.0, 0.0).astype(BF16)
+    leads = dot(pick, tails, 1, 0)
+    lead = solve(leads[:PARTS].astype(BF16))
+    coef = leads[PARTS:, :TILE].T
     copies = []
-    for k, ref in enumerate((b0_ref, b1_ref, b2_ref, b3_ref)):
-        leads = dot(pick, ref[:, ROWS:, :].reshape(8 * EXTRA, K), 1, 0)
-        lead = leads[:8].astype(BF16)
-        lead = dot(lead, inv_ref[:K, :], 1, 1) + dot(lead, inv_ref[K:, :], 1, 1)
-        coef = leads[8:, :TILE].T
-        a = ref[:, :ROWS, :].reshape(8 * ROWS, K)
-        z = dot(a, inv_ref[:K, :], 1, 1) + dot(a, inv_ref[K:, :], 1, 1)
+    for k, ref in enumerate(refs):
+        z = solve(ref[:, :ROWS, :].reshape(8 * ROWS, K))
         for s in range(8):
+            m = 8 * k + s
             z_ref[k, s * ROWS : (s + 1) * ROWS, :] = (
-                z[s * ROWS : (s + 1) * ROWS] + coef[:ROWS, s : s + 1] * lead[s : s + 1, :]
+                z[s * ROWS : (s + 1) * ROWS] + coef[:ROWS, m : m + 1] * lead[m : m + 1, :]
             )
         at = pl.multiple_of(((meta_ref[2] - k) & 3) * 8 * ROWS, 8 * ROWS)
-        copy = pltpu.make_async_copy(z_ref.at[k], z_hbm.at[pl.ds(at, 8 * ROWS), :], sem.at[k])
-        copy.start()
-        copies.append(copy)
+        copies.append(pltpu.make_async_copy(z_ref.at[k], z_hbm.at[pl.ds(at, 8 * ROWS), :], sem.at[k]))
+        copies[-1].start()
     for copy in copies:
         copy.wait()
 
@@ -343,7 +358,7 @@
     swap = [(0, 1), (1, 0)]
     keep, send = pl.pallas_call(
         sketch_kernel,
-        out_shape=(shape(HALF, K), shape(HALF, K)),
+        out_shape=(shape(HALF, K), shape(HALF, K, dtype=BF16)),
         in_specs=[SMEM] + [HBM] * 2,
         out_specs=(VMEM, VMEM),
         scratch_shapes=[
@@ -353,32 +368,42 @@
             pltpu.SemaphoreType.DMA,
             pltpu.SemaphoreType.DMA((SLOTS // LOAD,)),
         ],
-        compiler_params=pltpu.CompilerParams(vmem_limit_bytes=51 * 1024 * 1024),
+        compiler_params=pltpu.CompilerParams(vmem_limit_bytes=52 * 1024 * 1024),
         name="sketch",
     )(meta, tiles, omega.reshape(CB, TILE, K))
 
     def turn(a, k, axis="y"):
         return lax.ppermute(a, axis, [(i, (i + k) % 4) for i in range(4)])
 
-    half = keep + lax.ppermute(send, "c", swap)
+    half = keep + lax.ppermute(send, "c", swap).astype(F32)
     quarters = half.reshape(4, PIECE, K)
     sent = [quarters[k].astype(BF16) for k in range(4)]
     sent[2], later = lax.optimization_barrier((sent[2], meta))
-    flipped, order = pl.pallas_call(
-        flip_kernel,
-        out_shape=(shape(SLOTS, TILE, TILE, dtype=BF16), shape(START + 8, dtype=jnp.int32)),
-        in_specs=[SMEM, VMEM],
-        out_specs=(VMEM, SMEM),
-        scratch_shapes=[pltpu.SMEM((8,), jnp.int32), pltpu.SMEM((SLOTS,), jnp.int32)],
-        compiler_params=LIMIT,
-        cost_estimate=cost(4),
-        name="flip",
-    )(later, tiles[0, 0])
+    order = pl.pallas_call(
+        order_kernel,
+        out_shape=shape(SOURCE + SLOTS, dtype=jnp.int32),
+        in_specs=[SMEM],
+        out_specs=SMEM,
+        scratch_shapes=[pltpu.SMEM((8,), jnp.int32)],
+        compiler_params=LIMIT,
+        cost_estimate=cost(3),
+        name="order",
+    )(later)
     shard = quarters[0]
     for k in (2, 1, 3):
         shard = shard + turn(sent[k], k).astype(F32)
-    shard, flipped = lax.optimization_barrier((shard.astype(BF16), flipped))
+    shard, order = lax.optimization_barrier((shard.astype(BF16), order))
+    flipped = pl.pallas_call(
+        flip_kernel,
+        out_shape=shape(SLOTS, TILE, TILE, dtype=BF16),
+        in_specs=[SMEM, VMEM],
+        out_specs=VMEM,
+        compiler_params=LIMIT,
+        cost_estimate=cost(3),
+        name="flip",
+    )(order, tiles[0, 0])
     mine = jnp.concatenate([shard] + [turn(shard, k) for k in (1, 2, 3)], axis=0)
+    mine, flipped = lax.optimization_barrier((mine, flipped))
     other = lax.ppermute(mine, "c", swap)
     half_gram = pl.pallas_call(
         gram_kernel,
@@ -412,7 +437,6 @@
             cost_estimate=cost(10 if first else 1),
             name=f"back{first}",
         )(order, flipped, slab)
-    backs = [backs[3]] + [turn(backs[k - 1], k, "x") for k in (1, 2, 3)]
     grams = pl.pallas_call(
         gram_sum_kernel,
         out_shape=shape(8, EXTRA, K, dtype=BF16),
@@ -421,6 +445,8 @@
         compiler_params=LIMIT,
         name="gram_sum",
     )(*grams)
+    grams, *backs[:3] = lax.optimization_barrier((grams, *backs[:3]))
+    backs = [backs[3]] + [turn(backs[k - 1], k, "x") for k in (1, 2, 3)]
     grams = lax.all_to_all(grams, "z", 0, 0, tiled=True)
     size = (ROWS + EXTRA, K)
     parts = pl.pallas_call(
@@ -433,7 +459,7 @@
     )(*backs, grams)
     spread, gram = pl.pallas_call(
         sum_kernel,
-        out_shape=(shape(8, *size, dtype=BF16), shape(8, EXTRA, K, dtype=BF16)),
+        out_shape=(shape(8, ROWS + TAIL, K, dtype=BF16), shape(8, EXTRA, K, dtype=BF16)),
         in_specs=[VMEM],
         out_specs=(VMEM, VMEM),
         compiler_params=LIMIT,
@@ -442,18 +468,36 @@
     extras = [gram] + [turn(gram, k, "x") for k in (1, 2, 3)]
     line = lax.all_to_all(spread, "z", 0, 0, tiled=True)
     bodies = [line] + [turn(line, k, "x") for k in (1, 2, 3)]
-    q, r, inv = pl.pallas_call(
-        factor_kernel,
-        out_shape=(shape(2 * HALF, K, dtype=BF16), shape(K, K), shape(2 * K, K, dtype=BF16)),
-        in_specs=[SMEM] + [VMEM] * 5,
-        out_specs=(VMEM,) * 3,
+    begun = pl.pallas_call(
+        first_kernel,
+        out_shape=shape(K, 2 * K),
+        in_specs=[SMEM] + [VMEM] * 4,
+        out_specs=VMEM,
+        compiler_params=LIMIT,
+        cost_estimate=cost(3 * FIRST),
+        name="first",
+    )(meta, *extras)
+    r, inv = pl.pallas_call(
+        rest_kernel,
+        out_shape=(shape(K, K), shape(2 * K, K, dtype=BF16)),
+        in_specs=[VMEM],
+        out_specs=(VMEM,) * 2,
         scratch_shapes=[pltpu.VMEM((K, 2 * K), F32)],
         compiler_params=LIMIT,
-        cost_estimate=cost(13),
-        name="factor",
-    )(meta, *extras, slab)
+        cost_estimate=cost(12 - 3 * FIRST),
+        name="rest",
+    )(begun)
+    q = pl.pallas_call(
+        q_kernel,
+        out_shape=shape(2 * HALF, K, dtype=BF16),
+        in_specs=[VMEM] * 2,
+        out_specs=VMEM,
+        compiler_params=LIMIT,
+        cost_estimate=cost(2),
+        name="q",
+    )(slab, inv)
     z = pl.pallas_call(
-        back_solve_kernel,
+        solve_kernel,
         out_shape=shape(CB * TILE, K),
         in_specs=[SMEM] + [VMEM] * 5,
         out_specs=HBM,

time: 127 us -> 115 us (0.906)
  the two profiles are of different devices: /device:TPU:2 before, /device:TPU:1 now
where the time goes in v5:
time: 115 us; the launch traced here: 113 us
  starting transfers between devices  40.6 us (35%)
  Pallas kernels  30.9 us (27%)
  waiting for transfers between devices  24.3 us (21%)
  blocking collectives  13.2 us (11%)
  local copies, waits for them, and re-layouts  2.38 us (2%)
  between operations  1.63 us (1%)
    ppermute x18, starting transfers between devices, turn(): return lax.ppermute(a, axis, [(i, (i + k) % 4) for i in range(4)])  23.6 us
    ppermute x18, waiting for transfers between devices, turn(): return lax.ppermute(a, axis, [(i, (i + k) % 4) for i in range(4)])  16.9 us
    all_to_all x1, blocking collectives, on_device(): lax.all_to_all(parts, 'z', 0, 0, tiled=True)  13.2 us
    all_to_all x1, starting transfers between devices, on_device(): grams = lax.all_to_all(grams, 'z', 0, 0, tiled=True)  8.78 us
    pallas_call x1, Pallas kernels, on_device(): pl.pallas_call(rest_kernel, out_shape=(shape(K, K), shape(2 * K, K, dtype...  7.76 us
    all_to_all x1, waiting for transfers between devices, on_device(): grams = lax.all_to_all(grams, 'z', 0, 0, tiled=True)  4.72 us
    pallas_call x1, Pallas kernels, on_device(): pl.pallas_call(sketch_kernel, out_shape=(shape(HALF, K), shape(HALF, K, d...  3.75 us
    all_to_all x1, starting transfers between devices, on_device(): line = lax.all_to_all(spread, 'z', 0, 0, tiled=True)  3.42 us
  transfers between devices with their start and end apart: 22, of which 13 were waited for; matrix products, arithmetic and copies ran while one was open for 0% of the time, Pallas kernels for 19%

profile of v5, /device:TPU:1, one launch (start us, length us, event | category | flops | bytes accessed | tf_op | source)
XLA Modules:
  0.0 113.3 jit_solution(13356445901931568150)
XLA Ops:
  1.3 0.8 concatenate.6.meta_ref
  2.0 3.8 %sketch.1 = (f32[1024,256]{1,0:T(8,128)S(1)}, bf16[1024,256]{1,0:T(8,128)(2,1)S(1)}) custom-call(s32[132]{0:T(256)S(1)} %concatenate.6.meta_ref, bf16[1,1,64,128,128]{4,3,2,1,0:T(8,128)(2,1)} %tiles_hbm.1, bf16[16,128,256]{2,1,0:T(8,128)(2,1)} %bitcast.10), custom_call_target="tpu_custom_call" | custom-call | tf_op jit(solution)/shard_map/sketch/pallas_call | solution.py:359
  5.8 3.3 %collective-permute-start = (bf16[1024,256]{1,0:T(8,128)(2,1)S(1)}, bf16[1024,256]{1,0:T(8,128)(2,1)S(1)}, u32[]{:S(2)}, u32[]{:S(2)}) collective-permute-start(bf16[1024,256]{1,0:T(8,128)(2,1)S(1)} %get-tuple-element.28), channel_id=1, source_target_pairs={{0,1},{1,0},{2,3},{3,2},{4,5},{5,4},{6,7},{7,6},{8,9},{9,8},{10,11... | collective-permute-start | bytes 1572872 | tf_op jit(solution)/shard_map/ppermute | solution.py:378
  9.1 1.5 %collective-permute-done = bf16[1024,256]{1,0:T(8,128)(2,1)S(1)} collective-permute-done((bf16[1024,256]{1,0:T(8,128)(2,1)S(1)}, bf16[1024,256]{1,0:T(8,128)(2,1)S(1)}, u32[]{:S(2)}, u32[]{:S(2)}) %collective-permute-start) | collective-permute-done | bytes 524320 | tf_op jit(solution)/shard_map/ppermute | solution.py:378
  10.7 0.1 fusion.3
  10.8 2.1 %collective-permute-start.1 = (bf16[256,256]{1,0:T(8,128)(2,1)S(1)}, bf16[256,256]{1,0:T(8,128)(2,1)S(1)}, u32[]{:S(2)}, u32[]{:S(2)}) collective-permute-start(bf16[256,256]{1,0:T(8,128)(2,1)S(1)} %get-tuple-element.29), channel_id=1, source_target_pairs={{0,4},{2,6},{4,0},{6,2},{1,5},{3,7},{5,1},{7,3},{8,12},{10,14},{12... | collective-permute-start | bytes 393224 | tf_op jit(solution)/shard_map/ppermute | solution.py:376
  13.0 1.1 collective-permute-start.3
  14.0 0.4 collective-permute-start.2
  14.4 3.3 %order.1.meta_ref = s32[204]{0:T(256)S(1)} custom-call(s32[132]{0:T(256)S(1)} %concatenate.6.meta_ref), custom_call_target="tpu_custom_call" | custom-call | flops 3000000000 | bytes 1048576 | tf_op jit(solution)/shard_map/order/pallas_call | solution.py:382
  17.8 0.0 collective-permute-done.1
  17.8 0.4 collective-permute-done.3
  18.2 1.9 %collective-permute-done.2 = bf16[256,256]{1,0:T(8,128)(2,1)S(1)} collective-permute-done((bf16[256,256]{1,0:T(8,128)(2,1)S(1)}, bf16[256,256]{1,0:T(8,128)(2,1)S(1)}, u32[]{:S(2)}, u32[]{:S(2)}) %collective-permute-start.2) | collective-permute-done | bytes 131104 | tf_op jit(solution)/shard_map/ppermute | solution.py:376
  20.1 0.1 fusion.2
  20.2 0.4 collective-permute-start.6
  20.6 2.4 %collective-permute-start.5 = (bf16[256,256]{1,0:T(8,128)(2,1)S(1)}, bf16[256,256]{1,0:T(8,128)(2,1)S(1)}, u32[]{:S(2)}, u32[]{:S(2)}) collective-permute-start(bf16[256,256]{1,0:T(8,128)(2,1)S(1)} %fusion.2), channel_id=1, source_target_pairs={{0,4},{2,6},{4,0},{6,2},{1,5},{3,7},{5,1},{7,3},{8,12},{10,14},{12... | collective-permute-start | bytes 393224 | tf_op jit(solution)/shard_map/ppermute | solution.py:376
  23.0 0.8 collective-permute-start.4
  23.7 2.0 %flip.1.tiles_ref = bf16[64,128,128]{2,1,0:T(8,128)(2,1)S(1)} custom-call(s32[204]{0:T(256)S(1)} %order.1.meta_ref, bf16[64,128,128]{2,1,0:T(8,128)(2,1)S(1)} %bitcast.9), custom_call_target="tpu_custom_call" | custom-call | flops 3000000000 | bytes 1048576 | tf_op jit(solution)/shard_map/flip/pallas_call | solution.py:396
  25.7 0.0 copy-start.1
  25.7 0.0 collective-permute-done.6
  25.7 0.2 collective-permute-done.5
  25.9 4.2 %collective-permute-done.4 = bf16[256,256]{1,0:T(8,128)(2,1)S(1)} collective-permute-done((bf16[256,256]{1,0:T(8,128)(2,1)S(1)}, bf16[256,256]{1,0:T(8,128)(2,1)S(1)}, u32[]{:S(2)}, u32[]{:S(2)}) %collective-permute-start.4) | collective-permute-done | bytes 131104 | tf_op jit(solution)/shard_map/ppermute | solution.py:376
  30.1 1.4 %collective-permute-start.7 = (bf16[1024,256]{1,0:T(8,128)(2,1)S(1)}, bf16[1024,256]{1,0:T(8,128)(2,1)S(1)}, u32[]{:S(2)}, u32[]{:S(2)}) collective-permute-start(bf16[1024,256]{1,0:T(8,128)(2,1)S(1)} %pad_maximum_fusion.mine_ref), channel_id=1, source_target_pairs={{0,1},{1,0},{2,3},{3,2},{4,5},{5,4},{6,7},{7,6},{8,9},{9,8},{10,11... | collective-permute-start | bytes 1572872 | tf_op jit(solution)/shard_map/ppermute | solution.py:407
  31.5 0.3 gram.1.gram_ref
  31.8 1.2 %collective-permute-done.7.other_ref = bf16[1024,256]{1,0:T(8,128)(2,1)S(1)} collective-permute-done((bf16[1024,256]{1,0:T(8,128)(2,1)S(1)}, bf16[1024,256]{1,0:T(8,128)(2,1)S(1)}, u32[]{:S(2)}, u32[]{:S(2)}) %collective-permute-start.7) | collective-permute-done | bytes 524320 | tf_op jit(solution)/shard_map/ppermute | solution.py:407
  33.0 1.4 %slab.1 = (bf16[16,128,256]{2,1,0:T(8,128)(2,1)S(1)}, bf16[8,16,256]{2,1,0:T(8,128)(2,1)S(1)}, bf16[8,16,256]{2,1,0:T(8,128)(2,1)S(1)}, bf16[8,16,256]{2,1,0:T(8,128)(2,1)S(1)}, bf16[8,16,256]{2,1,0:T(8,128)(2,1)S(1)}) custom-call(s32[132]{0:T(256)S(1)} %concatenate.6.meta_ref, bf16[1024,256]{1,0:T(8,128)(2,1)S(1)} %pad_maximum_fusion.mine_ref, ...), custom_call_target="tpu_custom_call" | custom-call | flops 1000000000 | bytes 1048576 | tf_op jit(solution)/shard_map/slab/pallas_call | solution.py:417
  34.4 1.5 %collective-permute-start.8 = (bf16[8,16,256]{2,1,0:T(8,128)(2,1)S(1)}, bf16[8,16,256]{2,1,0:T(8,128)(2,1)S(1)}, u32[]{:S(2)}, u32[]{:S(2)}) collective-permute-start(bf16[8,16,256]{2,1,0:T(8,128)(2,1)S(1)} %get-tuple-element.37), channel_id=1, source_target_pairs={{0,8},{8,16},{16,24},{24,0},{1,9},{9,17},{17,25},{25,1},{2,10},{10... | collective-permute-start | bytes 196616 | tf_op jit(solution)/shard_map/ppermute | solution.py:376
  36.0 3.7 %collective-permute-start.9 = (bf16[8,16,256]{2,1,0:T(8,128)(2,1)S(1)}, bf16[8,16,256]{2,1,0:T(8,128)(2,1)S(1)}, u32[]{:S(2)}, u32[]{:S(2)}) collective-permute-start(bf16[8,16,256]{2,1,0:T(8,128)(2,1)S(1)} %get-tuple-element.38), channel_id=1, source_target_pairs={{0,16},{8,24},{16,0},{24,8},{1,17},{9,25},{17,1},{25,9},{2,18},{10... | collective-permute-start | bytes 196616 | tf_op jit(solution)/shard_map/ppermute | solution.py:376
  39.7 0.0 collective-permute-start.10
  39.7 1.9 %back1.1 = (bf16[8,64,256]{2,1,0:T(8,128)(2,1)S(1)}, bf16[8,64,256]{2,1,0:T(8,128)(2,1)S(1)}, bf16[8,64,256]{2,1,0:T(8,128)(2,1)S(1)}) custom-call(s32[204]{0:T(256)S(1)} %order.1.meta_ref, bf16[64,128,128]{2,1,0:T(8,128)(2,1)S(1)} %flip.1.tiles_ref, bf16[16,128,256]{2,1,0:T(8,128)(2,1)S(1)} %get-tuple-element.34.s_ref), custom_call_target="tpu_custom_call" | custom-call | flops 10000000000 | bytes 1048576 | tf_op jit(solution)/shard_map/back1/pallas_call | solution.py:430
  41.7 0.0 collective-permute-done.8.b_ref
  41.7 1.0 collective-permute-done.9.c_ref
  42.7 0.5 collective-permute-done.10.d_ref
  43.1 0.7 gram_sum.1
  43.8 0.0 collective-permute-start.11
  43.8 3.3 %collective-permute-start.12 = (bf16[8,64,256]{2,1,0:T(8,128)(2,1)S(1)}, bf16[8,64,256]{2,1,0:T(8,128)(2,1)S(1)}, u32[]{:S(2)}, u32[]{:S(2)}) collective-permute-start(bf16[8,64,256]{2,1,0:T(8,128)(2,1)S(1)} %get-tuple-element.44), channel_id=1, source_target_pairs={{0,16},{8,24},{16,0},{24,8},{1,17},{9,25},{17,1},{25,9},{2,18},{10... | collective-permute-start | bytes 786440 | tf_op jit(solution)/shard_map/ppermute | solution.py:376
  47.1 0.0 collective-permute-start.13
  47.1 8.8 %all-to-all-start = ((bf16[8,16,256]{2,1,0:T(8,128)(2,1)}), bf16[8,16,256]{2,1,0:T(8,128)(2,1)S(1)}, u32[]{:S(2)}, u32[]{:S(2)}) async-start(bf16[8,16,256]{2,1,0:T(8,128)(2,1)} %gram_sum.1), calls=%async_computation | async-start | bytes 131072 | tf_op jit(solution)/shard_map/all_to_all | solution.py:450
  55.9 1.6 %copy-done.2 = bf16[64,128,128]{2,1,0:T(8,128)(2,1)S(1)} copy-done((bf16[64,128,128]{2,1,0:T(8,128)(2,1)S(1)}, bf16[64,128,128]{2,1,0:T(8,128)(2,1)}, u32[]{:S(2)}) %copy-start.2) | copy-done | bytes 2097176
  57.5 0.9 back0.1.a_ref
  58.4 4.7 %all-to-all-done.gram_ref = bf16[8,16,256]{2,1,0:T(8,128)(2,1)S(1)} async-done(((bf16[8,16,256]{2,1,0:T(8,128)(2,1)}), bf16[8,16,256]{2,1,0:T(8,128)(2,1)S(1)}, u32[]{:S(2)}, u32[]{:S(2)}) %all-to-all-start) | async-done | bytes 65568 | tf_op jit(solution)/shard_map/all_to_all | solution.py:450
  63.2 0.0 collective-permute-done.11.b_ref
  63.2 0.0 collective-permute-done.12.c_ref
  63.2 0.0 collective-permute-done.13.d_ref
  63.2 0.2 partial.1
  63.3 13.2 %all_to_all.15.in_ref = bf16[8,80,256]{2,1,0:T(8,128)(2,1)S(1)} all-to-all(bf16[8,80,256]{2,1,0:T(8,128)(2,1)S(1)} %partial.1), channel_id=1, replica_groups=mesh['z'=8,'x'=4,'y'=4,'c'=2] {'z'}, dimensions={0} | all-to-all | bytes 655360 | tf_op jit(solution)/shard_map/all_to_all | solution.py:467
  76.5 1.1 %total.1 = (bf16[8,72,256]{2,1,0:T(8,128)(2,1)}, bf16[8,16,256]{2,1,0:T(8,128)(2,1)S(1)}) custom-call(bf16[8,80,256]{2,1,0:T(8,128)(2,1)S(1)} %all_to_all.15.in_ref), custom_call_target="tpu_custom_call" | custom-call | tf_op jit(solution)/shard_map/total/pallas_call | solution.py:460
  77.7 3.4 %all-to-all-start.2 = ((bf16[8,72,256]{2,1,0:T(8,128)(2,1)}), bf16[8,72,256]{2,1,0:T(8,128)(2,1)S(1)}, u32[]{:S(2)}, u32[]{:S(2)}) async-start(bf16[8,72,256]{2,1,0:T(8,128)(2,1)} %get-tuple-element.50), calls=%async_computation.2 | async-start | bytes 589824 | tf_op jit(solution)/shard_map/all_to_all | solution.py:469
  81.1 4.9 %collective-permute-start.16 = (bf16[8,16,256]{2,1,0:T(8,128)(2,1)S(1)}, bf16[8,16,256]{2,1,0:T(8,128)(2,1)S(1)}, u32[]{:S(2)}, u32[]{:S(2)}) collective-permute-start(bf16[8,16,256]{2,1,0:T(8,128)(2,1)S(1)} %get-tuple-element.47.e0_ref), channel_id=1, source_target_pairs={{0,24},{8,0},{16,8},{24,16},{1,25},{9,1},{17,9},{25,17},{2,26},{10... | collective-permute-start | bytes 196616 | tf_op jit(solution)/shard_map/ppermute | solution.py:376
  86.0 0.0 collective-permute-start.15
  86.0 0.7 collective-permute-start.14
  86.7 0.7 collective-permute-done.16.e3_ref
  87.3 3.4 %collective-permute-done.15.e2_ref = bf16[8,16,256]{2,1,0:T(8,128)(2,1)S(1)} collective-permute-done((bf16[8,16,256]{2,1,0:T(8,128)(2,1)S(1)}, bf16[8,16,256]{2,1,0:T(8,128)(2,1)S(1)}, u32[]{:S(2)}, u32[]{:S(2)}) %collective-permute-start.15) | collective-permute-done | bytes 65568 | tf_op jit(solution)/shard_map/ppermute | solution.py:376
  90.7 0.3 collective-permute-done.14.e1_ref
  91.0 3.3 %first.1.begun_ref = f32[256,512]{1,0:T(8,128)S(1)} custom-call(s32[132]{0:T(256)S(1)} %concatenate.6.meta_ref, bf16[8,16,256]{2,1,0:T(8,128)(2,1)S(1)} %get-tuple-element.47.e0_ref, bf16[8,16,256]{2,1,0:T(8,128)(2,1)S(1)} %collective-permute-done.14.e1_ref, bf16[8,16,256]{2,1,0:T(8,128)(2,1)S(1)} %collective-permute-done.15.e2_ref, ...), custom_call_target="tpu_custom_call" | custom-call | flops 3000000000 | bytes 1048576 | tf_op jit(solution)/shard_map/first/pallas_call | solution.py:471
  94.4 0.0 all-to-all-done.2.b0_ref
  94.4 1.2 %collective-permute-start.19 = (bf16[8,72,256]{2,1,0:T(8,128)(2,1)S(1)}, bf16[8,72,256]{2,1,0:T(8,128)(2,1)S(1)}, u32[]{:S(2)}, u32[]{:S(2)}) collective-permute-start(bf16[8,72,256]{2,1,0:T(8,128)(2,1)S(1)} %all-to-all-done.2.b0_ref), channel_id=1, source_target_pairs={{0,24},{8,0},{16,8},{24,16},{1,25},{9,1},{17,9},{25,17},{2,26},{10... | collective-permute-start | bytes 884744 | tf_op jit(solution)/shard_map/ppermute | solution.py:376
  95.6 0.3 collective-permute-start.18
  95.9 0.8 collective-permute-start.17
  96.7 7.8 %rest.1 = (f32[256,256]{1,0:T(8,128)}, bf16[512,256]{1,0:T(8,128)(2,1)S(1)}) custom-call(f32[256,512]{1,0:T(8,128)S(1)} %first.1.begun_ref), custom_call_target="tpu_custom_call" | custom-call | flops 8999999488 | bytes 1048576 | tf_op jit(solution)/shard_map/rest/pallas_call | solution.py:480
  104.5 1.7 %q.1 = bf16[2048,256]{1,0:T(8,128)(2,1)} custom-call(bf16[16,128,256]{2,1,0:T(8,128)(2,1)S(1)} %get-tuple-element.34.s_ref, bf16[512,256]{1,0:T(8,128)(2,1)S(1)} %get-tuple-element.48.inv_ref), custom_call_target="tpu_custom_call" | custom-call | flops 2000000000 | bytes 1048576 | tf_op jit(solution)/shard_map/q/pallas_call | solution.py:490
  106.2 0.0 collective-permute-done.19.b3_ref
  106.2 0.0 collective-permute-done.18.b2_ref
  106.2 4.4 %collective-permute-done.17.b1_ref = bf16[8,72,256]{2,1,0:T(8,128)(2,1)S(1)} collective-permute-done((bf16[8,72,256]{2,1,0:T(8,128)(2,1)S(1)}, bf16[8,72,256]{2,1,0:T(8,128)(2,1)S(1)}, u32[]{:S(2)}, u32[]{:S(2)}) %collective-permute-start.17) | collective-permute-done | bytes 294944 | tf_op jit(solution)/shard_map/ppermute | solution.py:376
  110.6 2.5 %z.1 = f32[2048,256]{1,0:T(8,128)} custom-call(s32[132]{0:T(256)S(1)} %concatenate.6.meta_ref, bf16[8,72,256]{2,1,0:T(8,128)(2,1)S(1)} %all-to-all-done.2.b0_ref, bf16[8,72,256]{2,1,0:T(8,128)(2,1)S(1)} %collective-permute-done.17.b1_ref, bf16[8,72,256]{2,1,0:T(8,128)(2,1)S(1)} %collective-permute-done.18.b2_ref, ...), custom_call_target="tpu_custom_call" | custom-call | tf_op jit(solution)/shard_map/z/pallas_call | solution.py:499
  (6 shorter events, 0.1 us)
Async XLA Ops:
  5.8 4.9 %collective-permute-start = (bf16[1024,256]{1,0:T(8,128)(2,1)S(1)}, bf16[1024,256]{1,0:T(8,128)(2,1)S(1)}, u32[]{:S(2)}, u32[]{:S(2)}) collective-permute-start(bf16[1024,256]{1,0:T(8,128)(2,1)S(1)} %get-tuple-element.28), channel_id=1, source_target_pairs={{0,1},{1,0},{2,3},{3,2},{4,5},{5,4},{6,7},{7,6},{8,9},{9,8},{10,11... | collective-permute-start | bytes 1572872 | tf_op jit(solution)/shard_map/ppermute | solution.py:378
  10.8 6.9 %collective-permute-start.1 = (bf16[256,256]{1,0:T(8,128)(2,1)S(1)}, bf16[256,256]{1,0:T(8,128)(2,1)S(1)}, u32[]{:S(2)}, u32[]{:S(2)}) collective-permute-start(bf16[256,256]{1,0:T(8,128)(2,1)S(1)} %get-tuple-element.29), channel_id=1, source_target_pairs={{0,4},{2,6},{4,0},{6,2},{1,5},{3,7},{5,1},{7,3},{8,12},{10,14},{12... | collective-permute-start | bytes 393224 | tf_op jit(solution)/shard_map/ppermute | solution.py:376
  13.0 5.2 %collective-permute-start.3 = (bf16[256,256]{1,0:T(8,128)(2,1)S(1)}, bf16[256,256]{1,0:T(8,128)(2,1)S(1)}, u32[]{:S(2)}, u32[]{:S(2)}) collective-permute-start(bf16[256,256]{1,0:T(8,128)(2,1)S(1)} %get-tuple-element.54), channel_id=1, source_target_pairs={{0,6},{2,0},{4,2},{6,4},{1,7},{3,1},{5,3},{7,5},{8,14},{10,8},{12,... | collective-permute-start | bytes 393224 | tf_op jit(solution)/shard_map/ppermute | solution.py:376
  14.0 9.7 %copy-start = (bf16[1,1,64,128,128]{4,3,2,1,0:T(8,128)(2,1)S(1)}, bf16[1,1,64,128,128]{4,3,2,1,0:T(8,128)(2,1)}, u32[]{:S(2)}) copy-start(bf16[1,1,64,128,128]{4,3,2,1,0:T(8,128)(2,1)} %tiles_hbm.1) | copy-start | bytes 6291460
  14.0 6.0 %collective-permute-start.2 = (bf16[256,256]{1,0:T(8,128)(2,1)S(1)}, bf16[256,256]{1,0:T(8,128)(2,1)S(1)}, u32[]{:S(2)}, u32[]{:S(2)}) collective-permute-start(bf16[256,256]{1,0:T(8,128)(2,1)S(1)} %get-tuple-element.55), channel_id=1, source_target_pairs={{0,2},{2,4},{4,6},{6,0},{1,3},{3,5},{5,7},{7,1},{8,10},{10,12},{12... | collective-permute-start | bytes 393224 | tf_op jit(solution)/shard_map/ppermute | solution.py:376
  20.2 5.6 %collective-permute-start.6 = (bf16[256,256]{1,0:T(8,128)(2,1)S(1)}, bf16[256,256]{1,0:T(8,128)(2,1)S(1)}, u32[]{:S(2)}, u32[]{:S(2)}) collective-permute-start(bf16[256,256]{1,0:T(8,128)(2,1)S(1)} %fusion.2), channel_id=1, source_target_pairs={{0,6},{2,0},{4,2},{6,4},{1,7},{3,1},{5,3},{7,5},{8,14},{10,8},{12,... | collective-permute-start | bytes 393224 | tf_op jit(solution)/shard_map/ppermute | solution.py:376
  20.6 5.3 %collective-permute-start.5 = (bf16[256,256]{1,0:T(8,128)(2,1)S(1)}, bf16[256,256]{1,0:T(8,128)(2,1)S(1)}, u32[]{:S(2)}, u32[]{:S(2)}) collective-permute-start(bf16[256,256]{1,0:T(8,128)(2,1)S(1)} %fusion.2), channel_id=1, source_target_pairs={{0,4},{2,6},{4,0},{6,2},{1,5},{3,7},{5,1},{7,3},{8,12},{10,14},{12... | collective-permute-start | bytes 393224 | tf_op jit(solution)/shard_map/ppermute | solution.py:376
  23.0 7.1 %collective-permute-start.4 = (bf16[256,256]{1,0:T(8,128)(2,1)S(1)}, bf16[256,256]{1,0:T(8,128)(2,1)S(1)}, u32[]{:S(2)}, u32[]{:S(2)}) collective-permute-start(bf16[256,256]{1,0:T(8,128)(2,1)S(1)} %fusion.2), channel_id=1, source_target_pairs={{0,2},{2,4},{4,6},{6,0},{1,3},{3,5},{5,7},{7,1},{8,10},{10,12},{12... | collective-permute-start | bytes 393224 | tf_op jit(solution)/shard_map/ppermute | solution.py:376
  25.7 14.0 %copy-start.1 = (bf16[64,128,128]{2,1,0:T(8,128)(2,1)}, bf16[64,128,128]{2,1,0:T(8,128)(2,1)S(1)}, u32[]{:S(2)}) copy-start(bf16[64,128,128]{2,1,0:T(8,128)(2,1)S(1)} %flip.1.tiles_ref) | copy-start | bytes 6291460
  30.1 3.0 %collective-permute-start.7 = (bf16[1024,256]{1,0:T(8,128)(2,1)S(1)}, bf16[1024,256]{1,0:T(8,128)(2,1)S(1)}, u32[]{:S(2)}, u32[]{:S(2)}) collective-permute-start(bf16[1024,256]{1,0:T(8,128)(2,1)S(1)} %pad_maximum_fusion.mine_ref), channel_id=1, source_target_pairs={{0,1},{1,0},{2,3},{3,2},{4,5},{5,4},{6,7},{7,6},{8,9},{9,8},{10,11... | collective-permute-start | bytes 1572872 | tf_op jit(solution)/shard_map/ppermute | solution.py:407
  34.4 7.2 %collective-permute-start.8 = (bf16[8,16,256]{2,1,0:T(8,128)(2,1)S(1)}, bf16[8,16,256]{2,1,0:T(8,128)(2,1)S(1)}, u32[]{:S(2)}, u32[]{:S(2)}) collective-permute-start(bf16[8,16,256]{2,1,0:T(8,128)(2,1)S(1)} %get-tuple-element.37), channel_id=1, source_target_pairs={{0,8},{8,16},{16,24},{24,0},{1,9},{9,17},{17,25},{25,1},{2,10},{10... | collective-permute-start | bytes 196616 | tf_op jit(solution)/shard_map/ppermute | solution.py:376
  36.0 6.7 %collective-permute-start.9 = (bf16[8,16,256]{2,1,0:T(8,128)(2,1)S(1)}, bf16[8,16,256]{2,1,0:T(8,128)(2,1)S(1)}, u32[]{:S(2)}, u32[]{:S(2)}) collective-permute-start(bf16[8,16,256]{2,1,0:T(8,128)(2,1)S(1)} %get-tuple-element.38), channel_id=1, source_target_pairs={{0,16},{8,24},{16,0},{24,8},{1,17},{9,25},{17,1},{25,9},{2,18},{10... | collective-permute-start | bytes 196616 | tf_op jit(solution)/shard_map/ppermute | solution.py:376
  39.7 3.4 %collective-permute-start.10 = (bf16[8,16,256]{2,1,0:T(8,128)(2,1)S(1)}, bf16[8,16,256]{2,1,0:T(8,128)(2,1)S(1)}, u32[]{:S(2)}, u32[]{:S(2)}) collective-permute-start(bf16[8,16,256]{2,1,0:T(8,128)(2,1)S(1)} %get-tuple-element.39), channel_id=1, source_target_pairs={{0,24},{8,0},{16,8},{24,16},{1,25},{9,1},{17,9},{25,17},{2,26},{10... | collective-permute-start | bytes 196616 | tf_op jit(solution)/shard_map/ppermute | solution.py:376
  43.8 19.3 %collective-permute-start.11 = (bf16[8,64,256]{2,1,0:T(8,128)(2,1)S(1)}, bf16[8,64,256]{2,1,0:T(8,128)(2,1)S(1)}, u32[]{:S(2)}, u32[]{:S(2)}) collective-permute-start(bf16[8,64,256]{2,1,0:T(8,128)(2,1)S(1)} %get-tuple-element.43), channel_id=1, source_target_pairs={{0,8},{8,16},{16,24},{24,0},{1,9},{9,17},{17,25},{25,1},{2,10},{10... | collective-permute-start | bytes 786440 | tf_op jit(solution)/shard_map/ppermute | solution.py:376
  43.8 19.3 %collective-permute-start.12 = (bf16[8,64,256]{2,1,0:T(8,128)(2,1)S(1)}, bf16[8,64,256]{2,1,0:T(8,128)(2,1)S(1)}, u32[]{:S(2)}, u32[]{:S(2)}) collective-permute-start(bf16[8,64,256]{2,1,0:T(8,128)(2,1)S(1)} %get-tuple-element.44), channel_id=1, source_target_pairs={{0,16},{8,24},{16,0},{24,8},{1,17},{9,25},{17,1},{25,9},{2,18},{10... | collective-permute-start | bytes 786440 | tf_op jit(solution)/shard_map/ppermute | solution.py:376
  47.1 16.0 %collective-permute-start.13 = (bf16[8,64,256]{2,1,0:T(8,128)(2,1)S(1)}, bf16[8,64,256]{2,1,0:T(8,128)(2,1)S(1)}, u32[]{:S(2)}, u32[]{:S(2)}) collective-permute-start(bf16[8,64,256]{2,1,0:T(8,128)(2,1)S(1)} %get-tuple-element.45), channel_id=1, source_target_pairs={{0,24},{8,0},{16,8},{24,16},{1,25},{9,1},{17,9},{25,17},{2,26},{10... | collective-permute-start | bytes 786440 | tf_op jit(solution)/shard_map/ppermute | solution.py:376
  47.1 16.0 %all-to-all-start = ((bf16[8,16,256]{2,1,0:T(8,128)(2,1)}), bf16[8,16,256]{2,1,0:T(8,128)(2,1)S(1)}, u32[]{:S(2)}, u32[]{:S(2)}) async-start(bf16[8,16,256]{2,1,0:T(8,128)(2,1)} %gram_sum.1), calls=%async_computation | async-start | bytes 131072 | tf_op jit(solution)/shard_map/all_to_all | solution.py:450
  55.9 1.6 %copy-start.2 = (bf16[64,128,128]{2,1,0:T(8,128)(2,1)S(1)}, bf16[64,128,128]{2,1,0:T(8,128)(2,1)}, u32[]{:S(2)}) copy-start(bf16[64,128,128]{2,1,0:T(8,128)(2,1)} %copy-done.1) | copy-start | bytes 6291460
  77.7 16.7 %all-to-all-start.2 = ((bf16[8,72,256]{2,1,0:T(8,128)(2,1)}), bf16[8,72,256]{2,1,0:T(8,128)(2,1)S(1)}, u32[]{:S(2)}, u32[]{:S(2)}) async-start(bf16[8,72,256]{2,1,0:T(8,128)(2,1)} %get-tuple-element.50), calls=%async_computation.2 | async-start | bytes 589824 | tf_op jit(solution)/shard_map/all_to_all | solution.py:469
  81.1 6.2 %collective-permute-start.16 = (bf16[8,16,256]{2,1,0:T(8,128)(2,1)S(1)}, bf16[8,16,256]{2,1,0:T(8,128)(2,1)S(1)}, u32[]{:S(2)}, u32[]{:S(2)}) collective-permute-start(bf16[8,16,256]{2,1,0:T(8,128)(2,1)S(1)} %get-tuple-element.47.e0_ref), channel_id=1, source_target_pairs={{0,24},{8,0},{16,8},{24,16},{1,25},{9,1},{17,9},{25,17},{2,26},{10... | collective-permute-start | bytes 196616 | tf_op jit(solution)/shard_map/ppermute | solution.py:376
  86.0 4.7 %collective-permute-start.15 = (bf16[8,16,256]{2,1,0:T(8,128)(2,1)S(1)}, bf16[8,16,256]{2,1,0:T(8,128)(2,1)S(1)}, u32[]{:S(2)}, u32[]{:S(2)}) collective-permute-start(bf16[8,16,256]{2,1,0:T(8,128)(2,1)S(1)} %get-tuple-element.47.e0_ref), channel_id=1, source_target_pairs={{0,16},{8,24},{16,0},{24,8},{1,17},{9,25},{17,1},{25,9},{2,18},{10... | collective-permute-start | bytes 196616 | tf_op jit(solution)/shard_map/ppermute | solution.py:376
  86.0 5.0 %collective-permute-start.14 = (bf16[8,16,256]{2,1,0:T(8,128)(2,1)S(1)}, bf16[8,16,256]{2,1,0:T(8,128)(2,1)S(1)}, u32[]{:S(2)}, u32[]{:S(2)}) collective-permute-start(bf16[8,16,256]{2,1,0:T(8,128)(2,1)S(1)} %get-tuple-element.47.e0_ref), channel_id=1, source_target_pairs={{0,8},{8,16},{16,24},{24,0},{1,9},{9,17},{17,25},{25,1},{2,10},{10... | collective-permute-start | bytes 196616 | tf_op jit(solution)/shard_map/ppermute | solution.py:376
  94.4 11.8 %collective-permute-start.19 = (bf16[8,72,256]{2,1,0:T(8,128)(2,1)S(1)}, bf16[8,72,256]{2,1,0:T(8,128)(2,1)S(1)}, u32[]{:S(2)}, u32[]{:S(2)}) collective-permute-start(bf16[8,72,256]{2,1,0:T(8,128)(2,1)S(1)} %all-to-all-done.2.b0_ref), channel_id=1, source_target_pairs={{0,24},{8,0},{16,8},{24,16},{1,25},{9,1},{17,9},{25,17},{2,26},{10... | collective-permute-start | bytes 884744 | tf_op jit(solution)/shard_map/ppermute | solution.py:376
  95.6 10.6 %collective-permute-start.18 = (bf16[8,72,256]{2,1,0:T(8,128)(2,1)S(1)}, bf16[8,72,256]{2,1,0:T(8,128)(2,1)S(1)}, u32[]{:S(2)}, u32[]{:S(2)}) collective-permute-start(bf16[8,72,256]{2,1,0:T(8,128)(2,1)S(1)} %all-to-all-done.2.b0_ref), channel_id=1, source_target_pairs={{0,16},{8,24},{16,0},{24,8},{1,17},{9,25},{17,1},{25,9},{2,18},{10... | collective-permute-start | bytes 884744 | tf_op jit(solution)/shard_map/ppermute | solution.py:376
  95.9 14.7 %collective-permute-start.17 = (bf16[8,72,256]{2,1,0:T(8,128)(2,1)S(1)}, bf16[8,72,256]{2,1,0:T(8,128)(2,1)S(1)}, u32[]{:S(2)}, u32[]{:S(2)}) collective-permute-start(bf16[8,72,256]{2,1,0:T(8,128)(2,1)S(1)} %all-to-all-done.2.b0_ref), channel_id=1, source_target_pairs={{0,8},{8,16},{16,24},{24,0},{1,9},{9,17},{17,25},{25,1},{2,10},{10... | collective-permute-start | bytes 884744 | tf_op jit(solution)/shard_map/ppermute | solution.py:376

commit v6 on v5

--- a/solution.py
+++ b/solution.py
@@ -127,7 +127,12 @@
     out_ref[...] = dot(mine_ref[...], mine_ref[...], 0, 0)
 
 
-def slab_kernel(meta_ref, mine_ref, other_ref, gram_ref, s_ref, g0_ref, g1_ref, g2_ref, g3_ref):
+def place(chunk, x):
+    far = chunk ^ x
+    return jnp.where(far == 3, 2, jnp.where(far == 2, 3, far))
+
+
+def slab_kernel(meta_ref, mine_ref, other_ref, gram_ref, s_ref, keep_ref, give_ref):
     core, chip, x = meta_ref[0], meta_ref[1], meta_ref[2]
     for k in range(4):
         at = ((chip - k) & 3) * 2
@@ -143,12 +148,13 @@
     e = iota((PARTS * EXTRA, 192), 0)
     p = iota((PARTS * EXTRA, 192), 1)
     slot = p // 6
-    first = (((slot // 8 - x) & 3) * 8 + slot % 8) * EXTRA + p % 6
+    first = (place(slot // 8, x) * 8 + slot % 8) * EXTRA + p % 6
     extra = dot(jnp.where(e == first, 1.0, 0.0).astype(BF16), high, 1, 0) + dot(
         jnp.where(e == first + 6, 1.0, 0.0).astype(BF16), rest, 1, 0
     )
-    for k, ref in enumerate((g0_ref, g1_ref, g2_ref, g3_ref)):
-        ref[...] = extra[k * 8 * EXTRA : (k + 1) * 8 * EXTRA].reshape(8, EXTRA, K).astype(BF16)
+    extra = extra.reshape(PARTS, EXTRA, K).astype(BF16)
+    keep_ref[...] = extra[: PARTS // 2]
+    give_ref[...] = extra[PARTS // 2 :]
 
 
 def back_kernel(first, last, meta_ref, tiles_ref, s_ref, *refs):
@@ -180,11 +186,16 @@
     return jnp.where(row < 6, high, jnp.where(row < 12, low, 0.0))
 
 
-def gram_sum_kernel(a_ref, b_ref, c_ref, d_ref, out_ref):
-    total = jnp.zeros((8 * EXTRA, K), F32)
-    for ref in (a_ref, b_ref, c_ref, d_ref):
-        total = total + ref[...].reshape(8 * EXTRA, K).astype(F32)
-    out_ref[...] = resplit(total).reshape(8, EXTRA, K).astype(BF16)
+def gram_pair_kernel(keep_ref, got_ref, mine_ref, pass_ref):
+    total = keep_ref[...].astype(F32) + got_ref[...].astype(F32)
+    total = resplit(total.reshape(16 * EXTRA, K)).reshape(16, EXTRA, K).astype(BF16)
+    mine_ref[...] = total[:8]
+    pass_ref[...] = total[8:]
+
+
+def gram_sum_kernel(mine_ref, got_ref, out_ref):
+    total = mine_ref[...].astype(F32) + got_ref[...].astype(F32)
+    out_ref[...] = resplit(total.reshape(8 * EXTRA, K)).reshape(8, EXTRA, K).astype(BF16)
 
 
 def partial_kernel(a_ref, b_ref, c_ref, d_ref, gram_ref, out_ref):
@@ -281,12 +292,12 @@
                 work[at + NB :, lo:hi] -= dot(down, work[at : at + NB, lo:hi], 1, 0, lax.Precision.HIGHEST)
 
 
-def first_kernel(meta_ref, e0_ref, e1_ref, e2_ref, e3_ref, work):
-    extra = jnp.concatenate([e[...].reshape(8 * EXTRA, K) for e in (e0_ref, e1_ref, e2_ref, e3_ref)], axis=0)
+def first_kernel(meta_ref, e0_ref, e1_ref, e2_ref, work):
+    extra = jnp.concatenate([e[...].reshape(-1, K) for e in (e0_ref, e1_ref, e2_ref)], axis=0)
     p = iota((192, PARTS * EXTRA), 0)
     e = iota((192, PARTS * EXTRA), 1)
     slot = p // 6
-    first = (((meta_ref[2] - slot // 8) & 3) * 8 + slot % 8) * EXTRA + p % 6
+    first = (place(slot // 8, meta_ref[2]) * 8 + slot % 8) * EXTRA + p % 6
     pick = jnp.where((e == first) | (e == first + 6), 1.0, 0.0).astype(BF16)
     packed = dot(pick, extra, 1, 0)
     work[: K // 2, :K] = packed[: K // 2]
@@ -414,16 +425,20 @@
         cost_estimate=cost(1),
         name="gram",
     )(mine)
-    slab, *grams = pl.pallas_call(
+    slab, keep, give = pl.pallas_call(
         slab_kernel,
-        out_shape=(shape(RB, TILE, K, dtype=BF16),) + (shape(8, EXTRA, K, dtype=BF16),) * 4,
+        out_shape=(shape(RB, TILE, K, dtype=BF16),) + (shape(16, EXTRA, K, dtype=BF16),) * 2,
         in_specs=[SMEM] + [VMEM] * 3,
-        out_specs=(VMEM,) * 5,
+        out_specs=(VMEM,) * 3,
         compiler_params=LIMIT,
         cost_estimate=cost(1),
         name="slab",
     )(meta, mine, other, half_gram)
-    grams = [grams[0]] + [turn(grams[k], k, "x") for k in (1, 2, 3)]
+
+    def mirror(a, bits):
+        return lax.ppermute(a, "x", [(i, i ^ bits) for i in range(4)])
+
+    got = mirror(give, 3)
     backs = []
     for first, last in ((1, 3), (0, 0)):
         count = last - first + 1
@@ -437,14 +452,25 @@
             cost_estimate=cost(10 if first else 1),
             name=f"back{first}",
         )(order, flipped, slab)
+    got, *backs[:3] = lax.optimization_barrier((got, *backs[:3]))
+    own, away = pl.pallas_call(
+        gram_pair_kernel,
+        out_shape=(shape(8, EXTRA, K, dtype=BF16),) * 2,
+        in_specs=[VMEM] * 2,
+        out_specs=(VMEM,) * 2,
+        compiler_params=LIMIT,
+        name="gram_pair",
+    )(keep, got)
+    away = mirror(away, 1)
+    away, backs[3] = lax.optimization_barrier((away, backs[3]))
     grams = pl.pallas_call(
         gram_sum_kernel,
         out_shape=shape(8, EXTRA, K, dtype=BF16),
-        in_specs=[VMEM] * 4,
+        in_specs=[VMEM] * 2,
         out_specs=VMEM,
         compiler_params=LIMIT,
         name="gram_sum",
-    )(*grams)
+    )(own, away)
     grams, *backs[:3] = lax.optimization_barrier((grams, *backs[:3]))
     backs = [backs[3]] + [turn(backs[k - 1], k, "x") for k in (1, 2, 3)]
     grams = lax.all_to_all(grams, "z", 0, 0, tiled=True)
@@ -465,13 +491,14 @@
         compiler_params=LIMIT,
         name="total",
     )(lax.all_to_all(parts, "z", 0, 0, tiled=True))
-    extras = [gram] + [turn(gram, k, "x") for k in (1, 2, 3)]
+    near = mirror(gram, 1)
+    extras = [gram, near, mirror(jnp.concatenate([gram, near], axis=0), 3)]
     line = lax.all_to_all(spread, "z", 0, 0, tiled=True)
     bodies = [line] + [turn(line, k, "x") for k in (1, 2, 3)]
     begun = pl.pallas_call(
         first_kernel,
         out_shape=shape(K, 2 * K),
-        in_specs=[SMEM] + [VMEM] * 4,
+        in_specs=[SMEM] + [VMEM] * 3,
         out_specs=VMEM,
         compiler_params=LIMIT,
         cost_estimate=cost(3 * FIRST),

time: 115 us -> 114 us (level); the launches traced: 113 us -> 114 us
  blocking collectives: 13.2 us -> 28.1 us
  starting transfers between devices: 40.6 us -> 27.9 us
  local copies, waits for them, and re-layouts: 2.38 us -> 0.78 us
    all_to_all x0 -> x1, blocking collectives: none -> 15 us  [on_device(): grams = lax.all_to_all(grams, 'z', 0, 0, tiled=True)]
    all_to_all x1 -> x0, starting transfers between devices: 8.78 us -> none  [on_device(): grams = lax.all_to_all(grams, 'z', 0, 0, tiled=True)]
    ppermute x0 -> x4, waiting for transfers between devices: none -> 8.14 us  [mirror(): return lax.ppermute(a, 'x', [(i, i ^ bits) for i in range(4)])]
    ppermute x18 -> x12, starting transfers between devices: 23.6 us -> 15.6 us  [turn(): return lax.ppermute(a, axis, [(i, (i + k) % 4) for i in range(4)])]
    ppermute x0 -> x4, starting transfers between devices: none -> 5.42 us  [mirror(): return lax.ppermute(a, 'x', [(i, i ^ bits) for i in range(4)])]
    all_to_all x1 -> x0, waiting for transfers between devices: 4.72 us -> none  [on_device(): grams = lax.all_to_all(grams, 'z', 0, 0, tiled=True)]
    ppermute x18 -> x12, waiting for transfers between devices: 16.9 us -> 12.4 us  [turn(): return lax.ppermute(a, axis, [(i, (i + k) % 4) for i in range(4)])]
    unnamed x6 -> x2, local copies, waits for them, and re-layouts: 1.6 us -> 0.01 us
  transfers between devices with their start and end apart: 22 -> 19, of which waited for: 13 -> 11; matrix products, arithmetic and copies ran while one was open for 0% -> 0% of each run, Pallas kernels for 19% -> 19%
where the time goes in v6:
time: 114 us
  Pallas kernels  30.4 us (27%)
  blocking collectives  28.1 us (25%)
  starting transfers between devices  27.9 us (24%)
  waiting for transfers between devices  24.4 us (21%)
  between operations  1.61 us (1%)
    ppermute x12, starting transfers between devices, turn(): return lax.ppermute(a, axis, [(i, (i + k) % 4) for i in range(4)])  15.6 us
    all_to_all x1, blocking collectives, on_device(): grams = lax.all_to_all(grams, 'z', 0, 0, tiled=True)  15 us
    all_to_all x1, blocking collectives, on_device(): lax.all_to_all(parts, 'z', 0, 0, tiled=True)  13.2 us
    ppermute x12, waiting for transfers between devices, turn(): return lax.ppermute(a, axis, [(i, (i + k) % 4) for i in range(4)])  12.4 us
    ppermute x4, waiting for transfers between devices, mirror(): return lax.ppermute(a, 'x', [(i, i ^ bits) for i in range(4)])  8.14 us
    pallas_call x1, Pallas kernels, on_device(): pl.pallas_call(rest_kernel, out_shape=(shape(K, K), shape(2 * K, K, dtype...  7.76 us
    ppermute x4, starting transfers between devices, mirror(): return lax.ppermute(a, 'x', [(i, i ^ bits) for i in range(4)])  5.42 us
    pallas_call x1, Pallas kernels, on_device(): pl.pallas_call(sketch_kernel, out_shape=(shape(HALF, K), shape(HALF, K, d...  3.75 us
  transfers between devices with their start and end apart: 19, of which 11 were waited for; matrix products, arithmetic and copies ran while one was open for 0% of the time, Pallas kernels for 19%

profile of v6, /device:TPU:1, one launch (start us, length us, event | category | flops | bytes accessed | tf_op | source)
XLA Modules:
  0.0 113.5 jit_solution(16284349986382150050)
XLA Ops:
  1.3 0.8 concatenate.9.meta_ref
  2.0 3.8 %sketch.1 = (f32[1024,256]{1,0:T(8,128)S(1)}, bf16[1024,256]{1,0:T(8,128)(2,1)S(1)}) custom-call(s32[132]{0:T(256)S(1)} %concatenate.9.meta_ref, bf16[1,1,64,128,128]{4,3,2,1,0:T(8,128)(2,1)} %tiles_hbm.1, bf16[16,128,256]{2,1,0:T(8,128)(2,1)} %bitcast.10), custom_call_target="tpu_custom_call" | custom-call | tf_op jit(solution)/shard_map/sketch/pallas_call | solution.py:370
  5.8 2.7 %collective-permute-start = (bf16[1024,256]{1,0:T(8,128)(2,1)S(1)}, bf16[1024,256]{1,0:T(8,128)(2,1)S(1)}, u32[]{:S(2)}, u32[]{:S(2)}) collective-permute-start(bf16[1024,256]{1,0:T(8,128)(2,1)S(1)} %get-tuple-element.34), channel_id=1, source_target_pairs={{0,1},{1,0},{2,3},{3,2},{4,5},{5,4},{6,7},{7,6},{8,9},{9,8},{10,11... | collective-permute-start | bytes 1572872 | tf_op jit(solution)/shard_map/ppermute | solution.py:389
  8.5 1.5 %collective-permute-done = bf16[1024,256]{1,0:T(8,128)(2,1)S(1)} collective-permute-done((bf16[1024,256]{1,0:T(8,128)(2,1)S(1)}, bf16[1024,256]{1,0:T(8,128)(2,1)S(1)}, u32[]{:S(2)}, u32[]{:S(2)}) %collective-permute-start) | collective-permute-done | bytes 524320 | tf_op jit(solution)/shard_map/ppermute | solution.py:389
  10.1 0.2 fusion.3
  10.3 1.9 %collective-permute-start.1 = (bf16[256,256]{1,0:T(8,128)(2,1)S(1)}, bf16[256,256]{1,0:T(8,128)(2,1)S(1)}, u32[]{:S(2)}, u32[]{:S(2)}) collective-permute-start(bf16[256,256]{1,0:T(8,128)(2,1)S(1)} %get-tuple-element.35), channel_id=1, source_target_pairs={{0,4},{2,6},{4,0},{6,2},{1,5},{3,7},{5,1},{7,3},{8,12},{10,14},{12... | collective-permute-start | bytes 393224 | tf_op jit(solution)/shard_map/ppermute | solution.py:387
  12.1 2.0 %collective-permute-start.3 = (bf16[256,256]{1,0:T(8,128)(2,1)S(1)}, bf16[256,256]{1,0:T(8,128)(2,1)S(1)}, u32[]{:S(2)}, u32[]{:S(2)}) collective-permute-start(bf16[256,256]{1,0:T(8,128)(2,1)S(1)} %get-tuple-element.66), channel_id=1, source_target_pairs={{0,6},{2,0},{4,2},{6,4},{1,7},{3,1},{5,3},{7,5},{8,14},{10,8},{12,... | collective-permute-start | bytes 393224 | tf_op jit(solution)/shard_map/ppermute | solution.py:387
  14.1 0.0 copy-start
  14.1 0.0 collective-permute-start.2
  14.1 3.3 %order.1.meta_ref = s32[204]{0:T(256)S(1)} custom-call(s32[132]{0:T(256)S(1)} %concatenate.9.meta_ref), custom_call_target="tpu_custom_call" | custom-call | flops 3000000000 | bytes 1048576 | tf_op jit(solution)/shard_map/order/pallas_call | solution.py:393
  17.4 0.0 collective-permute-done.1
  17.4 2.3 %collective-permute-done.3 = bf16[256,256]{1,0:T(8,128)(2,1)S(1)} collective-permute-done((bf16[256,256]{1,0:T(8,128)(2,1)S(1)}, bf16[256,256]{1,0:T(8,128)(2,1)S(1)}, u32[]{:S(2)}, u32[]{:S(2)}) %collective-permute-start.3) | collective-permute-done | bytes 131104 | tf_op jit(solution)/shard_map/ppermute | solution.py:387
  19.8 0.0 collective-permute-done.2
  19.8 0.1 fusion.2
  19.8 3.2 %collective-permute-start.6 = (bf16[256,256]{1,0:T(8,128)(2,1)S(1)}, bf16[256,256]{1,0:T(8,128)(2,1)S(1)}, u32[]{:S(2)}, u32[]{:S(2)}) collective-permute-start(bf16[256,256]{1,0:T(8,128)(2,1)S(1)} %fusion.2), channel_id=1, source_target_pairs={{0,6},{2,0},{4,2},{6,4},{1,7},{3,1},{5,3},{7,5},{8,14},{10,8},{12,... | collective-permute-start | bytes 393224 | tf_op jit(solution)/shard_map/ppermute | solution.py:387
  23.0 0.3 collective-permute-start.5
  23.4 0.3 collective-permute-start.4
  23.7 0.0 copy-done
  23.7 2.0 %flip.1.tiles_ref = bf16[64,128,128]{2,1,0:T(8,128)(2,1)S(1)} custom-call(s32[204]{0:T(256)S(1)} %order.1.meta_ref, bf16[64,128,128]{2,1,0:T(8,128)(2,1)S(1)} %bitcast.9), custom_call_target="tpu_custom_call" | custom-call | flops 3000000000 | bytes 1048576 | tf_op jit(solution)/shard_map/flip/pallas_call | solution.py:407
  25.7 2.7 %collective-permute-done.6 = bf16[256,256]{1,0:T(8,128)(2,1)S(1)} collective-permute-done((bf16[256,256]{1,0:T(8,128)(2,1)S(1)}, bf16[256,256]{1,0:T(8,128)(2,1)S(1)}, u32[]{:S(2)}, u32[]{:S(2)}) %collective-permute-start.6) | collective-permute-done | bytes 131104 | tf_op jit(solution)/shard_map/ppermute | solution.py:387
  28.4 0.4 collective-permute-done.5
  28.8 4.0 %collective-permute-done.4 = bf16[256,256]{1,0:T(8,128)(2,1)S(1)} collective-permute-done((bf16[256,256]{1,0:T(8,128)(2,1)S(1)}, bf16[256,256]{1,0:T(8,128)(2,1)S(1)}, u32[]{:S(2)}, u32[]{:S(2)}) %collective-permute-start.4) | collective-permute-done | bytes 131104 | tf_op jit(solution)/shard_map/ppermute | solution.py:387
  32.8 0.6 collective-permute-start.7
  33.4 0.3 gram.1.gram_ref
  33.7 1.2 %collective-permute-done.7.other_ref = bf16[1024,256]{1,0:T(8,128)(2,1)S(1)} collective-permute-done((bf16[1024,256]{1,0:T(8,128)(2,1)S(1)}, bf16[1024,256]{1,0:T(8,128)(2,1)S(1)}, u32[]{:S(2)}, u32[]{:S(2)}) %collective-permute-start.7) | collective-permute-done | bytes 524320 | tf_op jit(solution)/shard_map/ppermute | solution.py:418
  34.9 1.4 %slab.1 = (bf16[16,128,256]{2,1,0:T(8,128)(2,1)S(1)}, bf16[16,16,256]{2,1,0:T(8,128)(2,1)S(1)}, bf16[16,16,256]{2,1,0:T(8,128)(2,1)S(1)}) custom-call(s32[132]{0:T(256)S(1)} %concatenate.9.meta_ref, bf16[1024,256]{1,0:T(8,128)(2,1)S(1)} %pad_maximum_fusion.mine_ref, bf16[1024,256]{1,0:T(8,128)(2,1)S(1)} %collective-permute-done.7.other_ref, ...), custom_call_target="tpu_custom_call" | custom-call | flops 1000000000 | bytes 1048576 | tf_op jit(solution)/shard_map/slab/pallas_call | solution.py:428
  36.3 1.0 collective-permute-start.8
  37.3 1.6 %back1.1 = (bf16[8,64,256]{2,1,0:T(8,128)(2,1)S(1)}, bf16[8,64,256]{2,1,0:T(8,128)(2,1)S(1)}, bf16[8,64,256]{2,1,0:T(8,128)(2,1)S(1)}) custom-call(s32[204]{0:T(256)S(1)} %order.1.meta_ref, bf16[64,128,128]{2,1,0:T(8,128)(2,1)S(1)} %flip.1.tiles_ref, bf16[16,128,256]{2,1,0:T(8,128)(2,1)S(1)} %get-tuple-element.40.s_ref), custom_call_target="tpu_custom_call" | custom-call | flops 10000000000 | bytes 1048576 | tf_op jit(solution)/shard_map/back1/pallas_call | solution.py:445
  39.0 3.4 %collective-permute-done.8.got_ref = bf16[16,16,256]{2,1,0:T(8,128)(2,1)S(1)} collective-permute-done((bf16[16,16,256]{2,1,0:T(8,128)(2,1)S(1)}, bf16[16,16,256]{2,1,0:T(8,128)(2,1)S(1)}, u32[]{:S(2)}, u32[]{:S(2)}) %collective-permute-start.8) | collective-permute-done | bytes 131104 | tf_op jit(solution)/shard_map/ppermute | solution.py:439
  42.3 0.1 gram_pair.1
  42.4 0.1 collective-permute-start.9
  42.5 1.2 %back0.1.a_ref = bf16[8,64,256]{2,1,0:T(8,128)(2,1)S(1)} custom-call(s32[204]{0:T(256)S(1)} %order.1.meta_ref, bf16[64,128,128]{2,1,0:T(8,128)(2,1)S(1)} %flip.1.tiles_ref, bf16[16,128,256]{2,1,0:T(8,128)(2,1)S(1)} %get-tuple-element.40.s_ref), custom_call_target="tpu_custom_call" | custom-call | flops 1000000000 | bytes 1048576 | tf_op jit(solution)/shard_map/back0/pallas_call | solution.py:445
  43.8 1.9 %collective-permute-done.9.got_ref = bf16[8,16,256]{2,1,0:T(8,128)(2,1)S(1)} collective-permute-done((bf16[8,16,256]{2,1,0:T(8,128)(2,1)S(1)}, bf16[8,16,256]{2,1,0:T(8,128)(2,1)S(1)}, u32[]{:S(2)}, u32[]{:S(2)}) %collective-permute-start.9) | collective-permute-done | bytes 65568 | tf_op jit(solution)/shard_map/ppermute | solution.py:439
  45.7 0.1 gram_sum.1
  45.7 0.1 collective-permute-start.10
  45.8 2.1 %collective-permute-start.11 = (bf16[8,64,256]{2,1,0:T(8,128)(2,1)S(1)}, bf16[8,64,256]{2,1,0:T(8,128)(2,1)S(1)}, u32[]{:S(2)}, u32[]{:S(2)}) collective-permute-start(bf16[8,64,256]{2,1,0:T(8,128)(2,1)S(1)} %get-tuple-element.56), channel_id=1, source_target_pairs={{0,16},{8,24},{16,0},{24,8},{1,17},{9,25},{17,1},{25,9},{2,18},{10... | collective-permute-start | bytes 786440 | tf_op jit(solution)/shard_map/ppermute | solution.py:387
  47.9 1.5 %collective-permute-start.12 = (bf16[8,64,256]{2,1,0:T(8,128)(2,1)S(1)}, bf16[8,64,256]{2,1,0:T(8,128)(2,1)S(1)}, u32[]{:S(2)}, u32[]{:S(2)}) collective-permute-start(bf16[8,64,256]{2,1,0:T(8,128)(2,1)S(1)} %get-tuple-element.57), channel_id=1, source_target_pairs={{0,24},{8,0},{16,8},{24,16},{1,25},{9,1},{17,9},{25,17},{2,26},{10... | collective-permute-start | bytes 786440 | tf_op jit(solution)/shard_map/ppermute | solution.py:387
  49.4 15.0 %all_to_all.15.gram_ref = bf16[8,16,256]{2,1,0:T(8,128)(2,1)S(1)} all-to-all(bf16[8,16,256]{2,1,0:T(8,128)(2,1)S(1)} %gram_sum.1), channel_id=1, replica_groups=mesh['z'=8,'x'=4,'y'=4,'c'=2] {'z'}, dimensions={0} | all-to-all | bytes 131072 | tf_op jit(solution)/shard_map/all_to_all | solution.py:476
  64.4 0.0 collective-permute-done.10.b_ref
  64.4 0.0 collective-permute-done.11.c_ref
  64.4 0.0 collective-permute-done.12.d_ref
  64.4 0.2 partial.1
  64.5 13.2 %all_to_all.16.in_ref = bf16[8,80,256]{2,1,0:T(8,128)(2,1)S(1)} all-to-all(bf16[8,80,256]{2,1,0:T(8,128)(2,1)S(1)} %partial.1), channel_id=1, replica_groups=mesh['z'=8,'x'=4,'y'=4,'c'=2] {'z'}, dimensions={0} | all-to-all | bytes 655360 | tf_op jit(solution)/shard_map/all_to_all | solution.py:493
  77.7 1.1 %total.1 = (bf16[8,72,256]{2,1,0:T(8,128)(2,1)}, bf16[8,16,256]{2,1,0:T(8,128)(2,1)S(1)}) custom-call(bf16[8,80,256]{2,1,0:T(8,128)(2,1)S(1)} %all_to_all.16.in_ref), custom_call_target="tpu_custom_call" | custom-call | tf_op jit(solution)/shard_map/total/pallas_call | solution.py:486
  78.8 2.1 %collective-permute-start.13 = (bf16[8,16,256]{2,1,0:T(8,128)(2,1)S(1)}, bf16[8,16,256]{2,1,0:T(8,128)(2,1)S(1)}, u32[]{:S(2)}, u32[]{:S(2)}) collective-permute-start(bf16[8,16,256]{2,1,0:T(8,128)(2,1)S(1)} %get-tuple-element.59.e0_ref), channel_id=1, source_target_pairs={{0,8},{8,0},{16,24},{24,16},{1,9},{9,1},{17,25},{25,17},{2,10},{10... | collective-permute-start | bytes 196616 | tf_op jit(solution)/shard_map/ppermute | solution.py:439
  80.9 3.6 %all-to-all-start.2 = ((bf16[8,72,256]{2,1,0:T(8,128)(2,1)}), bf16[8,72,256]{2,1,0:T(8,128)(2,1)S(1)}, u32[]{:S(2)}, u32[]{:S(2)}) async-start(bf16[8,72,256]{2,1,0:T(8,128)(2,1)} %get-tuple-element.62), calls=%async_computation.2 | async-start | bytes 589824 | tf_op jit(solution)/shard_map/all_to_all | solution.py:496
  84.5 0.0 collective-permute-done.13.e1_ref
  84.5 2.2 %collective-permute-start.14 = (bf16[16,16,256]{2,1,0:T(8,128)(2,1)S(1)}, bf16[16,16,256]{2,1,0:T(8,128)(2,1)S(1)}, u32[]{:S(2)}, u32[]{:S(2)}) collective-permute-start(bf16[16,16,256]{2,1,0:T(8,128)(2,1)S(1)} %pad_maximum_fusion.1), channel_id=1, source_target_pairs={{0,24},{8,16},{16,8},{24,0},{1,25},{9,17},{17,9},{25,1},{2,26},{10... | collective-permute-start | bytes 393224 | tf_op jit(solution)/shard_map/ppermute | solution.py:439
  86.8 2.9 %collective-permute-done.14.e2_ref = bf16[16,16,256]{2,1,0:T(8,128)(2,1)S(1)} collective-permute-done((bf16[16,16,256]{2,1,0:T(8,128)(2,1)S(1)}, bf16[16,16,256]{2,1,0:T(8,128)(2,1)S(1)}, u32[]{:S(2)}, u32[]{:S(2)}) %collective-permute-start.14) | collective-permute-done | bytes 131104 | tf_op jit(solution)/shard_map/ppermute | solution.py:439
  89.6 3.4 %first.1.begun_ref = f32[256,512]{1,0:T(8,128)S(1)} custom-call(s32[132]{0:T(256)S(1)} %concatenate.9.meta_ref, bf16[8,16,256]{2,1,0:T(8,128)(2,1)S(1)} %get-tuple-element.59.e0_ref, bf16[8,16,256]{2,1,0:T(8,128)(2,1)S(1)} %collective-permute-done.13.e1_ref, bf16[16,16,256]{2,1,0:T(8,128)(2,1)S(1)} %collective-permute-done.14.e2_ref), custom_call_target="tpu_custom_call" | custom-call | flops 3000000000 | bytes 1048576 | tf_op jit(solution)/shard_map/first/pallas_call | solution.py:498
  93.0 1.2 %all-to-all-done.2.b0_ref = bf16[8,72,256]{2,1,0:T(8,128)(2,1)S(1)} async-done(((bf16[8,72,256]{2,1,0:T(8,128)(2,1)}), bf16[8,72,256]{2,1,0:T(8,128)(2,1)S(1)}, u32[]{:S(2)}, u32[]{:S(2)}) %all-to-all-start.2) | async-done | bytes 294944 | tf_op jit(solution)/shard_map/all_to_all | solution.py:496
  94.2 2.2 %collective-permute-start.17 = (bf16[8,72,256]{2,1,0:T(8,128)(2,1)S(1)}, bf16[8,72,256]{2,1,0:T(8,128)(2,1)S(1)}, u32[]{:S(2)}, u32[]{:S(2)}) collective-permute-start(bf16[8,72,256]{2,1,0:T(8,128)(2,1)S(1)} %all-to-all-done.2.b0_ref), channel_id=1, source_target_pairs={{0,24},{8,0},{16,8},{24,16},{1,25},{9,1},{17,9},{25,17},{2,26},{10... | collective-permute-start | bytes 884744 | tf_op jit(solution)/shard_map/ppermute | solution.py:387
  96.4 1.2 %collective-permute-start.16 = (bf16[8,72,256]{2,1,0:T(8,128)(2,1)S(1)}, bf16[8,72,256]{2,1,0:T(8,128)(2,1)S(1)}, u32[]{:S(2)}, u32[]{:S(2)}) collective-permute-start(bf16[8,72,256]{2,1,0:T(8,128)(2,1)S(1)} %all-to-all-done.2.b0_ref), channel_id=1, source_target_pairs={{0,16},{8,24},{16,0},{24,8},{1,17},{9,25},{17,1},{25,9},{2,18},{10... | collective-permute-start | bytes 884744 | tf_op jit(solution)/shard_map/ppermute | solution.py:387
  97.6 0.9 collective-permute-start.15
  98.4 7.8 %rest.1 = (f32[256,256]{1,0:T(8,128)}, bf16[512,256]{1,0:T(8,128)(2,1)S(1)}) custom-call(f32[256,512]{1,0:T(8,128)S(1)} %first.1.begun_ref), custom_call_target="tpu_custom_call" | custom-call | flops 8999999488 | bytes 1048576 | tf_op jit(solution)/shard_map/rest/pallas_call | solution.py:507
  106.2 1.7 %q.1 = bf16[2048,256]{1,0:T(8,128)(2,1)} custom-call(bf16[16,128,256]{2,1,0:T(8,128)(2,1)S(1)} %get-tuple-element.40.s_ref, bf16[512,256]{1,0:T(8,128)(2,1)S(1)} %get-tuple-element.60.inv_ref), custom_call_target="tpu_custom_call" | custom-call | flops 2000000000 | bytes 1048576 | tf_op jit(solution)/shard_map/q/pallas_call | solution.py:517
  107.9 0.0 collective-permute-done.17.b3_ref
  107.9 0.0 collective-permute-done.16.b2_ref
  107.9 3.0 %collective-permute-done.15.b1_ref = bf16[8,72,256]{2,1,0:T(8,128)(2,1)S(1)} collective-permute-done((bf16[8,72,256]{2,1,0:T(8,128)(2,1)S(1)}, bf16[8,72,256]{2,1,0:T(8,128)(2,1)S(1)}, u32[]{:S(2)}, u32[]{:S(2)}) %collective-permute-start.15) | collective-permute-done | bytes 294944 | tf_op jit(solution)/shard_map/ppermute | solution.py:387
  110.9 2.5 %z.1 = f32[2048,256]{1,0:T(8,128)} custom-call(s32[132]{0:T(256)S(1)} %concatenate.9.meta_ref, bf16[8,72,256]{2,1,0:T(8,128)(2,1)S(1)} %all-to-all-done.2.b0_ref, bf16[8,72,256]{2,1,0:T(8,128)(2,1)S(1)} %collective-permute-done.15.b1_ref, bf16[8,72,256]{2,1,0:T(8,128)(2,1)S(1)} %collective-permute-done.16.b2_ref, ...), custom_call_target="tpu_custom_call" | custom-call | tf_op jit(solution)/shard_map/z/pallas_call | solution.py:526
  (3 shorter events, 0.1 us)
Async XLA Ops:
  5.8 4.3 %collective-permute-start = (bf16[1024,256]{1,0:T(8,128)(2,1)S(1)}, bf16[1024,256]{1,0:T(8,128)(2,1)S(1)}, u32[]{:S(2)}, u32[]{:S(2)}) collective-permute-start(bf16[1024,256]{1,0:T(8,128)(2,1)S(1)} %get-tuple-element.34), channel_id=1, source_target_pairs={{0,1},{1,0},{2,3},{3,2},{4,5},{5,4},{6,7},{7,6},{8,9},{9,8},{10,11... | collective-permute-start | bytes 1572872 | tf_op jit(solution)/shard_map/ppermute | solution.py:389
  10.3 7.1 %collective-permute-start.1 = (bf16[256,256]{1,0:T(8,128)(2,1)S(1)}, bf16[256,256]{1,0:T(8,128)(2,1)S(1)}, u32[]{:S(2)}, u32[]{:S(2)}) collective-permute-start(bf16[256,256]{1,0:T(8,128)(2,1)S(1)} %get-tuple-element.35), channel_id=1, source_target_pairs={{0,4},{2,6},{4,0},{6,2},{1,5},{3,7},{5,1},{7,3},{8,12},{10,14},{12... | collective-permute-start | bytes 393224 | tf_op jit(solution)/shard_map/ppermute | solution.py:387
  12.1 7.6 %collective-permute-start.3 = (bf16[256,256]{1,0:T(8,128)(2,1)S(1)}, bf16[256,256]{1,0:T(8,128)(2,1)S(1)}, u32[]{:S(2)}, u32[]{:S(2)}) collective-permute-start(bf16[256,256]{1,0:T(8,128)(2,1)S(1)} %get-tuple-element.66), channel_id=1, source_target_pairs={{0,6},{2,0},{4,2},{6,4},{1,7},{3,1},{5,3},{7,5},{8,14},{10,8},{12,... | collective-permute-start | bytes 393224 | tf_op jit(solution)/shard_map/ppermute | solution.py:387
  14.1 9.6 %copy-start = (bf16[1,1,64,128,128]{4,3,2,1,0:T(8,128)(2,1)S(1)}, bf16[1,1,64,128,128]{4,3,2,1,0:T(8,128)(2,1)}, u32[]{:S(2)}) copy-start(bf16[1,1,64,128,128]{4,3,2,1,0:T(8,128)(2,1)} %tiles_hbm.1) | copy-start | bytes 6291460
  14.1 5.7 %collective-permute-start.2 = (bf16[256,256]{1,0:T(8,128)(2,1)S(1)}, bf16[256,256]{1,0:T(8,128)(2,1)S(1)}, u32[]{:S(2)}, u32[]{:S(2)}) collective-permute-start(bf16[256,256]{1,0:T(8,128)(2,1)S(1)} %get-tuple-element.67), channel_id=1, source_target_pairs={{0,2},{2,4},{4,6},{6,0},{1,3},{3,5},{5,7},{7,1},{8,10},{10,12},{12... | collective-permute-start | bytes 393224 | tf_op jit(solution)/shard_map/ppermute | solution.py:387
  19.8 8.5 %collective-permute-start.6 = (bf16[256,256]{1,0:T(8,128)(2,1)S(1)}, bf16[256,256]{1,0:T(8,128)(2,1)S(1)}, u32[]{:S(2)}, u32[]{:S(2)}) collective-permute-start(bf16[256,256]{1,0:T(8,128)(2,1)S(1)} %fusion.2), channel_id=1, source_target_pairs={{0,6},{2,0},{4,2},{6,4},{1,7},{3,1},{5,3},{7,5},{8,14},{10,8},{12,... | collective-permute-start | bytes 393224 | tf_op jit(solution)/shard_map/ppermute | solution.py:387
  23.0 5.8 %collective-permute-start.5 = (bf16[256,256]{1,0:T(8,128)(2,1)S(1)}, bf16[256,256]{1,0:T(8,128)(2,1)S(1)}, u32[]{:S(2)}, u32[]{:S(2)}) collective-permute-start(bf16[256,256]{1,0:T(8,128)(2,1)S(1)} %fusion.2), channel_id=1, source_target_pairs={{0,4},{2,6},{4,0},{6,2},{1,5},{3,7},{5,1},{7,3},{8,12},{10,14},{12... | collective-permute-start | bytes 393224 | tf_op jit(solution)/shard_map/ppermute | solution.py:387
  23.4 9.4 %collective-permute-start.4 = (bf16[256,256]{1,0:T(8,128)(2,1)S(1)}, bf16[256,256]{1,0:T(8,128)(2,1)S(1)}, u32[]{:S(2)}, u32[]{:S(2)}) collective-permute-start(bf16[256,256]{1,0:T(8,128)(2,1)S(1)} %fusion.2), channel_id=1, source_target_pairs={{0,2},{2,4},{4,6},{6,0},{1,3},{3,5},{5,7},{7,1},{8,10},{10,12},{12... | collective-permute-start | bytes 393224 | tf_op jit(solution)/shard_map/ppermute | solution.py:387
  32.8 2.1 %collective-permute-start.7 = (bf16[1024,256]{1,0:T(8,128)(2,1)S(1)}, bf16[1024,256]{1,0:T(8,128)(2,1)S(1)}, u32[]{:S(2)}, u32[]{:S(2)}) collective-permute-start(bf16[1024,256]{1,0:T(8,128)(2,1)S(1)} %pad_maximum_fusion.mine_ref), channel_id=1, source_target_pairs={{0,1},{1,0},{2,3},{3,2},{4,5},{5,4},{6,7},{7,6},{8,9},{9,8},{10,11... | collective-permute-start | bytes 1572872 | tf_op jit(solution)/shard_map/ppermute | solution.py:418
  36.3 6.0 %collective-permute-start.8 = (bf16[16,16,256]{2,1,0:T(8,128)(2,1)S(1)}, bf16[16,16,256]{2,1,0:T(8,128)(2,1)S(1)}, u32[]{:S(2)}, u32[]{:S(2)}) collective-permute-start(bf16[16,16,256]{2,1,0:T(8,128)(2,1)S(1)} %get-tuple-element.42), channel_id=1, source_target_pairs={{0,24},{8,16},{16,8},{24,0},{1,25},{9,17},{17,9},{25,1},{2,26},{10... | collective-permute-start | bytes 393224 | tf_op jit(solution)/shard_map/ppermute | solution.py:439
  42.4 3.2 %collective-permute-start.9 = (bf16[8,16,256]{2,1,0:T(8,128)(2,1)S(1)}, bf16[8,16,256]{2,1,0:T(8,128)(2,1)S(1)}, u32[]{:S(2)}, u32[]{:S(2)}) collective-permute-start(bf16[8,16,256]{2,1,0:T(8,128)(2,1)S(1)} %get-tuple-element.48), channel_id=1, source_target_pairs={{0,8},{8,0},{16,24},{24,16},{1,9},{9,1},{17,25},{25,17},{2,10},{10... | collective-permute-start | bytes 196616 | tf_op jit(solution)/shard_map/ppermute | solution.py:439
  45.7 18.6 %collective-permute-start.10 = (bf16[8,64,256]{2,1,0:T(8,128)(2,1)S(1)}, bf16[8,64,256]{2,1,0:T(8,128)(2,1)S(1)}, u32[]{:S(2)}, u32[]{:S(2)}) collective-permute-start(bf16[8,64,256]{2,1,0:T(8,128)(2,1)S(1)} %get-tuple-element.55), channel_id=1, source_target_pairs={{0,8},{8,16},{16,24},{24,0},{1,9},{9,17},{17,25},{25,1},{2,10},{10... | collective-permute-start | bytes 786440 | tf_op jit(solution)/shard_map/ppermute | solution.py:387
  45.8 18.6 %collective-permute-start.11 = (bf16[8,64,256]{2,1,0:T(8,128)(2,1)S(1)}, bf16[8,64,256]{2,1,0:T(8,128)(2,1)S(1)}, u32[]{:S(2)}, u32[]{:S(2)}) collective-permute-start(bf16[8,64,256]{2,1,0:T(8,128)(2,1)S(1)} %get-tuple-element.56), channel_id=1, source_target_pairs={{0,16},{8,24},{16,0},{24,8},{1,17},{9,25},{17,1},{25,9},{2,18},{10... | collective-permute-start | bytes 786440 | tf_op jit(solution)/shard_map/ppermute | solution.py:387
  47.9 16.5 %collective-permute-start.12 = (bf16[8,64,256]{2,1,0:T(8,128)(2,1)S(1)}, bf16[8,64,256]{2,1,0:T(8,128)(2,1)S(1)}, u32[]{:S(2)}, u32[]{:S(2)}) collective-permute-start(bf16[8,64,256]{2,1,0:T(8,128)(2,1)S(1)} %get-tuple-element.57), channel_id=1, source_target_pairs={{0,24},{8,0},{16,8},{24,16},{1,25},{9,1},{17,9},{25,17},{2,26},{10... | collective-permute-start | bytes 786440 | tf_op jit(solution)/shard_map/ppermute | solution.py:387
  78.8 5.7 %collective-permute-start.13 = (bf16[8,16,256]{2,1,0:T(8,128)(2,1)S(1)}, bf16[8,16,256]{2,1,0:T(8,128)(2,1)S(1)}, u32[]{:S(2)}, u32[]{:S(2)}) collective-permute-start(bf16[8,16,256]{2,1,0:T(8,128)(2,1)S(1)} %get-tuple-element.59.e0_ref), channel_id=1, source_target_pairs={{0,8},{8,0},{16,24},{24,16},{1,9},{9,1},{17,25},{25,17},{2,10},{10... | collective-permute-start | bytes 196616 | tf_op jit(solution)/shard_map/ppermute | solution.py:439
  80.9 13.2 %all-to-all-start.2 = ((bf16[8,72,256]{2,1,0:T(8,128)(2,1)}), bf16[8,72,256]{2,1,0:T(8,128)(2,1)S(1)}, u32[]{:S(2)}, u32[]{:S(2)}) async-start(bf16[8,72,256]{2,1,0:T(8,128)(2,1)} %get-tuple-element.62), calls=%async_computation.2 | async-start | bytes 589824 | tf_op jit(solution)/shard_map/all_to_all | solution.py:496
  84.5 5.1 %collective-permute-start.14 = (bf16[16,16,256]{2,1,0:T(8,128)(2,1)S(1)}, bf16[16,16,256]{2,1,0:T(8,128)(2,1)S(1)}, u32[]{:S(2)}, u32[]{:S(2)}) collective-permute-start(bf16[16,16,256]{2,1,0:T(8,128)(2,1)S(1)} %pad_maximum_fusion.1), channel_id=1, source_target_pairs={{0,24},{8,16},{16,8},{24,0},{1,25},{9,17},{17,9},{25,1},{2,26},{10... | collective-permute-start | bytes 393224 | tf_op jit(solution)/shard_map/ppermute | solution.py:439
  94.2 13.7 %collective-permute-start.17 = (bf16[8,72,256]{2,1,0:T(8,128)(2,1)S(1)}, bf16[8,72,256]{2,1,0:T(8,128)(2,1)S(1)}, u32[]{:S(2)}, u32[]{:S(2)}) collective-permute-start(bf16[8,72,256]{2,1,0:T(8,128)(2,1)S(1)} %all-to-all-done.2.b0_ref), channel_id=1, source_target_pairs={{0,24},{8,0},{16,8},{24,16},{1,25},{9,1},{17,9},{25,17},{2,26},{10... | collective-permute-start | bytes 884744 | tf_op jit(solution)/shard_map/ppermute | solution.py:387
  96.4 11.5 %collective-permute-start.16 = (bf16[8,72,256]{2,1,0:T(8,128)(2,1)S(1)}, bf16[8,72,256]{2,1,0:T(8,128)(2,1)S(1)}, u32[]{:S(2)}, u32[]{:S(2)}) collective-permute-start(bf16[8,72,256]{2,1,0:T(8,128)(2,1)S(1)} %all-to-all-done.2.b0_ref), channel_id=1, source_target_pairs={{0,16},{8,24},{16,0},{24,8},{1,17},{9,25},{17,1},{25,9},{2,18},{10... | collective-permute-start | bytes 884744 | tf_op jit(solution)/shard_map/ppermute | solution.py:387
  97.6 13.3 %collective-permute-start.15 = (bf16[8,72,256]{2,1,0:T(8,128)(2,1)S(1)}, bf16[8,72,256]{2,1,0:T(8,128)(2,1)S(1)}, u32[]{:S(2)}, u32[]{:S(2)}) collective-permute-start(bf16[8,72,256]{2,1,0:T(8,128)(2,1)S(1)} %all-to-all-done.2.b0_ref), channel_id=1, source_target_pairs={{0,8},{8,16},{16,24},{24,0},{1,9},{9,17},{17,25},{25,1},{2,10},{10... | collective-permute-start | bytes 884744 | tf_op jit(solution)/shard_map/ppermute | solution.py:387

commit v7 on v6

--- a/solution.py
+++ b/solution.py
@@ -24,6 +24,7 @@
 NB = 64
 FIRST = 1
 LOAD = 8
+FETCH = 16
 LIVE = 3
 AT = 4
 COLS = AT + SLOTS
@@ -49,9 +50,9 @@
     test = pltpu.make_async_copy(omega_hbm, omega_ref, omega_sem)
     big = [
         pltpu.make_async_copy(
-            tiles_hbm.at[0, 0, pl.ds(g * LOAD, LOAD)], tiles_ref.at[pl.ds(g * LOAD, LOAD)], tile_sem.at[g]
+            tiles_hbm.at[0, 0, pl.ds(g * FETCH, FETCH)], tiles_ref.at[pl.ds(g * FETCH, FETCH)], tile_sem.at[g]
         )
-        for g in range(SLOTS // LOAD)
+        for g in range(SLOTS // FETCH)
     ]
     big[0].start()
     test.start()
@@ -64,10 +65,10 @@
     for g, copy in enumerate(big):
         copy.wait()
 
-        @pl.when(g * LOAD < live)
+        @pl.when(g * FETCH < live)
         def _():
             prods, places = [], []
-            for t in range(g * LOAD, (g + 1) * LOAD):
+            for t in range(g * FETCH, (g + 1) * FETCH):
                 prod = dot(tiles_ref[t], omega_ref[meta_ref[COLS + t] & (CB - 1)], 1, 0)
                 prods.append(jnp.where(t < live, prod, 0.0))
                 block = meta_ref[AT + t] & (RB - 1)
@@ -377,7 +378,7 @@
             pltpu.VMEM((SLOTS, TILE, TILE), BF16),
             pltpu.VMEM((CB, TILE, K), BF16),
             pltpu.SemaphoreType.DMA,
-            pltpu.SemaphoreType.DMA((SLOTS // LOAD,)),
+            pltpu.SemaphoreType.DMA((SLOTS // FETCH,)),
         ],
         compiler_params=pltpu.CompilerParams(vmem_limit_bytes=52 * 1024 * 1024),
         name="sketch",

time: 114 us -> 114 us (level)
  Pallas kernels: 30.4 us -> 28.9 us
    ppermute x12, starting transfers between devices: 15.6 us -> 13.7 us  [turn(): return lax.ppermute(a, axis, [(i, (i + k) % 4) for i in range(4)])]
  transfers between devices with their start and end apart: 19 -> 19, of which waited for: 11 -> 12; matrix products, arithmetic and copies ran while one was open for 0% -> 0% of each run, Pallas kernels for 19% -> 18%
where the time goes in v7:
time: 114 us; the launch traced here: 113 us
  Pallas kernels  28.9 us (25%)
  blocking collectives  28.5 us (25%)
  starting transfers between devices  28 us (25%)
  waiting for transfers between devices  24.7 us (22%)
  between operations  1.59 us (1%)
    all_to_all x1, blocking collectives, on_device(): grams = lax.all_to_all(grams, 'z', 0, 0, tiled=True)  15.8 us
    ppermute x12, starting transfers between devices, turn(): return lax.ppermute(a, axis, [(i, (i + k) % 4) for i in range(4)])  13.7 us
    all_to_all x1, blocking collectives, on_device(): lax.all_to_all(parts, 'z', 0, 0, tiled=True)  12.7 us
    ppermute x12, waiting for transfers between devices, turn(): return lax.ppermute(a, axis, [(i, (i + k) % 4) for i in range(4)])  12.4 us
    ppermute x4, waiting for transfers between devices, mirror(): return lax.ppermute(a, 'x', [(i, i ^ bits) for i in range(4)])  8.47 us
    pallas_call x1, Pallas kernels, on_device(): pl.pallas_call(rest_kernel, out_shape=(shape(K, K), shape(2 * K, K, dtype...  7.76 us
    ppermute x4, starting transfers between devices, mirror(): return lax.ppermute(a, 'x', [(i, i ^ bits) for i in range(4)])  6.44 us
    ppermute x1, starting transfers between devices, on_device(): half = keep + lax.ppermute(send, 'c', swap).astype(F32)  3.76 us
  transfers between devices with their start and end apart: 19, of which 12 were waited for; matrix products, arithmetic and copies ran while one was open for 0% of the time, Pallas kernels for 18%

profile of v7, /device:TPU:1, one launch (start us, length us, event | category | flops | bytes accessed | tf_op | source)
XLA Modules:
  0.0 112.8 jit_solution(13570864477416150652)
XLA Ops:
  1.3 0.8 concatenate.9.meta_ref
  2.0 2.9 %sketch.1 = (f32[1024,256]{1,0:T(8,128)S(1)}, bf16[1024,256]{1,0:T(8,128)(2,1)S(1)}) custom-call(s32[132]{0:T(256)S(1)} %concatenate.9.meta_ref, bf16[1,1,64,128,128]{4,3,2,1,0:T(8,128)(2,1)} %tiles_hbm.1, bf16[16,128,256]{2,1,0:T(8,128)(2,1)} %bitcast.10), custom_call_target="tpu_custom_call" | custom-call | tf_op jit(solution)/shard_map/sketch/pallas_call | solution.py:371
  4.9 3.8 %collective-permute-start = (bf16[1024,256]{1,0:T(8,128)(2,1)S(1)}, bf16[1024,256]{1,0:T(8,128)(2,1)S(1)}, u32[]{:S(2)}, u32[]{:S(2)}) collective-permute-start(bf16[1024,256]{1,0:T(8,128)(2,1)S(1)} %get-tuple-element.34), channel_id=1, source_target_pairs={{0,1},{1,0},{2,3},{3,2},{4,5},{5,4},{6,7},{7,6},{8,9},{9,8},{10,11... | collective-permute-start | bytes 1572872 | tf_op jit(solution)/shard_map/ppermute | solution.py:390
  8.7 1.5 %collective-permute-done = bf16[1024,256]{1,0:T(8,128)(2,1)S(1)} collective-permute-done((bf16[1024,256]{1,0:T(8,128)(2,1)S(1)}, bf16[1024,256]{1,0:T(8,128)(2,1)S(1)}, u32[]{:S(2)}, u32[]{:S(2)}) %collective-permute-start) | collective-permute-done | bytes 524320 | tf_op jit(solution)/shard_map/ppermute | solution.py:390
  10.2 0.2 fusion.3
  10.4 1.8 %collective-permute-start.1 = (bf16[256,256]{1,0:T(8,128)(2,1)S(1)}, bf16[256,256]{1,0:T(8,128)(2,1)S(1)}, u32[]{:S(2)}, u32[]{:S(2)}) collective-permute-start(bf16[256,256]{1,0:T(8,128)(2,1)S(1)} %get-tuple-element.35), channel_id=1, source_target_pairs={{0,4},{2,6},{4,0},{6,2},{1,5},{3,7},{5,1},{7,3},{8,12},{10,14},{12... | collective-permute-start | bytes 393224 | tf_op jit(solution)/shard_map/ppermute | solution.py:388
  12.3 0.8 collective-permute-start.3
  13.0 0.0 copy-start
  13.0 0.7 collective-permute-start.2
  13.7 3.3 %order.1.meta_ref = s32[204]{0:T(256)S(1)} custom-call(s32[132]{0:T(256)S(1)} %concatenate.9.meta_ref), custom_call_target="tpu_custom_call" | custom-call | flops 3000000000 | bytes 1048576 | tf_op jit(solution)/shard_map/order/pallas_call | solution.py:394
  17.0 0.0 collective-permute-done.1
  17.1 1.9 %collective-permute-done.3 = bf16[256,256]{1,0:T(8,128)(2,1)S(1)} collective-permute-done((bf16[256,256]{1,0:T(8,128)(2,1)S(1)}, bf16[256,256]{1,0:T(8,128)(2,1)S(1)}, u32[]{:S(2)}, u32[]{:S(2)}) %collective-permute-start.3) | collective-permute-done | bytes 131104 | tf_op jit(solution)/shard_map/ppermute | solution.py:388
  19.0 0.9 collective-permute-done.2
  19.8 0.1 fusion.2
  19.9 2.1 %collective-permute-start.6 = (bf16[256,256]{1,0:T(8,128)(2,1)S(1)}, bf16[256,256]{1,0:T(8,128)(2,1)S(1)}, u32[]{:S(2)}, u32[]{:S(2)}) collective-permute-start(bf16[256,256]{1,0:T(8,128)(2,1)S(1)} %fusion.2), channel_id=1, source_target_pairs={{0,6},{2,0},{4,2},{6,4},{1,7},{3,1},{5,3},{7,5},{8,14},{10,8},{12,... | collective-permute-start | bytes 393224 | tf_op jit(solution)/shard_map/ppermute | solution.py:388
  22.0 0.3 collective-permute-start.5
  22.3 0.7 collective-permute-start.4
  23.0 0.0 copy-done
  23.0 2.0 %flip.1.tiles_ref = bf16[64,128,128]{2,1,0:T(8,128)(2,1)S(1)} custom-call(s32[204]{0:T(256)S(1)} %order.1.meta_ref, bf16[64,128,128]{2,1,0:T(8,128)(2,1)S(1)} %bitcast.9), custom_call_target="tpu_custom_call" | custom-call | flops 3000000000 | bytes 1048576 | tf_op jit(solution)/shard_map/flip/pallas_call | solution.py:408
  25.0 0.2 collective-permute-done.6
  25.2 2.6 %collective-permute-done.5 = bf16[256,256]{1,0:T(8,128)(2,1)S(1)} collective-permute-done((bf16[256,256]{1,0:T(8,128)(2,1)S(1)}, bf16[256,256]{1,0:T(8,128)(2,1)S(1)}, u32[]{:S(2)}, u32[]{:S(2)}) %collective-permute-start.5) | collective-permute-done | bytes 131104 | tf_op jit(solution)/shard_map/ppermute | solution.py:388
  27.8 4.0 %collective-permute-done.4 = bf16[256,256]{1,0:T(8,128)(2,1)S(1)} collective-permute-done((bf16[256,256]{1,0:T(8,128)(2,1)S(1)}, bf16[256,256]{1,0:T(8,128)(2,1)S(1)}, u32[]{:S(2)}, u32[]{:S(2)}) %collective-permute-start.4) | collective-permute-done | bytes 131104 | tf_op jit(solution)/shard_map/ppermute | solution.py:388
  31.8 0.6 collective-permute-start.7
  32.3 0.3 gram.1.gram_ref
  32.7 1.2 %collective-permute-done.7.other_ref = bf16[1024,256]{1,0:T(8,128)(2,1)S(1)} collective-permute-done((bf16[1024,256]{1,0:T(8,128)(2,1)S(1)}, bf16[1024,256]{1,0:T(8,128)(2,1)S(1)}, u32[]{:S(2)}, u32[]{:S(2)}) %collective-permute-start.7) | collective-permute-done | bytes 524320 | tf_op jit(solution)/shard_map/ppermute | solution.py:419
  33.9 1.4 %slab.1 = (bf16[16,128,256]{2,1,0:T(8,128)(2,1)S(1)}, bf16[16,16,256]{2,1,0:T(8,128)(2,1)S(1)}, bf16[16,16,256]{2,1,0:T(8,128)(2,1)S(1)}) custom-call(s32[132]{0:T(256)S(1)} %concatenate.9.meta_ref, bf16[1024,256]{1,0:T(8,128)(2,1)S(1)} %pad_maximum_fusion.mine_ref, bf16[1024,256]{1,0:T(8,128)(2,1)S(1)} %collective-permute-done.7.other_ref, ...), custom_call_target="tpu_custom_call" | custom-call | flops 1000000000 | bytes 1048576 | tf_op jit(solution)/shard_map/slab/pallas_call | solution.py:429
  35.3 2.0 %collective-permute-start.8 = (bf16[16,16,256]{2,1,0:T(8,128)(2,1)S(1)}, bf16[16,16,256]{2,1,0:T(8,128)(2,1)S(1)}, u32[]{:S(2)}, u32[]{:S(2)}) collective-permute-start(bf16[16,16,256]{2,1,0:T(8,128)(2,1)S(1)} %get-tuple-element.42), channel_id=1, source_target_pairs={{0,24},{8,16},{16,8},{24,0},{1,25},{9,17},{17,9},{25,1},{2,26},{10... | collective-permute-start | bytes 393224 | tf_op jit(solution)/shard_map/ppermute | solution.py:440
  37.3 1.3 %back1.1 = (bf16[8,64,256]{2,1,0:T(8,128)(2,1)S(1)}, bf16[8,64,256]{2,1,0:T(8,128)(2,1)S(1)}, bf16[8,64,256]{2,1,0:T(8,128)(2,1)S(1)}) custom-call(s32[204]{0:T(256)S(1)} %order.1.meta_ref, bf16[64,128,128]{2,1,0:T(8,128)(2,1)S(1)} %flip.1.tiles_ref, bf16[16,128,256]{2,1,0:T(8,128)(2,1)S(1)} %get-tuple-element.40.s_ref), custom_call_target="tpu_custom_call" | custom-call | flops 10000000000 | bytes 1048576 | tf_op jit(solution)/shard_map/back1/pallas_call | solution.py:446
  38.6 2.7 %collective-permute-done.8.got_ref = bf16[16,16,256]{2,1,0:T(8,128)(2,1)S(1)} collective-permute-done((bf16[16,16,256]{2,1,0:T(8,128)(2,1)S(1)}, bf16[16,16,256]{2,1,0:T(8,128)(2,1)S(1)}, u32[]{:S(2)}, u32[]{:S(2)}) %collective-permute-start.8) | collective-permute-done | bytes 131104 | tf_op jit(solution)/shard_map/ppermute | solution.py:440
  41.3 0.1 gram_pair.1
  41.4 0.1 collective-permute-start.9
  41.5 0.9 back0.1.a_ref
  42.4 2.2 %collective-permute-done.9.got_ref = bf16[8,16,256]{2,1,0:T(8,128)(2,1)S(1)} collective-permute-done((bf16[8,16,256]{2,1,0:T(8,128)(2,1)S(1)}, bf16[8,16,256]{2,1,0:T(8,128)(2,1)S(1)}, u32[]{:S(2)}, u32[]{:S(2)}) %collective-permute-start.9) | collective-permute-done | bytes 65568 | tf_op jit(solution)/shard_map/ppermute | solution.py:440
  44.6 0.1 gram_sum.1
  44.7 0.1 collective-permute-start.10
  44.8 3.1 %collective-permute-start.11 = (bf16[8,64,256]{2,1,0:T(8,128)(2,1)S(1)}, bf16[8,64,256]{2,1,0:T(8,128)(2,1)S(1)}, u32[]{:S(2)}, u32[]{:S(2)}) collective-permute-start(bf16[8,64,256]{2,1,0:T(8,128)(2,1)S(1)} %get-tuple-element.56), channel_id=1, source_target_pairs={{0,16},{8,24},{16,0},{24,8},{1,17},{9,25},{17,1},{25,9},{2,18},{10... | collective-permute-start | bytes 786440 | tf_op jit(solution)/shard_map/ppermute | solution.py:388
  47.8 0.6 collective-permute-start.12
  48.4 15.8 %all_to_all.15.gram_ref = bf16[8,16,256]{2,1,0:T(8,128)(2,1)S(1)} all-to-all(bf16[8,16,256]{2,1,0:T(8,128)(2,1)S(1)} %gram_sum.1), channel_id=1, replica_groups=mesh['z'=8,'x'=4,'y'=4,'c'=2] {'z'}, dimensions={0} | all-to-all | bytes 131072 | tf_op jit(solution)/shard_map/all_to_all | solution.py:477
  64.3 0.0 collective-permute-done.10.b_ref
  64.3 0.0 collective-permute-done.11.c_ref
  64.3 0.0 collective-permute-done.12.d_ref
  64.3 0.2 partial.1
  64.5 12.7 %all_to_all.16.in_ref = bf16[8,80,256]{2,1,0:T(8,128)(2,1)S(1)} all-to-all(bf16[8,80,256]{2,1,0:T(8,128)(2,1)S(1)} %partial.1), channel_id=1, replica_groups=mesh['z'=8,'x'=4,'y'=4,'c'=2] {'z'}, dimensions={0} | all-to-all | bytes 655360 | tf_op jit(solution)/shard_map/all_to_all | solution.py:494
  77.1 1.1 %total.1 = (bf16[8,72,256]{2,1,0:T(8,128)(2,1)}, bf16[8,16,256]{2,1,0:T(8,128)(2,1)S(1)}) custom-call(bf16[8,80,256]{2,1,0:T(8,128)(2,1)S(1)} %all_to_all.16.in_ref), custom_call_target="tpu_custom_call" | custom-call | tf_op jit(solution)/shard_map/total/pallas_call | solution.py:487
  78.3 2.9 %collective-permute-start.13 = (bf16[8,16,256]{2,1,0:T(8,128)(2,1)S(1)}, bf16[8,16,256]{2,1,0:T(8,128)(2,1)S(1)}, u32[]{:S(2)}, u32[]{:S(2)}) collective-permute-start(bf16[8,16,256]{2,1,0:T(8,128)(2,1)S(1)} %get-tuple-element.59.e0_ref), channel_id=1, source_target_pairs={{0,8},{8,0},{16,24},{24,16},{1,9},{9,1},{17,25},{25,17},{2,10},{10... | collective-permute-start | bytes 196616 | tf_op jit(solution)/shard_map/ppermute | solution.py:440
  81.1 3.6 %all-to-all-start.2 = ((bf16[8,72,256]{2,1,0:T(8,128)(2,1)}), bf16[8,72,256]{2,1,0:T(8,128)(2,1)S(1)}, u32[]{:S(2)}, u32[]{:S(2)}) async-start(bf16[8,72,256]{2,1,0:T(8,128)(2,1)} %get-tuple-element.62), calls=%async_computation.2 | async-start | bytes 589824 | tf_op jit(solution)/shard_map/all_to_all | solution.py:497
  84.7 0.0 collective-permute-done.13.e1_ref
  84.7 1.5 %collective-permute-start.14 = (bf16[16,16,256]{2,1,0:T(8,128)(2,1)S(1)}, bf16[16,16,256]{2,1,0:T(8,128)(2,1)S(1)}, u32[]{:S(2)}, u32[]{:S(2)}) collective-permute-start(bf16[16,16,256]{2,1,0:T(8,128)(2,1)S(1)} %pad_maximum_fusion.1), channel_id=1, source_target_pairs={{0,24},{8,16},{16,8},{24,0},{1,25},{9,17},{17,9},{25,1},{2,26},{10... | collective-permute-start | bytes 393224 | tf_op jit(solution)/shard_map/ppermute | solution.py:440
  86.2 3.6 %collective-permute-done.14.e2_ref = bf16[16,16,256]{2,1,0:T(8,128)(2,1)S(1)} collective-permute-done((bf16[16,16,256]{2,1,0:T(8,128)(2,1)S(1)}, bf16[16,16,256]{2,1,0:T(8,128)(2,1)S(1)}, u32[]{:S(2)}, u32[]{:S(2)}) %collective-permute-start.14) | collective-permute-done | bytes 131104 | tf_op jit(solution)/shard_map/ppermute | solution.py:440
  89.8 3.4 %first.1.begun_ref = f32[256,512]{1,0:T(8,128)S(1)} custom-call(s32[132]{0:T(256)S(1)} %concatenate.9.meta_ref, bf16[8,16,256]{2,1,0:T(8,128)(2,1)S(1)} %get-tuple-element.59.e0_ref, bf16[8,16,256]{2,1,0:T(8,128)(2,1)S(1)} %collective-permute-done.13.e1_ref, bf16[16,16,256]{2,1,0:T(8,128)(2,1)S(1)} %collective-permute-done.14.e2_ref), custom_call_target="tpu_custom_call" | custom-call | flops 3000000000 | bytes 1048576 | tf_op jit(solution)/shard_map/first/pallas_call | solution.py:499
  93.2 1.2 %all-to-all-done.2.b0_ref = bf16[8,72,256]{2,1,0:T(8,128)(2,1)S(1)} async-done(((bf16[8,72,256]{2,1,0:T(8,128)(2,1)}), bf16[8,72,256]{2,1,0:T(8,128)(2,1)S(1)}, u32[]{:S(2)}, u32[]{:S(2)}) %all-to-all-start.2) | async-done | bytes 294944 | tf_op jit(solution)/shard_map/all_to_all | solution.py:497
  94.4 1.5 %collective-permute-start.17 = (bf16[8,72,256]{2,1,0:T(8,128)(2,1)S(1)}, bf16[8,72,256]{2,1,0:T(8,128)(2,1)S(1)}, u32[]{:S(2)}, u32[]{:S(2)}) collective-permute-start(bf16[8,72,256]{2,1,0:T(8,128)(2,1)S(1)} %all-to-all-done.2.b0_ref), channel_id=1, source_target_pairs={{0,24},{8,0},{16,8},{24,16},{1,25},{9,1},{17,9},{25,17},{2,26},{10... | collective-permute-start | bytes 884744 | tf_op jit(solution)/shard_map/ppermute | solution.py:388
  95.9 1.2 %collective-permute-start.16 = (bf16[8,72,256]{2,1,0:T(8,128)(2,1)S(1)}, bf16[8,72,256]{2,1,0:T(8,128)(2,1)S(1)}, u32[]{:S(2)}, u32[]{:S(2)}) collective-permute-start(bf16[8,72,256]{2,1,0:T(8,128)(2,1)S(1)} %all-to-all-done.2.b0_ref), channel_id=1, source_target_pairs={{0,16},{8,24},{16,0},{24,8},{1,17},{9,25},{17,1},{25,9},{2,18},{10... | collective-permute-start | bytes 884744 | tf_op jit(solution)/shard_map/ppermute | solution.py:388
  97.0 0.9 collective-permute-start.15
  97.9 7.8 %rest.1 = (f32[256,256]{1,0:T(8,128)}, bf16[512,256]{1,0:T(8,128)(2,1)S(1)}) custom-call(f32[256,512]{1,0:T(8,128)S(1)} %first.1.begun_ref), custom_call_target="tpu_custom_call" | custom-call | flops 8999999488 | bytes 1048576 | tf_op jit(solution)/shard_map/rest/pallas_call | solution.py:508
  105.7 1.7 %q.1 = bf16[2048,256]{1,0:T(8,128)(2,1)} custom-call(bf16[16,128,256]{2,1,0:T(8,128)(2,1)S(1)} %get-tuple-element.40.s_ref, bf16[512,256]{1,0:T(8,128)(2,1)S(1)} %get-tuple-element.60.inv_ref), custom_call_target="tpu_custom_call" | custom-call | flops 2000000000 | bytes 1048576 | tf_op jit(solution)/shard_map/q/pallas_call | solution.py:518
  107.4 0.0 collective-permute-done.17.b3_ref
  107.4 0.0 collective-permute-done.16.b2_ref
  107.4 2.8 %collective-permute-done.15.b1_ref = bf16[8,72,256]{2,1,0:T(8,128)(2,1)S(1)} collective-permute-done((bf16[8,72,256]{2,1,0:T(8,128)(2,1)S(1)}, bf16[8,72,256]{2,1,0:T(8,128)(2,1)S(1)}, u32[]{:S(2)}, u32[]{:S(2)}) %collective-permute-start.15) | collective-permute-done | bytes 294944 | tf_op jit(solution)/shard_map/ppermute | solution.py:388
  110.2 2.5 %z.1 = f32[2048,256]{1,0:T(8,128)} custom-call(s32[132]{0:T(256)S(1)} %concatenate.9.meta_ref, bf16[8,72,256]{2,1,0:T(8,128)(2,1)S(1)} %all-to-all-done.2.b0_ref, bf16[8,72,256]{2,1,0:T(8,128)(2,1)S(1)} %collective-permute-done.15.b1_ref, bf16[8,72,256]{2,1,0:T(8,128)(2,1)S(1)} %collective-permute-done.16.b2_ref, ...), custom_call_target="tpu_custom_call" | custom-call | tf_op jit(solution)/shard_map/z/pallas_call | solution.py:527
  (3 shorter events, 0.1 us)
Async XLA Ops:
  4.9 5.3 %collective-permute-start = (bf16[1024,256]{1,0:T(8,128)(2,1)S(1)}, bf16[1024,256]{1,0:T(8,128)(2,1)S(1)}, u32[]{:S(2)}, u32[]{:S(2)}) collective-permute-start(bf16[1024,256]{1,0:T(8,128)(2,1)S(1)} %get-tuple-element.34), channel_id=1, source_target_pairs={{0,1},{1,0},{2,3},{3,2},{4,5},{5,4},{6,7},{7,6},{8,9},{9,8},{10,11... | collective-permute-start | bytes 1572872 | tf_op jit(solution)/shard_map/ppermute | solution.py:390
  10.4 6.6 %collective-permute-start.1 = (bf16[256,256]{1,0:T(8,128)(2,1)S(1)}, bf16[256,256]{1,0:T(8,128)(2,1)S(1)}, u32[]{:S(2)}, u32[]{:S(2)}) collective-permute-start(bf16[256,256]{1,0:T(8,128)(2,1)S(1)} %get-tuple-element.35), channel_id=1, source_target_pairs={{0,4},{2,6},{4,0},{6,2},{1,5},{3,7},{5,1},{7,3},{8,12},{10,14},{12... | collective-permute-start | bytes 393224 | tf_op jit(solution)/shard_map/ppermute | solution.py:388
  12.3 6.7 %collective-permute-start.3 = (bf16[256,256]{1,0:T(8,128)(2,1)S(1)}, bf16[256,256]{1,0:T(8,128)(2,1)S(1)}, u32[]{:S(2)}, u32[]{:S(2)}) collective-permute-start(bf16[256,256]{1,0:T(8,128)(2,1)S(1)} %get-tuple-element.66), channel_id=1, source_target_pairs={{0,6},{2,0},{4,2},{6,4},{1,7},{3,1},{5,3},{7,5},{8,14},{10,8},{12,... | collective-permute-start | bytes 393224 | tf_op jit(solution)/shard_map/ppermute | solution.py:388
  13.0 10.0 %copy-start = (bf16[1,1,64,128,128]{4,3,2,1,0:T(8,128)(2,1)S(1)}, bf16[1,1,64,128,128]{4,3,2,1,0:T(8,128)(2,1)}, u32[]{:S(2)}) copy-start(bf16[1,1,64,128,128]{4,3,2,1,0:T(8,128)(2,1)} %tiles_hbm.1) | copy-start | bytes 6291460
  13.0 6.8 %collective-permute-start.2 = (bf16[256,256]{1,0:T(8,128)(2,1)S(1)}, bf16[256,256]{1,0:T(8,128)(2,1)S(1)}, u32[]{:S(2)}, u32[]{:S(2)}) collective-permute-start(bf16[256,256]{1,0:T(8,128)(2,1)S(1)} %get-tuple-element.67), channel_id=1, source_target_pairs={{0,2},{2,4},{4,6},{6,0},{1,3},{3,5},{5,7},{7,1},{8,10},{10,12},{12... | collective-permute-start | bytes 393224 | tf_op jit(solution)/shard_map/ppermute | solution.py:388
  19.9 5.3 %collective-permute-start.6 = (bf16[256,256]{1,0:T(8,128)(2,1)S(1)}, bf16[256,256]{1,0:T(8,128)(2,1)S(1)}, u32[]{:S(2)}, u32[]{:S(2)}) collective-permute-start(bf16[256,256]{1,0:T(8,128)(2,1)S(1)} %fusion.2), channel_id=1, source_target_pairs={{0,6},{2,0},{4,2},{6,4},{1,7},{3,1},{5,3},{7,5},{8,14},{10,8},{12,... | collective-permute-start | bytes 393224 | tf_op jit(solution)/shard_map/ppermute | solution.py:388
  22.0 5.8 %collective-permute-start.5 = (bf16[256,256]{1,0:T(8,128)(2,1)S(1)}, bf16[256,256]{1,0:T(8,128)(2,1)S(1)}, u32[]{:S(2)}, u32[]{:S(2)}) collective-permute-start(bf16[256,256]{1,0:T(8,128)(2,1)S(1)} %fusion.2), channel_id=1, source_target_pairs={{0,4},{2,6},{4,0},{6,2},{1,5},{3,7},{5,1},{7,3},{8,12},{10,14},{12... | collective-permute-start | bytes 393224 | tf_op jit(solution)/shard_map/ppermute | solution.py:388
  22.3 9.4 %collective-permute-start.4 = (bf16[256,256]{1,0:T(8,128)(2,1)S(1)}, bf16[256,256]{1,0:T(8,128)(2,1)S(1)}, u32[]{:S(2)}, u32[]{:S(2)}) collective-permute-start(bf16[256,256]{1,0:T(8,128)(2,1)S(1)} %fusion.2), channel_id=1, source_target_pairs={{0,2},{2,4},{4,6},{6,0},{1,3},{3,5},{5,7},{7,1},{8,10},{10,12},{12... | collective-permute-start | bytes 393224 | tf_op jit(solution)/shard_map/ppermute | solution.py:388
  31.8 2.1 %collective-permute-start.7 = (bf16[1024,256]{1,0:T(8,128)(2,1)S(1)}, bf16[1024,256]{1,0:T(8,128)(2,1)S(1)}, u32[]{:S(2)}, u32[]{:S(2)}) collective-permute-start(bf16[1024,256]{1,0:T(8,128)(2,1)S(1)} %pad_maximum_fusion.mine_ref), channel_id=1, source_target_pairs={{0,1},{1,0},{2,3},{3,2},{4,5},{5,4},{6,7},{7,6},{8,9},{9,8},{10,11... | collective-permute-start | bytes 1572872 | tf_op jit(solution)/shard_map/ppermute | solution.py:419
  35.3 6.0 %collective-permute-start.8 = (bf16[16,16,256]{2,1,0:T(8,128)(2,1)S(1)}, bf16[16,16,256]{2,1,0:T(8,128)(2,1)S(1)}, u32[]{:S(2)}, u32[]{:S(2)}) collective-permute-start(bf16[16,16,256]{2,1,0:T(8,128)(2,1)S(1)} %get-tuple-element.42), channel_id=1, source_target_pairs={{0,24},{8,16},{16,8},{24,0},{1,25},{9,17},{17,9},{25,1},{2,26},{10... | collective-permute-start | bytes 393224 | tf_op jit(solution)/shard_map/ppermute | solution.py:440
  41.4 3.2 %collective-permute-start.9 = (bf16[8,16,256]{2,1,0:T(8,128)(2,1)S(1)}, bf16[8,16,256]{2,1,0:T(8,128)(2,1)S(1)}, u32[]{:S(2)}, u32[]{:S(2)}) collective-permute-start(bf16[8,16,256]{2,1,0:T(8,128)(2,1)S(1)} %get-tuple-element.48), channel_id=1, source_target_pairs={{0,8},{8,0},{16,24},{24,16},{1,9},{9,1},{17,25},{25,17},{2,10},{10... | collective-permute-start | bytes 196616 | tf_op jit(solution)/shard_map/ppermute | solution.py:440
  44.7 19.6 %collective-permute-start.10 = (bf16[8,64,256]{2,1,0:T(8,128)(2,1)S(1)}, bf16[8,64,256]{2,1,0:T(8,128)(2,1)S(1)}, u32[]{:S(2)}, u32[]{:S(2)}) collective-permute-start(bf16[8,64,256]{2,1,0:T(8,128)(2,1)S(1)} %get-tuple-element.55), channel_id=1, source_target_pairs={{0,8},{8,16},{16,24},{24,0},{1,9},{9,17},{17,25},{25,1},{2,10},{10... | collective-permute-start | bytes 786440 | tf_op jit(solution)/shard_map/ppermute | solution.py:388
  44.8 19.5 %collective-permute-start.11 = (bf16[8,64,256]{2,1,0:T(8,128)(2,1)S(1)}, bf16[8,64,256]{2,1,0:T(8,128)(2,1)S(1)}, u32[]{:S(2)}, u32[]{:S(2)}) collective-permute-start(bf16[8,64,256]{2,1,0:T(8,128)(2,1)S(1)} %get-tuple-element.56), channel_id=1, source_target_pairs={{0,16},{8,24},{16,0},{24,8},{1,17},{9,25},{17,1},{25,9},{2,18},{10... | collective-permute-start | bytes 786440 | tf_op jit(solution)/shard_map/ppermute | solution.py:388
  47.8 16.5 %collective-permute-start.12 = (bf16[8,64,256]{2,1,0:T(8,128)(2,1)S(1)}, bf16[8,64,256]{2,1,0:T(8,128)(2,1)S(1)}, u32[]{:S(2)}, u32[]{:S(2)}) collective-permute-start(bf16[8,64,256]{2,1,0:T(8,128)(2,1)S(1)} %get-tuple-element.57), channel_id=1, source_target_pairs={{0,24},{8,0},{16,8},{24,16},{1,25},{9,1},{17,9},{25,17},{2,26},{10... | collective-permute-start | bytes 786440 | tf_op jit(solution)/shard_map/ppermute | solution.py:388
  78.3 6.4 %collective-permute-start.13 = (bf16[8,16,256]{2,1,0:T(8,128)(2,1)S(1)}, bf16[8,16,256]{2,1,0:T(8,128)(2,1)S(1)}, u32[]{:S(2)}, u32[]{:S(2)}) collective-permute-start(bf16[8,16,256]{2,1,0:T(8,128)(2,1)S(1)} %get-tuple-element.59.e0_ref), channel_id=1, source_target_pairs={{0,8},{8,0},{16,24},{24,16},{1,9},{9,1},{17,25},{25,17},{2,10},{10... | collective-permute-start | bytes 196616 | tf_op jit(solution)/shard_map/ppermute | solution.py:440
  81.1 13.2 %all-to-all-start.2 = ((bf16[8,72,256]{2,1,0:T(8,128)(2,1)}), bf16[8,72,256]{2,1,0:T(8,128)(2,1)S(1)}, u32[]{:S(2)}, u32[]{:S(2)}) async-start(bf16[8,72,256]{2,1,0:T(8,128)(2,1)} %get-tuple-element.62), calls=%async_computation.2 | async-start | bytes 589824 | tf_op jit(solution)/shard_map/all_to_all | solution.py:497
  84.7 5.1 %collective-permute-start.14 = (bf16[16,16,256]{2,1,0:T(8,128)(2,1)S(1)}, bf16[16,16,256]{2,1,0:T(8,128)(2,1)S(1)}, u32[]{:S(2)}, u32[]{:S(2)}) collective-permute-start(bf16[16,16,256]{2,1,0:T(8,128)(2,1)S(1)} %pad_maximum_fusion.1), channel_id=1, source_target_pairs={{0,24},{8,16},{16,8},{24,0},{1,25},{9,17},{17,9},{25,1},{2,26},{10... | collective-permute-start | bytes 393224 | tf_op jit(solution)/shard_map/ppermute | solution.py:440
  94.4 13.0 %collective-permute-start.17 = (bf16[8,72,256]{2,1,0:T(8,128)(2,1)S(1)}, bf16[8,72,256]{2,1,0:T(8,128)(2,1)S(1)}, u32[]{:S(2)}, u32[]{:S(2)}) collective-permute-start(bf16[8,72,256]{2,1,0:T(8,128)(2,1)S(1)} %all-to-all-done.2.b0_ref), channel_id=1, source_target_pairs={{0,24},{8,0},{16,8},{24,16},{1,25},{9,1},{17,9},{25,17},{2,26},{10... | collective-permute-start | bytes 884744 | tf_op jit(solution)/shard_map/ppermute | solution.py:388
  95.9 11.5 %collective-permute-start.16 = (bf16[8,72,256]{2,1,0:T(8,128)(2,1)S(1)}, bf16[8,72,256]{2,1,0:T(8,128)(2,1)S(1)}, u32[]{:S(2)}, u32[]{:S(2)}) collective-permute-start(bf16[8,72,256]{2,1,0:T(8,128)(2,1)S(1)} %all-to-all-done.2.b0_ref), channel_id=1, source_target_pairs={{0,16},{8,24},{16,0},{24,8},{1,17},{9,25},{17,1},{25,9},{2,18},{10... | collective-permute-start | bytes 884744 | tf_op jit(solution)/shard_map/ppermute | solution.py:388
  97.0 13.2 %collective-permute-start.15 = (bf16[8,72,256]{2,1,0:T(8,128)(2,1)S(1)}, bf16[8,72,256]{2,1,0:T(8,128)(2,1)S(1)}, u32[]{:S(2)}, u32[]{:S(2)}) collective-permute-start(bf16[8,72,256]{2,1,0:T(8,128)(2,1)S(1)} %all-to-all-done.2.b0_ref), channel_id=1, source_target_pairs={{0,8},{8,16},{16,24},{24,0},{1,9},{9,17},{17,25},{25,1},{2,10},{10... | collective-permute-start | bytes 884744 | tf_op jit(solution)/shard_map/ppermute | solution.py:388
